TPU v7x, 512 devices: a whole 4x4x16 slice. The times are simulated.
512 devices in a mesh: ax: 128 (over x_hi, y, z), rad: 4 (over x_lo, core).
Axes of the slice: x: 4 (x_hi: 2, x_lo: 2; x = x_hi * 2 + x_lo), y: 4, z: 16, core: 2. Of those that a mesh axis runs over, the one named last changes fastest.
Arguments:
- gas_state: float32 [6, 1024, 64, 512], P(None, 'ax', 'rad'), as said below
- viscosity: float32 [1024, 64, 512], P('ax', 'rad'), may hold values from 0.05 to 0.3
- droplets: float32 [4, 2097152], P(None, ('ax', 'rad')), as said below
- drop_cells: int32 [2097152], P(('ax', 'rad')), may hold values from 0 to 65535
- move_lists: int32 [512, 4, 64], P(('ax', 'rad')), may hold values from 0 to 4095, as said below
- move_counts: int32 [512, 4], P(('ax', 'rad')), may hold values from 0 to 64, as said below
Outputs:
- gas_out: float32 [6, 1024, 64, 512], P(None, 'ax', 'rad')
- drops_out: float32 [4, 2097152], P(None, ('ax', 'rad'))
- arrivals_out: float32 [4, 131072], P(None, ('ax', 'rad'))
Inputs may be any that keep to these rules, and one draw needn't show every extreme that they name: `gas_state`: component 0 lies in 0.8 to 1.2; component 4 divided by component 0 in 0.5 to 1.5; component 5 divided by component 0 in 0 to 0.5. `droplets`: on each tile the slots with positive mass come first, and tiles at lower axial index hold more of them; every slot of the tiles at axial index 0 is filled. Masses are 0 or in 0.5 to 2; temperatures in 0.5 to 1.5. `move_lists`: the 256 entries of one tile are distinct slots of that tile with positive mass. `move_counts`: 64 is reached in each direction by some tile; lists toward outside the grid are empty.
All inputs are finite; a program needn't handle non-finite values.
Results may differ from a plain program's by a relative error of at most 0.0003.
Values sent between devices are 32-bit elements; how exact they have to be, the bound alone decides.
No kernel may reach another device: no remote copies, remote signals or barrier semaphores. Data moves between devices by JAX's collectives and lax.ppermute only.
A program may use at most 64 MiB of HBM per device.

v0:
```python
import math

import jax
import jax.numpy as jnp
from jax import lax
from jax.sharding import PartitionSpec as P

time_step = 0.2
highest = lax.Precision.HIGHEST


def extended(x, sides, width):
    for axis, dim in sides:
        devices, length = (lax.axis_size(axis), x.shape[dim])
        up = [(i, (i + 1) % devices) for i in range(devices - 1)]
        down = [(j, i) for i, j in up]
        last = lax.slice_in_dim(x, length - width, length, axis=dim)
        first = lax.slice_in_dim(x, 0, width, axis=dim)
        before = lax.ppermute(last, axis, up)
        after = lax.ppermute(first, axis, down)
        x = jnp.concatenate([before, x, after], axis=dim)
    return x


def shifted(block, axis, distance):
    devices = range(lax.axis_size(axis))
    route = [(i - distance, i) for i in devices if i - distance in devices]
    return lax.ppermute(block, axis, route)


def window(padded, start, length, axis):
    return lax.slice_in_dim(padded, start, start + length, axis=axis)


def second(padded, length, axis):
    parts = [window(padded, offset, length, axis) for offset in range(5)]
    return (-parts[0] + 16.0 * parts[1] - 30.0 * parts[2] + 16.0 * parts[3] - parts[4]) / 12.0


def gradient(padded, length, axis):
    parts = [window(padded, offset, length, axis) for offset in range(5)]
    return (parts[0] - 8.0 * parts[1] + 8.0 * parts[3] - parts[4]) / 12.0


def evaporate(records, sampled_draw_outcomes):
    particle_weight, drop_temp, drop_axial, drop_radial = (
        records[0],
        records[1],
        records[2],
        records[3],
    )
    ambient_compressible_lattice = sampled_draw_outcomes[0]
    lengthwise_flow_state = sampled_draw_outcomes[1] / ambient_compressible_lattice
    spoke_flow_state = sampled_draw_outcomes[2] / ambient_compressible_lattice
    ambient_thermal_value = sampled_draw_outcomes[4] / ambient_compressible_lattice
    released_burnable_share = sampled_draw_outcomes[5] / ambient_compressible_lattice
    living = particle_weight > 0.0
    safe_temp = jnp.where(living, drop_temp, jnp.ones_like(drop_temp))
    balance = jnp.exp(-1.0 / safe_temp)
    slip_square = (lengthwise_flow_state - drop_axial) ** 2 + (spoke_flow_state - drop_radial) ** 2
    evaporated = (
        0.1
        * jnp.cbrt(particle_weight)
        * (jnp.log(1.0 - released_burnable_share) - jnp.log(1.0 - balance))
        * (1.0 + 0.3 * (1.0 + slip_square) ** 0.25)
    )
    updated = jnp.stack(
        [
            particle_weight - evaporated,
            drop_temp + 0.1 * (ambient_thermal_value - drop_temp) - 0.5 * evaporated,
            drop_axial + 0.2 * (lengthwise_flow_state - drop_axial),
            drop_radial + 0.2 * (spoke_flow_state - drop_radial),
        ]
    )
    updated = jnp.where(living[None], updated, jnp.zeros_like(updated))
    sources = jnp.stack(
        [
            evaporated,
            evaporated * drop_axial + 0.2 * particle_weight * (drop_axial - lengthwise_flow_state),
            evaporated * drop_radial + 0.2 * particle_weight * (drop_radial - spoke_flow_state),
            jnp.zeros_like(particle_weight),
            evaporated * drop_temp + 0.1 * particle_weight * (drop_temp - ambient_thermal_value),
            evaporated,
        ]
    )
    return (updated, sources)


def advance(gas_state, viscosity, axial_pad, radial_pad):
    axial_count = gas_state.shape[1]
    radial_count = gas_state.shape[2]
    around_count = gas_state.shape[3]
    azimuth_pad = jnp.concatenate([gas_state[..., -2:], gas_state, gas_state[..., :2]], axis=3)
    speeds = gas_state[1:4] / gas_state[0]
    laplace = (
        second(axial_pad, axial_count, 1)
        + second(radial_pad, radial_count, 2)
        + second(azimuth_pad, around_count, 3)
    )
    transport = (
        speeds[0] * gradient(axial_pad, axial_count, 1)
        + speeds[1] * gradient(radial_pad, radial_count, 2)
        + speeds[2] * gradient(azimuth_pad, around_count, 3)
    )
    return gas_state + time_step * (viscosity * laplace - transport)


def block_update(summed, gas_rows, piece, where_cells):
    components = summed.shape[0]
    row_count = summed.shape[1]
    around_count = summed.shape[2]
    row_ids = jnp.arange(row_count, dtype=jnp.int32)
    around_ids = jnp.arange(around_count, dtype=jnp.int32)
    pick_row = (row_ids[:, None] == (where_cells // around_count)[None, :]).astype(jnp.float32)
    pick_around = (around_ids[None, :] == (where_cells % around_count)[:, None]).astype(jnp.float32)
    columns = jnp.dot(
        gas_rows.reshape(components * row_count, around_count), pick_around.T, precision=highest
    )
    sampled = jnp.sum(columns.reshape(components, row_count, -1) * pick_row[None], axis=1)
    piece_new, piece_terms = evaporate(piece, sampled)
    spread = (piece_terms[:, None, :] * pick_row[None]).reshape(components * row_count, -1)
    deposit = jnp.dot(spread, pick_around, precision=highest)
    return (summed + deposit.reshape(summed.shape), piece_new)


def sweep_all(summed, gas_rows, records, cells):
    fields = records.shape[0]
    count = cells.shape[0]
    blocksize = math.gcd(count, 512)
    turns = count // blocksize
    pieces = records.reshape(fields, turns, blocksize).transpose(1, 0, 2)
    where_all = cells.reshape(turns, blocksize)

    def step(carry, inputs):
        return block_update(carry, gas_rows, inputs[0], inputs[1])

    summed, news = lax.scan(step, summed, (pieces, where_all))
    return (summed, news.transpose(1, 0, 2).reshape(fields, count))


def body(gas_state, viscosity, droplets, drop_cells, move_lists, move_counts):
    padded = extended(gas_state, (("ax", 1), ("rad", 2)), 2)
    axial_pad = padded[:, :, 2:-2]
    radial_pad = padded[:, 2:-2]
    advanced = advance(gas_state, viscosity, axial_pad, radial_pad)
    fields = droplets.shape[0]
    capacity = move_lists.shape[2]
    slot_count = droplets.shape[1]
    records = jnp.concatenate([droplets, drop_cells.astype(jnp.float32)[None]], 0)
    weights = (
        (jnp.arange(capacity, dtype=jnp.int32)[None, :] < move_counts[0][:, None])
        .astype(jnp.float32)
        .reshape(-1)
    )
    slot_ids = jnp.arange(slot_count, dtype=jnp.int32)
    chosen = (move_lists[0].reshape(-1)[:, None] == slot_ids[None, :]).astype(
        jnp.float32
    ) * weights[:, None]
    outgoing = jnp.dot(records, chosen.T, precision=highest).reshape(fields + 1, 4, capacity)
    departed = jnp.max(chosen, axis=0)
    from_below = shifted(outgoing[:, 0], "ax", 1)
    from_above = shifted(outgoing[:, 1], "ax", -1)
    from_inner = shifted(outgoing[:, 2], "rad", 1)
    from_outer = shifted(outgoing[:, 3], "rad", -1)
    arrived = jnp.concatenate([from_below, from_above, from_inner, from_outer], axis=1)
    components = gas_state.shape[0]
    around_count = gas_state.shape[3]
    gas_rows = gas_state.reshape(components, -1, around_count)
    summed = jnp.zeros_like(gas_rows)
    arrive_cells = arrived[fields].astype(jnp.int32)
    summed, arrive_new = sweep_all(summed, gas_rows, arrived[:fields], arrive_cells)
    stayers = jnp.concatenate([(droplets[0] * (1.0 - departed))[None], droplets[1:]], 0)
    summed, stay_new = sweep_all(summed, gas_rows, stayers, drop_cells)
    gas_out = advanced + summed.reshape(gas_state.shape)
    return (gas_out, stay_new, arrive_new)


def solution(mesh):
    placed = (
        P(None, "ax", "rad", None),
        P("ax", "rad", None),
        P(None, ("ax", "rad")),
        P(("ax", "rad")),
        P(("ax", "rad"), None, None),
        P(("ax", "rad"), None),
    )
    return jax.shard_map(
        body,
        mesh=mesh,
        in_specs=placed,
        out_specs=(P(None, "ax", "rad", None), P(None, ("ax", "rad")), P(None, ("ax", "rad"))),
        check_vma=False,
    )
```

profile of v0, /device:TPU:6, one launch (start us, length us, event | category | flops | bytes accessed | tf_op | source)
XLA Modules:
  0.0 127.2 jit_solution(3497618497890616092)
XLA Ops:
  0.6 0.7 fusion.48
  1.4 0.8 eq.106
  2.2 0.7 convert_element_type.46
  2.9 4.4 %fusion.21 = f32[5,256]{1,0:T(8,128)S(1)} fusion(f32[256]{0:T(256)S(1)} %reshape.416, s32[256]{0:T(256)S(1)} %eq.106, f32[1,4096]{1,0:T(1,128)S(1)} %bitcast.147, f32[4,4096]{1,0:T(4,128)} %param.10), kind=kOutput, calls=%fused_computation.51 | convolution fusion | flops 65032192 | bytes 89088 | tf_op jit(solution)/shard_map/dot_general | solution.py:159
  7.4 3.8 %collective-permute-start.4 = (f32[5,64]{1,0:T(8,128)S(1)}, f32[5,64]{1,0:T(8,128)S(1)}, u32[]{:S(2)}, u32[]{:S(2)}) collective-permute-start(f32[5,64]{1,0:T(8,128)S(1)} %bitcast.152), channel_id=1, source_target_pairs={{0,4},{4,8},{8,12},{12,16},{16,20},{20,24},{24,28},{28,32},{32,36}... | collective-permute-start | bytes 3848 | tf_op jit(solution)/shard_map/ppermute | solution.py:28
  11.3 12.8 %collective-permute-start.5 = (f32[5,64]{1,0:T(8,128)S(1)}, f32[5,64]{1,0:T(8,128)S(1)}, u32[]{:S(2)}, u32[]{:S(2)}) collective-permute-start(f32[5,64]{1,0:T(8,128)S(1)} %bitcast.150), channel_id=1, source_target_pairs={{4,0},{8,4},{12,8},{16,12},{20,16},{24,20},{28,24},{32,28},{36,32}... | collective-permute-start | bytes 3848 | tf_op jit(solution)/shard_map/ppermute | solution.py:28
  24.1 1.9 %collective-permute-start.6 = (f32[5,64]{1,0:T(8,128)S(1)}, f32[5,64]{1,0:T(8,128)S(1)}, u32[]{:S(2)}, u32[]{:S(2)}) collective-permute-start(f32[5,64]{1,0:T(8,128)S(1)} %bitcast.151), channel_id=1, source_target_pairs={{0,1},{1,2},{2,3},{4,5},{5,6},{6,7},{8,9},{9,10},{10,11},{12,13},{... | collective-permute-start | bytes 3848 | tf_op jit(solution)/shard_map/ppermute | solution.py:28
  26.0 3.6 %collective-permute-start.7 = (f32[5,64]{1,0:T(8,128)S(1)}, f32[5,64]{1,0:T(8,128)S(1)}, u32[]{:S(2)}, u32[]{:S(2)}) collective-permute-start(f32[5,64]{1,0:T(8,128)S(1)} %bitcast.153), channel_id=1, source_target_pairs={{1,0},{2,1},{3,2},{5,4},{6,5},{7,6},{9,8},{10,9},{11,10},{13,12},{... | collective-permute-start | bytes 3848 | tf_op jit(solution)/shard_map/ppermute | solution.py:28
  29.7 1.0 fusion.56
  30.6 1.9 %collective-permute-start = (f32[6,2,16,512]{3,2,1,0:T(8,128)}, f32[6,2,16,512]{3,2,1,0:T(8,128)}, u32[]{:S(2)}, u32[]{:S(2)}) collective-permute-start(f32[6,2,16,512]{3,2,1,0:T(8,128)} %get-tuple-element.152), channel_id=1, source_target_pairs={{0,4},{4,8},{8,12},{12,16},{16,20},{20,24},{24,28},{28,32},{32,36}... | collective-permute-start | bytes 1179656 | tf_op jit(solution)/shard_map/ppermute | solution.py:19
  32.5 0.9 select_reduce_fusion
  33.5 1.0 fusion.57
  34.7 1.0 fusion.41
  35.6 0.7 broadcast_multiply_fusion
  36.5 9.6 %collective-permute-start.1 = (f32[6,2,16,512]{3,2,1,0:T(8,128)}, f32[6,2,16,512]{3,2,1,0:T(8,128)}, u32[]{:S(2)}, u32[]{:S(2)}) collective-permute-start(f32[6,2,16,512]{3,2,1,0:T(8,128)} %get-tuple-element.151), channel_id=1, source_target_pairs={{4,0},{8,4},{12,8},{16,12},{20,16},{24,20},{28,24},{32,28},{36,32}... | collective-permute-start | bytes 1179656 | tf_op jit(solution)/shard_map/ppermute | solution.py:20
  46.2 1.0 convolution_bitcast_fusion.1
  47.9 2.1 %fusion.33 = f32[6,128,512]{2,1,0:T(8,128)} fusion(f32[6,256]{1,0:T(8,128)S(1)} %stack.51, f32[128,256]{1,0:T(8,128)S(1)} %fusion.47, s32[256]{0:T(256)S(1)} %and_select_fusion.2), kind=kOutput, calls=%fused_computation.77 | convolution fusion | flops 1208287232 | bytes 1711104 | tf_op jit(solution)/shard_map/while/body/eval_jaxpr/dot_general | solution.py:122
  50.0 1.1 constant_dynamic-update-slice_fusion.1
  51.1 1.7 %constant_dynamic-update-slice_fusion = (f32[6,10,16,512]{3,2,1,0:T(8,128)S(1)}, f32[6,12,16,512]{3,2,1,0:T(8,128)S(1)}, f32[6,10,16,512]{3,2,1,0:T(8,128)}) fusion(f32[6,10,16,512]{3,2,1,0:T(8,128)S(1)} %get-tuple-element.158, f32[6,8,16,512]{3,2,1,0:T(8,128)S(1)} %copy-done, f32[6,12,16,512]{3,2,1,0:T(8,128)S(1)} %get-tuple-element.159), kind=kLoop, calls=%fused_computation.101 | loop fusion | bytes 6291456 | tf_op jit(solution)/shard_map/concatenate | solution.py:21
  52.8 0.7 collective-permute-done.1
  53.4 1.8 %constant_dynamic-update-slice_fusion.2 = (f32[6,10,16,512]{3,2,1,0:T(8,128)}, f32[6,12,16,512]{3,2,1,0:T(8,128)S(1)}) fusion(f32[6,10,16,512]{3,2,1,0:T(8,128)} %get-tuple-element.150, f32[6,2,16,512]{3,2,1,0:T(8,128)} %collective-permute-done.1, f32[6,12,16,512]{3,2,1,0:T(8,128)S(1)} %get-tuple-element.149), kind=kLoop, calls=%fused_computation.103 | loop fusion | bytes 1179648 | tf_op jit(solution)/shard_map/concatenate | solution.py:21
  55.5 1.1 copy.58
  56.6 1.9 %collective-permute-start.2 = (f32[6,12,2,512]{3,1,2,0:T(8,128)}, f32[6,12,2,512]{3,1,2,0:T(8,128)}, u32[]{:S(2)}, u32[]{:S(2)}) collective-permute-start(f32[6,12,2,512]{3,1,2,0:T(8,128)} %copy.58), channel_id=1, source_target_pairs={{0,1},{1,2},{2,3},{4,5},{5,6},{6,7},{8,9},{9,10},{10,11},{12,13},{... | collective-permute-start | bytes 884744 | tf_op jit(solution)/shard_map/ppermute | solution.py:19
  58.6 0.8 copy.60
  59.4 3.8 %collective-permute-start.3 = (f32[6,12,2,512]{3,1,2,0:T(8,128)}, f32[6,12,2,512]{3,1,2,0:T(8,128)}, u32[]{:S(2)}, u32[]{:S(2)}) collective-permute-start(f32[6,12,2,512]{3,1,2,0:T(8,128)} %copy.60), channel_id=1, source_target_pairs={{1,0},{2,1},{3,2},{5,4},{6,5},{7,6},{9,8},{10,9},{11,10},{13,12},{... | collective-permute-start | bytes 884744 | tf_op jit(solution)/shard_map/ppermute | solution.py:20
  63.2 52.0 %while.4 = (s32[]{:T(128)}, f32[6,128,512]{2,1,0:T(8,128)}, f32[8,4,512]{2,1,0:T(4,128)}, f32[8,4,512]{2,1,0:T(4,128)S(1)}, s32[8,512]{1,0:T(8,128)S(1)}, /*inde...) while((s32[]{:T(128)}, f32[6,128,512]{2,1,0:T(8,128)}, ...), condition=%wide.region_4.5_spmd, body=%wide.region_2.4_spmd.sunk | while | flops 4834109440 | bytes 30824232 | solution.py:137
  63.3 1.6 %convolution_bitcast_fusion.3 = f32[768,512]{0,1:T(8,128)S(1)} fusion(f32[768,512]{1,0:T(8,128)S(1)} %bitcast.139, s32[512]{0:T(512)S(1)} %add_select_fusion.2), kind=kOutput, calls=%fused_computation.4.clone.1 | convolution fusion | flops 2416181248 | bytes 3147776 | tf_op jit(solution)/shard_map/while/body/eval_jaxpr/dot_general | solution.py:116
  65.7 0.6 fusion.76
  66.7 1.8 %fusion.75 = f32[6,128,512]{2,1,0:T(8,128)S(1)} fusion(f32[6,128,512]{2,1,0:T(8,128)S(1)} %copy-done.2, f32[6,512]{1,0:T(8,128)S(1)} %stack.54, f32[128,512]{1,0:T(8,128)S(1)} %fusion.72, s32[512]{0:T(512)S(1)} %add_select_fusion.2), kind=kOutput, calls=%fused_computation.3.clone.1 | convolution fusion | flops 2416967680 | bytes 3422208 | tf_op jit(solution)/shard_map/while/body/eval_jaxpr/dot_general | solution.py:122
  68.6 1.1 copy-done.3
  69.8 1.6 %convolution_bitcast_fusion.3 = f32[768,512]{0,1:T(8,128)S(1)} fusion(f32[768,512]{1,0:T(8,128)S(1)} %bitcast.139, s32[512]{0:T(512)S(1)} %add_select_fusion.2), kind=kOutput, calls=%fused_computation.4.clone.1 | convolution fusion | flops 2416181248 | bytes 3147776 | tf_op jit(solution)/shard_map/while/body/eval_jaxpr/dot_general | solution.py:116
  72.2 0.6 fusion.76
  73.2 1.8 %fusion.75 = f32[6,128,512]{2,1,0:T(8,128)S(1)} fusion(f32[6,128,512]{2,1,0:T(8,128)S(1)} %copy-done.2, f32[6,512]{1,0:T(8,128)S(1)} %stack.54, f32[128,512]{1,0:T(8,128)S(1)} %fusion.72, s32[512]{0:T(512)S(1)} %add_select_fusion.2), kind=kOutput, calls=%fused_computation.3.clone.1 | convolution fusion | flops 2416967680 | bytes 3422208 | tf_op jit(solution)/shard_map/while/body/eval_jaxpr/dot_general | solution.py:122
  75.1 1.1 copy-done.3
  76.3 1.6 %convolution_bitcast_fusion.3 = f32[768,512]{0,1:T(8,128)S(1)} fusion(f32[768,512]{1,0:T(8,128)S(1)} %bitcast.139, s32[512]{0:T(512)S(1)} %add_select_fusion.2), kind=kOutput, calls=%fused_computation.4.clone.1 | convolution fusion | flops 2416181248 | bytes 3147776 | tf_op jit(solution)/shard_map/while/body/eval_jaxpr/dot_general | solution.py:116
  77.9 0.5 copy.81
  78.7 0.6 fusion.76
  79.7 1.8 %fusion.75 = f32[6,128,512]{2,1,0:T(8,128)S(1)} fusion(f32[6,128,512]{2,1,0:T(8,128)S(1)} %copy-done.2, f32[6,512]{1,0:T(8,128)S(1)} %stack.54, f32[128,512]{1,0:T(8,128)S(1)} %fusion.72, s32[512]{0:T(512)S(1)} %add_select_fusion.2), kind=kOutput, calls=%fused_computation.3.clone.1 | convolution fusion | flops 2416967680 | bytes 3422208 | tf_op jit(solution)/shard_map/while/body/eval_jaxpr/dot_general | solution.py:122
  81.6 1.1 copy-done.3
  82.8 1.6 %convolution_bitcast_fusion.3 = f32[768,512]{0,1:T(8,128)S(1)} fusion(f32[768,512]{1,0:T(8,128)S(1)} %bitcast.139, s32[512]{0:T(512)S(1)} %add_select_fusion.2), kind=kOutput, calls=%fused_computation.4.clone.1 | convolution fusion | flops 2416181248 | bytes 3147776 | tf_op jit(solution)/shard_map/while/body/eval_jaxpr/dot_general | solution.py:116
  84.4 0.5 copy.81
  85.2 0.6 fusion.76
  86.2 1.8 %fusion.75 = f32[6,128,512]{2,1,0:T(8,128)S(1)} fusion(f32[6,128,512]{2,1,0:T(8,128)S(1)} %copy-done.2, f32[6,512]{1,0:T(8,128)S(1)} %stack.54, f32[128,512]{1,0:T(8,128)S(1)} %fusion.72, s32[512]{0:T(512)S(1)} %add_select_fusion.2), kind=kOutput, calls=%fused_computation.3.clone.1 | convolution fusion | flops 2416967680 | bytes 3422208 | tf_op jit(solution)/shard_map/while/body/eval_jaxpr/dot_general | solution.py:122
  88.1 1.1 copy-done.3
  89.3 1.6 %convolution_bitcast_fusion.3 = f32[768,512]{0,1:T(8,128)S(1)} fusion(f32[768,512]{1,0:T(8,128)S(1)} %bitcast.139, s32[512]{0:T(512)S(1)} %add_select_fusion.2), kind=kOutput, calls=%fused_computation.4.clone.1 | convolution fusion | flops 2416181248 | bytes 3147776 | tf_op jit(solution)/shard_map/while/body/eval_jaxpr/dot_general | solution.py:116
  91.7 0.6 fusion.76
  92.7 1.8 %fusion.75 = f32[6,128,512]{2,1,0:T(8,128)S(1)} fusion(f32[6,128,512]{2,1,0:T(8,128)S(1)} %copy-done.2, f32[6,512]{1,0:T(8,128)S(1)} %stack.54, f32[128,512]{1,0:T(8,128)S(1)} %fusion.72, s32[512]{0:T(512)S(1)} %add_select_fusion.2), kind=kOutput, calls=%fused_computation.3.clone.1 | convolution fusion | flops 2416967680 | bytes 3422208 | tf_op jit(solution)/shard_map/while/body/eval_jaxpr/dot_general | solution.py:122
  94.6 1.1 copy-done.3
  95.8 1.6 %convolution_bitcast_fusion.3 = f32[768,512]{0,1:T(8,128)S(1)} fusion(f32[768,512]{1,0:T(8,128)S(1)} %bitcast.139, s32[512]{0:T(512)S(1)} %add_select_fusion.2), kind=kOutput, calls=%fused_computation.4.clone.1 | convolution fusion | flops 2416181248 | bytes 3147776 | tf_op jit(solution)/shard_map/while/body/eval_jaxpr/dot_general | solution.py:116
  98.2 0.6 fusion.76
  99.2 1.8 %fusion.75 = f32[6,128,512]{2,1,0:T(8,128)S(1)} fusion(f32[6,128,512]{2,1,0:T(8,128)S(1)} %copy-done.2, f32[6,512]{1,0:T(8,128)S(1)} %stack.54, f32[128,512]{1,0:T(8,128)S(1)} %fusion.72, s32[512]{0:T(512)S(1)} %add_select_fusion.2), kind=kOutput, calls=%fused_computation.3.clone.1 | convolution fusion | flops 2416967680 | bytes 3422208 | tf_op jit(solution)/shard_map/while/body/eval_jaxpr/dot_general | solution.py:122
  101.1 1.1 copy-done.3
  102.3 1.6 %convolution_bitcast_fusion.3 = f32[768,512]{0,1:T(8,128)S(1)} fusion(f32[768,512]{1,0:T(8,128)S(1)} %bitcast.139, s32[512]{0:T(512)S(1)} %add_select_fusion.2), kind=kOutput, calls=%fused_computation.4.clone.1 | convolution fusion | flops 2416181248 | bytes 3147776 | tf_op jit(solution)/shard_map/while/body/eval_jaxpr/dot_general | solution.py:116
  104.7 0.6 fusion.76
  105.7 1.8 %fusion.75 = f32[6,128,512]{2,1,0:T(8,128)S(1)} fusion(f32[6,128,512]{2,1,0:T(8,128)S(1)} %copy-done.2, f32[6,512]{1,0:T(8,128)S(1)} %stack.54, f32[128,512]{1,0:T(8,128)S(1)} %fusion.72, s32[512]{0:T(512)S(1)} %add_select_fusion.2), kind=kOutput, calls=%fused_computation.3.clone.1 | convolution fusion | flops 2416967680 | bytes 3422208 | tf_op jit(solution)/shard_map/while/body/eval_jaxpr/dot_general | solution.py:122
  107.6 1.1 copy-done.3
  108.8 1.6 %convolution_bitcast_fusion.3 = f32[768,512]{0,1:T(8,128)S(1)} fusion(f32[768,512]{1,0:T(8,128)S(1)} %bitcast.139, s32[512]{0:T(512)S(1)} %add_select_fusion.2), kind=kOutput, calls=%fused_computation.4.clone.1 | convolution fusion | flops 2416181248 | bytes 3147776 | tf_op jit(solution)/shard_map/while/body/eval_jaxpr/dot_general | solution.py:116
  111.2 0.6 fusion.76
  112.2 1.8 %fusion.75 = f32[6,128,512]{2,1,0:T(8,128)S(1)} fusion(f32[6,128,512]{2,1,0:T(8,128)S(1)} %copy-done.2, f32[6,512]{1,0:T(8,128)S(1)} %stack.54, f32[128,512]{1,0:T(8,128)S(1)} %fusion.72, s32[512]{0:T(512)S(1)} %add_select_fusion.2), kind=kOutput, calls=%fused_computation.3.clone.1 | convolution fusion | flops 2416967680 | bytes 3422208 | tf_op jit(solution)/shard_map/while/body/eval_jaxpr/dot_general | solution.py:122
  114.1 1.1 copy-done.3
  115.2 0.6 maximum_select_fusion.1
  115.9 1.2 copy.59
  117.1 1.2 copy.61
  118.4 8.9 %fusion.30 = f32[6,8,16,512]{3,2,1,0:T(8,128)} fusion(f32[6,8,16,512]{3,2,1,0:T(8,128)} %bitcast.140, f32[6,8,16,512]{3,2,1,0:T(8,128)S(1)} %get-tuple-element.273, f32[6,8,16,2]{3,2,1,0:T(8,128)S(1)} %copy-done.7, f32[6,8,16,2]{3,2,1,0:T(8,128)S(1)} %copy-done.6, f32[6,12,2,512]{3,2,1,0:T(2,128)S(1)} %copy.61, f32[6,12,16,512]{3,2,1,0:T(8,128)} %copy-done.5, ...), kind=kLoop, calls=%fused_computation.72 | loop fusion | flops 22413312 | bytes 15020032 | tf_op jit(solution)/shard_map/add | solution.py:174
  (180 shorter events, 10.5 us)
Async XLA Ops:
  2.9 26.7 %copy-start = (f32[6,8,16,512]{3,2,1,0:T(8,128)S(1)}, f32[6,8,16,512]{3,2,1,0:T(8,128)}, u32[]{:S(2)}) copy-start(f32[6,8,16,512]{3,2,1,0:T(8,128)} %param.8) | copy-start | bytes 4718596
  7.3 26.1 %copy-start.11 = (f32[4,4096]{1,0:T(4,128)S(1)}, f32[4,4096]{1,0:T(4,128)}, u32[]{:S(2)}) copy-start(f32[4,4096]{1,0:T(4,128)} %param.10) | copy-start | bytes 196612
  7.4 29.0 %collective-permute-start.4 = (f32[5,64]{1,0:T(8,128)S(1)}, f32[5,64]{1,0:T(8,128)S(1)}, u32[]{:S(2)}, u32[]{:S(2)}) collective-permute-start(f32[5,64]{1,0:T(8,128)S(1)} %bitcast.152), channel_id=1, source_target_pairs={{0,4},{4,8},{8,12},{12,16},{16,20},{20,24},{24,28},{28,32},{32,36}... | collective-permute-start | bytes 3848 | tf_op jit(solution)/shard_map/ppermute | solution.py:28
  11.3 34.9 %collective-permute-start.5 = (f32[5,64]{1,0:T(8,128)S(1)}, f32[5,64]{1,0:T(8,128)S(1)}, u32[]{:S(2)}, u32[]{:S(2)}) collective-permute-start(f32[5,64]{1,0:T(8,128)S(1)} %bitcast.150), channel_id=1, source_target_pairs={{4,0},{8,4},{12,8},{16,12},{20,16},{24,20},{28,24},{32,28},{36,32}... | collective-permute-start | bytes 3848 | tf_op jit(solution)/shard_map/ppermute | solution.py:28
  24.1 22.1 %collective-permute-start.6 = (f32[5,64]{1,0:T(8,128)S(1)}, f32[5,64]{1,0:T(8,128)S(1)}, u32[]{:S(2)}, u32[]{:S(2)}) collective-permute-start(f32[5,64]{1,0:T(8,128)S(1)} %bitcast.151), channel_id=1, source_target_pairs={{0,1},{1,2},{2,3},{4,5},{5,6},{6,7},{8,9},{9,10},{10,11},{12,13},{... | collective-permute-start | bytes 3848 | tf_op jit(solution)/shard_map/ppermute | solution.py:28
  26.0 20.1 %collective-permute-start.7 = (f32[5,64]{1,0:T(8,128)S(1)}, f32[5,64]{1,0:T(8,128)S(1)}, u32[]{:S(2)}, u32[]{:S(2)}) collective-permute-start(f32[5,64]{1,0:T(8,128)S(1)} %bitcast.153), channel_id=1, source_target_pairs={{1,0},{2,1},{3,2},{5,4},{6,5},{7,6},{9,8},{10,9},{11,10},{13,12},{... | collective-permute-start | bytes 3848 | tf_op jit(solution)/shard_map/ppermute | solution.py:28
  30.6 19.4 %collective-permute-start = (f32[6,2,16,512]{3,2,1,0:T(8,128)}, f32[6,2,16,512]{3,2,1,0:T(8,128)}, u32[]{:S(2)}, u32[]{:S(2)}) collective-permute-start(f32[6,2,16,512]{3,2,1,0:T(8,128)} %get-tuple-element.152), channel_id=1, source_target_pairs={{0,4},{4,8},{8,12},{12,16},{16,20},{20,24},{24,28},{28,32},{32,36}... | collective-permute-start | bytes 1179656 | tf_op jit(solution)/shard_map/ppermute | solution.py:19
  34.5 1.1 copy-start.10
  34.7 1.7 %copy-start.12 = (s32[4096]{0:T(1024)S(1)}, s32[4096]{0:T(1024)}, u32[]{:S(2)}) copy-start(s32[4096]{0:T(1024)} %param.11) | copy-start | bytes 49156
  36.5 17.0 %collective-permute-start.1 = (f32[6,2,16,512]{3,2,1,0:T(8,128)}, f32[6,2,16,512]{3,2,1,0:T(8,128)}, u32[]{:S(2)}, u32[]{:S(2)}) collective-permute-start(f32[6,2,16,512]{3,2,1,0:T(8,128)} %get-tuple-element.151), channel_id=1, source_target_pairs={{4,0},{8,4},{12,8},{16,12},{20,16},{24,20},{28,24},{32,28},{36,32}... | collective-permute-start | bytes 1179656 | tf_op jit(solution)/shard_map/ppermute | solution.py:20
  52.8 6.6 %copy-start.4 = (f32[6,10,16,512]{3,2,1,0:T(8,128)}, f32[6,10,16,512]{3,2,1,0:T(8,128)S(1)}, u32[]{:S(2)}) copy-start(f32[6,10,16,512]{3,2,1,0:T(8,128)S(1)} %get-tuple-element.148) | copy-start | bytes 5898244
  55.2 8.0 %copy-start.5 = (f32[6,12,16,512]{3,2,1,0:T(8,128)}, f32[6,12,16,512]{3,2,1,0:T(8,128)S(1)}, u32[]{:S(2)}) copy-start(f32[6,12,16,512]{3,2,1,0:T(8,128)S(1)} %get-tuple-element.161) | copy-start | bytes 7077892
  56.6 59.2 %collective-permute-start.2 = (f32[6,12,2,512]{3,1,2,0:T(8,128)}, f32[6,12,2,512]{3,1,2,0:T(8,128)}, u32[]{:S(2)}, u32[]{:S(2)}) collective-permute-start(f32[6,12,2,512]{3,1,2,0:T(8,128)} %copy.58), channel_id=1, source_target_pairs={{0,1},{1,2},{2,3},{4,5},{5,6},{6,7},{8,9},{9,10},{10,11},{12,13},{... | collective-permute-start | bytes 884744 | tf_op jit(solution)/shard_map/ppermute | solution.py:19
  59.4 57.7 %collective-permute-start.3 = (f32[6,12,2,512]{3,1,2,0:T(8,128)}, f32[6,12,2,512]{3,1,2,0:T(8,128)}, u32[]{:S(2)}, u32[]{:S(2)}) collective-permute-start(f32[6,12,2,512]{3,1,2,0:T(8,128)} %copy.60), channel_id=1, source_target_pairs={{1,0},{2,1},{3,2},{5,4},{6,5},{7,6},{9,8},{10,9},{11,10},{13,12},{... | collective-permute-start | bytes 884744 | tf_op jit(solution)/shard_map/ppermute | solution.py:20
  65.3 1.4 %copy-start.2 = (f32[6,128,512]{2,1,0:T(8,128)S(1)}, f32[6,128,512]{2,1,0:T(8,128)}, u32[]{:S(2)}) copy-start(f32[6,128,512]{2,1,0:T(8,128)} %get-tuple-element.245) | copy-start | bytes 4718596 | tf_op jit(solution)/shard_map/while
  66.7 3.0 %copy-start.1 = (f32[6,8,16,512]{3,2,1,0:T(8,128)S(1)}, f32[6,8,16,512]{3,2,1,0:T(8,128)}, u32[]{:S(2)}) copy-start(f32[6,8,16,512]{3,2,1,0:T(8,128)} %get-tuple-element.280) | copy-start | bytes 4718596 | tf_op jit(solution)/shard_map/while
  68.6 1.1 copy-start.3
  71.8 1.4 %copy-start.2 = (f32[6,128,512]{2,1,0:T(8,128)S(1)}, f32[6,128,512]{2,1,0:T(8,128)}, u32[]{:S(2)}) copy-start(f32[6,128,512]{2,1,0:T(8,128)} %get-tuple-element.245) | copy-start | bytes 4718596 | tf_op jit(solution)/shard_map/while
  73.2 3.0 %copy-start.1 = (f32[6,8,16,512]{3,2,1,0:T(8,128)S(1)}, f32[6,8,16,512]{3,2,1,0:T(8,128)}, u32[]{:S(2)}) copy-start(f32[6,8,16,512]{3,2,1,0:T(8,128)} %get-tuple-element.280) | copy-start | bytes 4718596 | tf_op jit(solution)/shard_map/while
  75.1 1.1 copy-start.3
  78.3 1.4 %copy-start.2 = (f32[6,128,512]{2,1,0:T(8,128)S(1)}, f32[6,128,512]{2,1,0:T(8,128)}, u32[]{:S(2)}) copy-start(f32[6,128,512]{2,1,0:T(8,128)} %get-tuple-element.245) | copy-start | bytes 4718596 | tf_op jit(solution)/shard_map/while
  79.7 3.0 %copy-start.1 = (f32[6,8,16,512]{3,2,1,0:T(8,128)S(1)}, f32[6,8,16,512]{3,2,1,0:T(8,128)}, u32[]{:S(2)}) copy-start(f32[6,8,16,512]{3,2,1,0:T(8,128)} %get-tuple-element.280) | copy-start | bytes 4718596 | tf_op jit(solution)/shard_map/while
  81.6 1.1 copy-start.3
  84.8 1.4 %copy-start.2 = (f32[6,128,512]{2,1,0:T(8,128)S(1)}, f32[6,128,512]{2,1,0:T(8,128)}, u32[]{:S(2)}) copy-start(f32[6,128,512]{2,1,0:T(8,128)} %get-tuple-element.245) | copy-start | bytes 4718596 | tf_op jit(solution)/shard_map/while
  86.2 3.0 %copy-start.1 = (f32[6,8,16,512]{3,2,1,0:T(8,128)S(1)}, f32[6,8,16,512]{3,2,1,0:T(8,128)}, u32[]{:S(2)}) copy-start(f32[6,8,16,512]{3,2,1,0:T(8,128)} %get-tuple-element.280) | copy-start | bytes 4718596 | tf_op jit(solution)/shard_map/while
  88.1 1.1 copy-start.3
  91.3 1.4 %copy-start.2 = (f32[6,128,512]{2,1,0:T(8,128)S(1)}, f32[6,128,512]{2,1,0:T(8,128)}, u32[]{:S(2)}) copy-start(f32[6,128,512]{2,1,0:T(8,128)} %get-tuple-element.245) | copy-start | bytes 4718596 | tf_op jit(solution)/shard_map/while
  92.7 3.0 %copy-start.1 = (f32[6,8,16,512]{3,2,1,0:T(8,128)S(1)}, f32[6,8,16,512]{3,2,1,0:T(8,128)}, u32[]{:S(2)}) copy-start(f32[6,8,16,512]{3,2,1,0:T(8,128)} %get-tuple-element.280) | copy-start | bytes 4718596 | tf_op jit(solution)/shard_map/while
  94.6 1.1 copy-start.3
  97.8 1.4 %copy-start.2 = (f32[6,128,512]{2,1,0:T(8,128)S(1)}, f32[6,128,512]{2,1,0:T(8,128)}, u32[]{:S(2)}) copy-start(f32[6,128,512]{2,1,0:T(8,128)} %get-tuple-element.245) | copy-start | bytes 4718596 | tf_op jit(solution)/shard_map/while
  99.2 3.0 %copy-start.1 = (f32[6,8,16,512]{3,2,1,0:T(8,128)S(1)}, f32[6,8,16,512]{3,2,1,0:T(8,128)}, u32[]{:S(2)}) copy-start(f32[6,8,16,512]{3,2,1,0:T(8,128)} %get-tuple-element.280) | copy-start | bytes 4718596 | tf_op jit(solution)/shard_map/while
  101.1 1.1 copy-start.3
  104.3 1.4 %copy-start.2 = (f32[6,128,512]{2,1,0:T(8,128)S(1)}, f32[6,128,512]{2,1,0:T(8,128)}, u32[]{:S(2)}) copy-start(f32[6,128,512]{2,1,0:T(8,128)} %get-tuple-element.245) | copy-start | bytes 4718596 | tf_op jit(solution)/shard_map/while
  105.7 3.0 %copy-start.1 = (f32[6,8,16,512]{3,2,1,0:T(8,128)S(1)}, f32[6,8,16,512]{3,2,1,0:T(8,128)}, u32[]{:S(2)}) copy-start(f32[6,8,16,512]{3,2,1,0:T(8,128)} %get-tuple-element.280) | copy-start | bytes 4718596 | tf_op jit(solution)/shard_map/while
  107.6 1.1 copy-start.3
  110.8 1.4 %copy-start.2 = (f32[6,128,512]{2,1,0:T(8,128)S(1)}, f32[6,128,512]{2,1,0:T(8,128)}, u32[]{:S(2)}) copy-start(f32[6,128,512]{2,1,0:T(8,128)} %get-tuple-element.245) | copy-start | bytes 4718596 | tf_op jit(solution)/shard_map/while
  112.2 3.0 %copy-start.1 = (f32[6,8,16,512]{3,2,1,0:T(8,128)S(1)}, f32[6,8,16,512]{3,2,1,0:T(8,128)}, u32[]{:S(2)}) copy-start(f32[6,8,16,512]{3,2,1,0:T(8,128)} %get-tuple-element.280) | copy-start | bytes 4718596 | tf_op jit(solution)/shard_map/while
  114.1 1.1 copy-start.3
  115.2 3.1 %copy-start.6 = (f32[6,8,16,2]{3,2,1,0:T(8,128)S(1)}, f32[6,8,16,2]{3,2,1,0:T(8,128)}, u32[]{:S(2)}) copy-start(f32[6,8,16,2]{3,2,1,0:T(8,128)} %get-tuple-element.153) | copy-start | bytes 18436
  115.2 3.1 %copy-start.7 = (f32[6,8,16,2]{3,2,1,0:T(8,128)S(1)}, f32[6,8,16,2]{3,2,1,0:T(8,128)}, u32[]{:S(2)}) copy-start(f32[6,8,16,2]{3,2,1,0:T(8,128)} %get-tuple-element.154) | copy-start | bytes 18436
  115.2 3.1 %copy-start.8 = (f32[8,16,512]{2,1,0:T(8,128)S(1)}, f32[8,16,512]{2,1,0:T(8,128)}, u32[]{:S(2)}) copy-start(f32[8,16,512]{2,1,0:T(8,128)} %broadcast_multiply_fusion) | copy-start | bytes 786436
  115.2 3.1 %copy-start.9 = (f32[8,16,512]{2,1,0:T(8,128)S(1)}, f32[8,16,512]{2,1,0:T(8,128)}, u32[]{:S(2)}) copy-start(f32[8,16,512]{2,1,0:T(8,128)} %get-tuple-element.155) | copy-start | bytes 786436
where the time goes:
time: 128 us; the launch traced here: 127 us
  starting transfers between devices  39.5 us (31%)
  matrix products  34.7 us (27%)
  local copies, waits for them, and re-layouts  28.3 us (22%)
  other arithmetic  22.3 us (17%)
    ppermute x4, starting transfers between devices, shifted(): return lax.ppermute(block, axis, route)  22.2 us
    dot_general x9, matrix products, block_update(): deposit = jnp.dot(spread, pick_around, precision=highest)  16.6 us
    dot_general x9, matrix products, block_update(): jnp.dot(gas_rows.reshape(components * row_count, around_count), pick_arou...  13.7 us
    ppermute x2, starting transfers between devices, extended(): after = lax.ppermute(first, axis, down)  13.5 us
    while x48, local copies, waits for them, and re-layouts  11.8 us
    add x1, other arithmetic, body(): gas_out = advanced + summed.reshape(gas_state.shape)  8.86 us
    dynamic_update_slice x8, other arithmetic, sweep_all(): summed, news = lax.scan(step, summed, (pieces, where_all))  4.96 us
    dot_general x1, matrix products, body(): jnp.dot(records, chosen.T, precision=highest)  4.36 us
  transfers between devices with their start and end apart: 8, of which 1 were waited for; matrix products, arithmetic and copies ran while one was open for 42% of the time, Pallas kernels for 0%

commit v1 on v0

v1 whole, which is shorter than its diff:
```python
import functools

import jax
import jax.numpy as jnp
from jax import lax
from jax.experimental import pallas as pl
from jax.experimental.pallas import tpu as pltpu
from jax.sharding import PartitionSpec as P

time_step = 0.2
f32 = jnp.float32
bf16 = jnp.bfloat16
VM = pl.BlockSpec(memory_space=pltpu.VMEM)
SM = pl.BlockSpec(memory_space=pltpu.SMEM)
C, CX, CY, CZ = 6, 8, 16, 512
ROWS = CX * CY
SLOTS, CAP = 4096, 64
params = pltpu.CompilerParams(vmem_limit_bytes=48 << 20)


def split2(x):
    hi = x.astype(bf16)
    return hi, (x - hi.astype(f32)).astype(bf16)


def split3(x):
    hi = x.astype(bf16)
    rest = x - hi.astype(f32)
    mid = rest.astype(bf16)
    return hi, mid, (rest - mid.astype(f32)).astype(bf16)


def prep_kernel(gas, drops, cells, lists, counts, up, down, outer, inner, kept):
    slots = lists[0]
    entry = jnp.concatenate([slots[d : d + 1, :] for d in range(4)], axis=1)
    lane = lax.broadcasted_iota(jnp.int32, (1, CAP), 1)
    used = jnp.concatenate([(lane < counts[0, d]).astype(jnp.int32) for d in range(4)], axis=1)
    low = (lax.broadcasted_iota(jnp.int32, (128, 4 * CAP), 0) == (entry & 127)).astype(f32).astype(bf16)
    place = jnp.where(used > 0, entry >> 7, -1)
    high = (lax.broadcasted_iota(jnp.int32, (32, 4 * CAP), 0) == place).astype(f32)
    fields = []
    for f in range(4):
        fields.append(jnp.concatenate([drops[f : f + 1, 128 * s : 128 * s + 128] for s in range(32)], axis=0))
    parts = []
    for f in range(4):
        parts.extend(split3(fields[f]))
    parts.extend(split2(cells[...].astype(f32)))
    picked = jnp.dot(jnp.concatenate(parts, axis=0), low, preferred_element_type=f32)
    for f in range(5):
        count = 3 if f < 4 else 2
        total = picked[96 * f : 96 * f + 32]
        for k in range(1, count):
            total = total + picked[96 * f + 32 * k : 96 * f + 32 * k + 32]
        chosen = jnp.sum(jnp.where(high > 0, total, 0.0), axis=0, keepdims=True)
        for d, message in enumerate((up, down, outer, inner)):
            base = message.shape[0] - 8
            message[base + f : base + f + 1, 0:CAP] = chosen[:, CAP * d : CAP * d + CAP]
    gone = lax.dot_general(high.astype(bf16), low, (((1,), (1,)), ((), ())), preferred_element_type=f32)
    kept[...] = fields[0] * (1.0 - gone)
    for c in range(C):
        up[32 * c : 32 * c + 32, :] = gas[c, ROWS - 32 : ROWS, :]
        down[32 * c : 32 * c + 32, :] = gas[c, 0:32, :]
        for i in range(CX):
            at = (c * CX + i) * 2
            outer[at : at + 2, :] = gas[c, i * CY + CY - 2 : i * CY + CY, :]
            inner[at : at + 2, :] = gas[c, i * CY : i * CY + 2, :]


def evaporate(mass, temp, axial, radial, samples):
    axial_gas, radial_gas, gas_temp, fuel = samples
    living = mass > 0.0
    safe_temp = jnp.where(living, temp, 1.0)
    root = jnp.where(living, jnp.exp(jnp.log(jnp.where(living, mass, 1.0)) * (1.0 / 3.0)), 0.0)
    balance = jnp.exp(-1.0 / safe_temp)
    slip = (axial_gas - axial) ** 2 + (radial_gas - radial) ** 2
    wind = jnp.sqrt(jnp.sqrt(1.0 + slip))
    evaporated = 0.1 * root * (jnp.log(1.0 - fuel) - jnp.log(1.0 - balance)) * (1.0 + 0.3 * wind)
    updated = (
        mass - evaporated,
        temp + 0.1 * (gas_temp - temp) - 0.5 * evaporated,
        axial + 0.2 * (axial_gas - axial),
        radial + 0.2 * (radial_gas - radial),
    )
    updated = tuple(jnp.where(living, u, 0.0) for u in updated)
    terms = (
        evaporated,
        evaporated * axial + 0.2 * mass * (axial - axial_gas),
        evaporated * radial + 0.2 * mass * (radial - radial_gas),
        evaporated * temp + 0.1 * mass * (temp - gas_temp),
    )
    return updated, terms


def one_hot(index, size):
    width = index.shape[1]
    return (lax.broadcasted_iota(jnp.int32, (size, width), 0) == index).astype(f32).astype(bf16)


def gather_block(table, where):
    around = one_hot(where & (CZ - 1), CZ)
    got = jnp.dot(table[...], around, preferred_element_type=f32)
    mask = lax.broadcasted_iota(jnp.int32, (ROWS, where.shape[1]), 0) == (where >> 9)
    samples = []
    for k in range(4):
        both = got[2 * ROWS * k : 2 * ROWS * k + ROWS] + got[2 * ROWS * k + ROWS : 2 * ROWS * k + 2 * ROWS]
        samples.append(jnp.sum(jnp.where(mask, both, 0.0), axis=0, keepdims=True))
    return samples


def deposit_block(terms, where):
    around = one_hot(where & (CZ - 1), CZ)
    mask = lax.broadcasted_iota(jnp.int32, (ROWS, where.shape[1]), 0) == (where >> 9)
    halves = [split2(t) for t in terms]
    spread = jnp.concatenate(
        [
            jnp.concatenate([jnp.where(mask, h[side].astype(f32), 0.0).astype(bf16) for h in halves], axis=0)
            for side in range(2)
        ],
        axis=1,
    )
    twice = jnp.concatenate([around, around], axis=1)
    return lax.dot_general(spread, twice, (((1,), (1,)), ((), ())), preferred_element_type=f32)


def row_of(ref, lead, first, count):
    return jnp.concatenate([ref[lead, s : s + 1, :] for s in range(first, first + count)], axis=1)


def main_kernel(gas, viscosity, drops, cells, kept, out, drops_out, table, speed, samples, terms, source):
    inverse = 1.0 / gas[0]
    for k, c in enumerate((1, 2, 4, 5)):
        quotient = gas[c] * inverse
        if k < 2:
            speed[k] = quotient
        hi, lo = split2(quotient)
        table[2 * ROWS * k : 2 * ROWS * k + ROWS, :] = hi
        table[2 * ROWS * k + ROWS : 2 * ROWS * k + 2 * ROWS, :] = lo
    speed[2] = gas[3] * inverse

    for b in range(8):
        where = jnp.concatenate([cells[s : s + 1, :] for s in range(4 * b, 4 * b + 4)], axis=1)
        got = gather_block(table, where)
        for k in range(4):
            for s in range(4):
                samples[k, 4 * b + s : 4 * b + s + 1, :] = got[k][:, 128 * s : 128 * s + 128]
    fields = [
        jnp.concatenate([drops[f : f + 1, 128 * s : 128 * s + 128] for s in range(32)], axis=0) for f in range(1, 4)
    ]
    updated, new_terms = evaporate(kept[...], *fields, [samples[k] for k in range(4)])
    for f in range(4):
        terms[f] = new_terms[f]
        for s in range(32):
            drops_out[f : f + 1, 128 * s : 128 * s + 128] = updated[f][s : s + 1, :]
    for b in range(8):
        where = jnp.concatenate([cells[s : s + 1, :] for s in range(4 * b, 4 * b + 4)], axis=1)
        part = deposit_block([row_of(terms, k, 4 * b, 4) for k in range(4)], where)
        if b == 0:
            source[...] = part
        else:
            source[...] += part

    lane = lax.broadcasted_iota(jnp.int32, (CY, CZ), 0)

    def component(c, carry):
        slot = jnp.where(c < 3, c, jnp.where(c == 5, 0, c - 1))
        scale = jnp.where(c == 3, 0.0, 1.0)
        layers = [gas[c, CY * i : CY * i + CY, :] for i in range(CX)]
        for i in range(CX):
            rows = slice(CY * i, CY * i + CY)
            x = layers[i]
            zero = jnp.zeros_like(x)
            ax = [layers[i + k] if 0 <= i + k < CX else zero for k in (-2, -1, 1, 2)]
            ra = []
            for k in (-2, -1, 1, 2):
                moved = pltpu.roll(x, (-k) % CY, axis=0)
                ok = (lane + k >= 0) & (lane + k < CY)
                ra.append(jnp.where(ok, moved, 0.0))
            az = [pltpu.roll(x, (-k) % CZ, axis=1) for k in (-2, -1, 1, 2)]
            near = (ax[1] + ax[2]) + (ra[1] + ra[2]) + (az[1] + az[2])
            far = (ax[0] + ax[3]) + (ra[0] + ra[3]) + (az[0] + az[3])
            laplace = (16.0 * near - far - 90.0 * x) * (1.0 / 12.0)
            transport = zero
            for j, n in enumerate((ax, ra, az)):
                slope = (8.0 * (n[2] - n[1]) - (n[3] - n[0])) * (1.0 / 12.0)
                transport = transport + speed[j, rows, :] * slope
            advanced = x + time_step * (viscosity[rows, :] * laplace - transport)
            out[c, rows, :] = advanced + scale * source[pl.ds(pl.multiple_of(slot * ROWS + CY * i, CY), CY), :]
        return carry

    lax.fori_loop(0, C, component, 0)


def final_kernel(part, gas, viscosity, table, below, above, inner, outer, out, arrivals_out):
    got = jnp.concatenate([m[m.shape[0] - 8 : m.shape[0], 0:CAP] for m in (below, above, inner, outer)], axis=1)
    where = got[4:5].astype(jnp.int32)
    samples = gather_block(table, where)
    updated, terms = evaporate(got[0:1], got[1:2], got[2:3], got[3:4], samples)
    arrivals_out[...] = jnp.concatenate(updated, axis=0)
    source = deposit_block(terms, where)
    lane = lax.broadcasted_iota(jnp.int32, (CY, CZ), 0)
    for i in range(CX):
        rows = slice(CY * i, CY * i + CY)
        inverse = 1.0 / gas[0, rows, :]
        factor = viscosity[rows, :] * (time_step / 12.0)
        axial = gas[1, rows, :] * inverse * (time_step / 12.0)
        radial = gas[2, rows, :] * inverse * (time_step / 12.0)
        wa = (-factor - axial, 16.0 * factor + 8.0 * axial, 16.0 * factor - 8.0 * axial, axial - factor)
        wr = (-factor - radial, 16.0 * factor + 8.0 * radial, 16.0 * factor - 8.0 * radial, radial - factor)
        first = jnp.where(lane == 0, wr[1], jnp.where(lane == 1, wr[0], 0.0))
        second = jnp.where(lane == 0, wr[0], 0.0)
        third = jnp.where(lane == CY - 1, wr[2], jnp.where(lane == CY - 2, wr[3], 0.0))
        fourth = jnp.where(lane == CY - 1, wr[3], 0.0)
        for c in range(C):
            at = (c * CX + i) * 2
            value = part[c, rows, :]
            value = value + first * inner[at + 1 : at + 2, :] + second * inner[at : at + 1, :]
            value = value + third * outer[at : at + 1, :] + fourth * outer[at + 1 : at + 2, :]
            b0, b1 = below[32 * c : 32 * c + CY, :], below[32 * c + CY : 32 * c + 2 * CY, :]
            a0, a1 = above[32 * c : 32 * c + CY, :], above[32 * c + CY : 32 * c + 2 * CY, :]
            if i == 0:
                value = value + wa[0] * b0 + wa[1] * b1
            elif i == 1:
                value = value + wa[0] * b1
            elif i == CX - 2:
                value = value + wa[3] * a0
            elif i == CX - 1:
                value = value + wa[2] * a0 + wa[3] * a1
            slot = (0, 1, 2, None, 3, 0)[c]
            if slot is not None:
                value = value + source[slot * ROWS + CY * i : slot * ROWS + CY * i + CY, :]
            out[c, rows, :] = value


def body(gas_state, viscosity, droplets, drop_cells, move_lists, move_counts):
    gas = gas_state.reshape(C, ROWS, CZ)
    thick = viscosity.reshape(ROWS, CZ)
    cells = drop_cells.reshape(32, 128)
    shape = jax.ShapeDtypeStruct
    up, down, outer, inner, kept = pl.pallas_call(
        prep_kernel,
        out_shape=(
            shape((200, CZ), f32),
            shape((200, CZ), f32),
            shape((104, CZ), f32),
            shape((104, CZ), f32),
            shape((32, 128), f32),
        ),
        in_specs=[VM, VM, VM, VM, SM],
        out_specs=(VM,) * 5,
        compiler_params=params,
        name="prep",
    )(gas, droplets, cells, move_lists, move_counts)
    n_ax, n_rad = lax.axis_size("ax"), lax.axis_size("rad")
    forward = lambda n: [(i, i + 1) for i in range(n - 1)]
    back = lambda n: [(i + 1, i) for i in range(n - 1)]
    from_below = lax.ppermute(up, "ax", forward(n_ax))
    from_above = lax.ppermute(down, "ax", back(n_ax))
    from_inner = lax.ppermute(outer, "rad", forward(n_rad))
    from_outer = lax.ppermute(inner, "rad", back(n_rad))
    part, drops_out, table = pl.pallas_call(
        main_kernel,
        out_shape=(
            shape((C, ROWS, CZ), f32),
            shape((4, SLOTS), f32),
            shape((8 * ROWS, CZ), bf16),
        ),
        in_specs=[VM] * 5,
        out_specs=(VM,) * 3,
        scratch_shapes=[
            pltpu.VMEM((3, ROWS, CZ), f32),
            pltpu.VMEM((4, 32, 128), f32),
            pltpu.VMEM((4, 32, 128), f32),
            pltpu.VMEM((4 * ROWS, CZ), f32),
        ],
        compiler_params=params,
        cost_estimate=pl.CostEstimate(flops=8_000_000_000, bytes_accessed=6_000_000, transcendentals=0),
        name="main",
    )(gas, thick, droplets, cells, kept)
    out, arrivals_out = pl.pallas_call(
        final_kernel,
        out_shape=(shape((C, ROWS, CZ), f32), shape((4, 4 * CAP), f32)),
        in_specs=[VM] * 8,
        out_specs=(VM,) * 2,
        compiler_params=params,
        name="final",
    )(part, gas, thick, table, from_below, from_above, from_inner, from_outer)
    return out.reshape(gas_state.shape), drops_out, arrivals_out


def solution(mesh):
    placed = (
        P(None, "ax", "rad", None),
        P("ax", "rad", None),
        P(None, ("ax", "rad")),
        P(("ax", "rad")),
        P(("ax", "rad"), None, None),
        P(("ax", "rad"), None),
    )
    return jax.shard_map(
        body,
        mesh=mesh,
        in_specs=placed,
        out_specs=(P(None, "ax", "rad", None), P(None, ("ax", "rad")), P(None, ("ax", "rad"))),
        check_vma=False,
    )
```

time: 128 us -> 44.1 us (0.34)
  matrix products: 34.7 us -> 0 us
  local copies, waits for them, and re-layouts: 28.3 us -> 4.3 us
  other arithmetic: 22.3 us -> 0 us
  starting transfers between devices: 39.5 us -> 22.2 us
  Pallas kernels: 0 us -> 16.5 us
    dot_general x19 -> x0, matrix products: 34.7 us -> none  [the longest x9 16.6 us: block_update(): deposit = jnp.dot(spread, pick_around, precision=highest)]
    ppermute x8 -> x4, starting transfers between devices: 39.5 us -> 22.2 us  [the longest x1 12.8 us: body(): from_above = lax.ppermute(down, 'ax', back(n_ax))]
    pallas_call x0 -> x3, Pallas kernels: none -> 16.5 us  [the longest x1 12.7 us: body(): pl.pallas_call(main_kernel, out_shape=(shape((C, ROWS, CZ), f32), shape((...]
    while x48 -> x0, local copies, waits for them, and re-layouts: 11.8 us -> none
    add x10 -> x0, other arithmetic: 8.97 us -> none  [the longest x1 8.86 us: body(): gas_out = advanced + summed.reshape(gas_state.shape)]
    dynamic_update_slice x8 -> x0, other arithmetic: 4.96 us -> none  [sweep_all(): summed, news = lax.scan(step, summed, (pieces, where_all))]
    slice x7 -> x0, local copies, waits for them, and re-layouts: 4.25 us -> none  [the longest x2 1.77 us: extended(): first = lax.slice_in_dim(x, 0, width, axis=dim)]
    dot_general x9 -> x0, local copies, waits for them, and re-layouts: 3.99 us -> none  [block_update(): jnp.dot(gas_rows.reshape(components * row_count, around_count), pick_arou...]
  transfers between devices with their start and end apart: 8 -> 4, of which waited for: 1 -> 0; matrix products, arithmetic and copies ran while one was open for 42% -> 0% of each run, Pallas kernels for 0% -> 29%
where the time goes in v1:
time: 44.1 us; the launch traced here: 43.7 us
  starting transfers between devices  22.2 us (50%)
  Pallas kernels  16.5 us (37%)
  local copies, waits for them, and re-layouts  4.3 us (10%)
  between operations  0.71 us (2%)
    ppermute x1, starting transfers between devices, body(): from_above = lax.ppermute(down, 'ax', back(n_ax))  12.8 us
    pallas_call x1, Pallas kernels, body(): pl.pallas_call(main_kernel, out_shape=(shape((C, ROWS, CZ), f32), shape((...  12.7 us
    unnamed x12, local copies, waits for them, and re-layouts  4.3 us
    ppermute x1, starting transfers between devices, body(): from_below = lax.ppermute(up, 'ax', forward(n_ax))  3.83 us
    ppermute x1, starting transfers between devices, body(): from_outer = lax.ppermute(inner, 'rad', back(n_rad))  3.64 us
    pallas_call x1, Pallas kernels, body(): pl.pallas_call(final_kernel, out_shape=(shape((C, ROWS, CZ), f32), shape(...  2.82 us
    ppermute x1, starting transfers between devices, body(): from_inner = lax.ppermute(outer, 'rad', forward(n_rad))  1.92 us
    pallas_call x1, Pallas kernels, body(): pl.pallas_call(prep_kernel, out_shape=(shape((200, CZ), f32), shape((200,...  1.03 us
  transfers between devices with their start and end apart: 4, of which 0 were waited for; matrix products, arithmetic and copies ran while one was open for 0% of the time, Pallas kernels for 29%

profile of v1, /device:TPU:6, one launch (start us, length us, event | category | flops | bytes accessed | tf_op | source)
XLA Modules:
  0.0 43.7 jit_solution(15384165952100916520)
XLA Ops:
  0.6 0.0 copy-start
  0.6 1.4 %copy-done = f32[6,8,16,512]{3,2,1,0:T(8,128)S(1)} copy-done((f32[6,8,16,512]{3,2,1,0:T(8,128)S(1)}, f32[6,8,16,512]{3,2,1,0:T(8,128)}, u32[]{:S(2)}) %copy-start) | copy-done | bytes 1572888
  2.0 0.0 copy-start.2
  2.0 0.8 %copy-done.2 = f32[4,4096]{1,0:T(4,128)S(1)} copy-done((f32[4,4096]{1,0:T(4,128)S(1)}, f32[4,4096]{1,0:T(4,128)}, u32[]{:S(2)}) %copy-start.2) | copy-done | bytes 65560
  2.9 0.0 copy-start.3
  2.9 0.7 %copy-done.3 = s32[4096]{0:T(1024)S(1)} copy-done((s32[4096]{0:T(1024)S(1)}, s32[4096]{0:T(1024)}, u32[]{:S(2)}) %copy-start.3) | copy-done | bytes 16408
  3.6 0.0 copy-start.4
  3.6 0.7 %copy-done.4 = s32[1,4,64]{2,1,0:T(4,128)S(1)} copy-done((s32[1,4,64]{2,1,0:T(4,128)S(1)}, s32[1,4,64]{2,1,0:T(4,128)}, u32[]{:S(2)}) %copy-start.4) | copy-done | bytes 1048
  4.3 0.0 copy-start.5
  4.3 0.7 %copy-done.5 = s32[1,4]{1,0:T(1,128)S(1)} copy-done((s32[1,4]{1,0:T(1,128)S(1)}, s32[1,4]{1,0:T(1,128)}, u32[]{:S(2)}) %copy-start.5) | copy-done | bytes 40
  4.9 0.0 copy-start.1
  4.9 1.0 %prep.1 = (f32[200,512]{1,0:T(8,128)S(1)}, f32[200,512]{1,0:T(8,128)S(1)}, f32[104,512]{1,0:T(8,128)S(1)}, f32[104,512]{1,0:T(8,128)S(1)}, f32[32,128]{1,0:T(8,128)S(1)}) custom-call(f32[6,128,512]{2,1,0:T(8,128)S(1)} %bitcast.4, f32[4,4096]{1,0:T(4,128)S(1)} %copy-done.2, s32[32,128]{1,0:T(8,128)S(1)} %bitcast.9, s32[1,4,64]{2,1,0:T(4,128)S(1)} %copy-done.4, ...), custom_call_target="tpu_custom_call" | custom-call | tf_op jit(solution)/shard_map/prep/pallas_call | solution.py:239
  6.0 1.9 %collective-permute-start.2 = (f32[104,512]{1,0:T(8,128)S(1)}, f32[104,512]{1,0:T(8,128)S(1)}, u32[]{:S(2)}, u32[]{:S(2)}) collective-permute-start(f32[104,512]{1,0:T(8,128)S(1)} %get-tuple-element.18), channel_id=1, source_target_pairs={{0,1},{1,2},{2,3},{4,5},{5,6},{6,7},{8,9},{9,10},{10,11},{12,13},{... | collective-permute-start | bytes 638984 | tf_op jit(solution)/shard_map/ppermute | solution.py:258
  7.9 3.6 %collective-permute-start.3 = (f32[104,512]{1,0:T(8,128)S(1)}, f32[104,512]{1,0:T(8,128)S(1)}, u32[]{:S(2)}, u32[]{:S(2)}) collective-permute-start(f32[104,512]{1,0:T(8,128)S(1)} %get-tuple-element.19), channel_id=1, source_target_pairs={{1,0},{2,1},{3,2},{5,4},{6,5},{7,6},{9,8},{10,9},{11,10},{13,12},{... | collective-permute-start | bytes 638984 | tf_op jit(solution)/shard_map/ppermute | solution.py:259
  11.6 3.8 %collective-permute-start = (f32[200,512]{1,0:T(8,128)S(1)}, f32[200,512]{1,0:T(8,128)S(1)}, u32[]{:S(2)}, u32[]{:S(2)}) collective-permute-start(f32[200,512]{1,0:T(8,128)S(1)} %get-tuple-element.16), channel_id=1, source_target_pairs={{0,4},{4,8},{8,12},{12,16},{16,20},{20,24},{24,28},{28,32},{32,36}... | collective-permute-start | bytes 1228808 | tf_op jit(solution)/shard_map/ppermute | solution.py:256
  15.4 12.8 %collective-permute-start.1 = (f32[200,512]{1,0:T(8,128)S(1)}, f32[200,512]{1,0:T(8,128)S(1)}, u32[]{:S(2)}, u32[]{:S(2)}) collective-permute-start(f32[200,512]{1,0:T(8,128)S(1)} %get-tuple-element.17), channel_id=1, source_target_pairs={{4,0},{8,4},{12,8},{16,12},{20,16},{24,20},{28,24},{32,28},{36,32}... | collective-permute-start | bytes 1228808 | tf_op jit(solution)/shard_map/ppermute | solution.py:257
  28.2 0.0 copy-done.1
  28.2 12.7 %main.1 = (f32[6,128,512]{2,1,0:T(8,128)S(1)}, f32[4,4096]{1,0:T(4,128)}, bf16[1024,512]{1,0:T(8,128)(2,1)S(1)}) custom-call(f32[6,128,512]{2,1,0:T(8,128)S(1)} %bitcast.5, f32[128,512]{1,0:T(8,128)S(1)} %bitcast.7, f32[4,4096]{1,0:T(4,128)S(1)} %copy-done.2, s32[32,128]{1,0:T(8,128)S(1)} %bitcast.10, f32[32,128]{1,0:T(8,128)S(1)} %get-tuple-element.13.kept), custom_call_target="tpu_custom_call" | custom-call | flops 8000000000 | bytes 6000000 | tf_op jit(solution)/shard_map/main/pallas_call | solution.py:260
  40.9 0.0 collective-permute-done.2.inner
  40.9 0.0 collective-permute-done.3.outer
  40.9 0.0 collective-permute-done.below
  40.9 0.0 collective-permute-done.1.above
  40.9 2.8 %final.1 = (f32[6,128,512]{2,1,0:T(8,128)}, f32[4,256]{1,0:T(4,128)}) custom-call(f32[6,128,512]{2,1,0:T(8,128)S(1)} %get-tuple-element.14.part, f32[6,128,512]{2,1,0:T(8,128)S(1)} %bitcast.6, f32[128,512]{1,0:T(8,128)S(1)} %bitcast.8, bf16[1024,512]{1,0:T(8,128)(2,1)S(1)} %get-tuple-element.15.table, f32[200,512]{1,0:T(8,128)S(1)} %collective-permute-done.below, ...), custom_call_target="tpu_custom_call" | custom-call | tf_op jit(solution)/shard_map/final/pallas_call | solution.py:279
Async XLA Ops:
  0.6 1.4 %copy-start = (f32[6,8,16,512]{3,2,1,0:T(8,128)S(1)}, f32[6,8,16,512]{3,2,1,0:T(8,128)}, u32[]{:S(2)}) copy-start(f32[6,8,16,512]{3,2,1,0:T(8,128)} %param.6) | copy-start | bytes 4718596
  2.0 0.8 %copy-start.2 = (f32[4,4096]{1,0:T(4,128)S(1)}, f32[4,4096]{1,0:T(4,128)}, u32[]{:S(2)}) copy-start(f32[4,4096]{1,0:T(4,128)} %drops.3) | copy-start | bytes 196612
  2.9 0.7 %copy-start.3 = (s32[4096]{0:T(1024)S(1)}, s32[4096]{0:T(1024)}, u32[]{:S(2)}) copy-start(s32[4096]{0:T(1024)} %param.9) | copy-start | bytes 49156
  3.6 0.7 %copy-start.4 = (s32[1,4,64]{2,1,0:T(4,128)S(1)}, s32[1,4,64]{2,1,0:T(4,128)}, u32[]{:S(2)}) copy-start(s32[1,4,64]{2,1,0:T(4,128)} %lists.1) | copy-start | bytes 3076
  4.3 0.7 %copy-start.5 = (s32[1,4]{1,0:T(1,128)S(1)}, s32[1,4]{1,0:T(1,128)}, u32[]{:S(2)}) copy-start(s32[1,4]{1,0:T(1,128)} %counts.1) | copy-start | bytes 52
  4.9 23.3 %copy-start.1 = (f32[8,16,512]{2,1,0:T(8,128)S(1)}, f32[8,16,512]{2,1,0:T(8,128)}, u32[]{:S(2)}) copy-start(f32[8,16,512]{2,1,0:T(8,128)} %param.7) | copy-start | bytes 786436
  6.0 34.9 %collective-permute-start.2 = (f32[104,512]{1,0:T(8,128)S(1)}, f32[104,512]{1,0:T(8,128)S(1)}, u32[]{:S(2)}, u32[]{:S(2)}) collective-permute-start(f32[104,512]{1,0:T(8,128)S(1)} %get-tuple-element.18), channel_id=1, source_target_pairs={{0,1},{1,2},{2,3},{4,5},{5,6},{6,7},{8,9},{9,10},{10,11},{12,13},{... | collective-permute-start | bytes 638984 | tf_op jit(solution)/shard_map/ppermute | solution.py:258
  7.9 33.0 %collective-permute-start.3 = (f32[104,512]{1,0:T(8,128)S(1)}, f32[104,512]{1,0:T(8,128)S(1)}, u32[]{:S(2)}, u32[]{:S(2)}) collective-permute-start(f32[104,512]{1,0:T(8,128)S(1)} %get-tuple-element.19), channel_id=1, source_target_pairs={{1,0},{2,1},{3,2},{5,4},{6,5},{7,6},{9,8},{10,9},{11,10},{13,12},{... | collective-permute-start | bytes 638984 | tf_op jit(solution)/shard_map/ppermute | solution.py:259
  11.6 29.3 %collective-permute-start = (f32[200,512]{1,0:T(8,128)S(1)}, f32[200,512]{1,0:T(8,128)S(1)}, u32[]{:S(2)}, u32[]{:S(2)}) collective-permute-start(f32[200,512]{1,0:T(8,128)S(1)} %get-tuple-element.16), channel_id=1, source_target_pairs={{0,4},{4,8},{8,12},{12,16},{16,20},{20,24},{24,28},{28,32},{32,36}... | collective-permute-start | bytes 1228808 | tf_op jit(solution)/shard_map/ppermute | solution.py:256
  15.4 25.5 %collective-permute-start.1 = (f32[200,512]{1,0:T(8,128)S(1)}, f32[200,512]{1,0:T(8,128)S(1)}, u32[]{:S(2)}, u32[]{:S(2)}) collective-permute-start(f32[200,512]{1,0:T(8,128)S(1)} %get-tuple-element.17), channel_id=1, source_target_pairs={{4,0},{8,4},{12,8},{16,12},{20,16},{24,20},{28,24},{32,28},{36,32}... | collective-permute-start | bytes 1228808 | tf_op jit(solution)/shard_map/ppermute | solution.py:257

commit v2 on v1

--- a/solution.py
+++ b/solution.py
@@ -11,7 +11,7 @@
 f32 = jnp.float32
 bf16 = jnp.bfloat16
 VM = pl.BlockSpec(memory_space=pltpu.VMEM)
-SM = pl.BlockSpec(memory_space=pltpu.SMEM)
+HB = pl.BlockSpec(memory_space=pltpu.HBM)
 C, CX, CY, CZ = 6, 8, 16, 512
 ROWS = CX * CY
 SLOTS, CAP = 4096, 64
@@ -30,7 +30,25 @@
     return hi, mid, (rest - mid.astype(f32)).astype(bf16)
 
 
-def prep_kernel(gas, drops, cells, lists, counts, up, down, outer, inner, kept):
+def parity(axis):
+    return lax.rem(lax.axis_index(axis), 2)
+
+
+def prep_kernel(
+    gas_in, drops_in, cells_in, lists_in, counts_in,
+    axial_a, axial_b, radial_a, radial_b, kept, gas, drops, cells, lists, counts, sems,
+):
+    small = [
+        pltpu.make_async_copy(source, target, sems.at[n])
+        for n, (source, target) in enumerate(
+            ((drops_in, drops), (cells_in, cells), (lists_in, lists), (counts_in, counts))
+        )
+    ]
+    large = [pltpu.make_async_copy(gas_in.at[c], gas.at[c], sems.at[4 + c]) for c in range(C)]
+    for copy in small + large:
+        copy.start()
+    for copy in small:
+        copy.wait()
     slots = lists[0]
     entry = jnp.concatenate([slots[d : d + 1, :] for d in range(4)], axis=1)
     lane = lax.broadcasted_iota(jnp.int32, (1, CAP), 1)
@@ -46,24 +64,38 @@
         parts.extend(split3(fields[f]))
     parts.extend(split2(cells[...].astype(f32)))
     picked = jnp.dot(jnp.concatenate(parts, axis=0), low, preferred_element_type=f32)
+    chosen = []
     for f in range(5):
         count = 3 if f < 4 else 2
         total = picked[96 * f : 96 * f + 32]
         for k in range(1, count):
             total = total + picked[96 * f + 32 * k : 96 * f + 32 * k + 32]
-        chosen = jnp.sum(jnp.where(high > 0, total, 0.0), axis=0, keepdims=True)
-        for d, message in enumerate((up, down, outer, inner)):
-            base = message.shape[0] - 8
-            message[base + f : base + f + 1, 0:CAP] = chosen[:, CAP * d : CAP * d + CAP]
+        chosen.append(jnp.sum(jnp.where(high > 0, total, 0.0), axis=0, keepdims=True))
+    chosen = jnp.concatenate(chosen + [jnp.zeros((3, 4 * CAP), f32)], axis=0)
     gone = lax.dot_general(high.astype(bf16), low, (((1,), (1,)), ((), ())), preferred_element_type=f32)
     kept[...] = fields[0] * (1.0 - gone)
-    for c in range(C):
-        up[32 * c : 32 * c + 32, :] = gas[c, ROWS - 32 : ROWS, :]
-        down[32 * c : 32 * c + 32, :] = gas[c, 0:32, :]
-        for i in range(CX):
-            at = (c * CX + i) * 2
-            outer[at : at + 2, :] = gas[c, i * CY + CY - 2 : i * CY + CY, :]
-            inner[at : at + 2, :] = gas[c, i * CY : i * CY + 2, :]
+    by_way = [chosen[:, CAP * d : CAP * d + CAP] for d in range(4)]
+    odd_ax, odd_rad = parity("ax"), parity("rad")
+    for axis, odd, (even_way, odd_way) in (("ax", odd_ax, (axial_a, axial_b)), ("rad", odd_rad, (radial_a, radial_b))):
+        plus, minus = by_way[0:2] if axis == "ax" else by_way[2:4]
+        base = even_way.shape[0] - 8
+        even_way[base : base + 8, 0:CAP] = jnp.where(odd == 0, plus, minus)
+        odd_way[base : base + 8, 0:CAP] = jnp.where(odd == 0, minus, plus)
+    for copy in large:
+        copy.wait()
+    for message, last in ((axial_a, odd_ax == 0), (axial_b, odd_ax == 1)):
+        near = pl.multiple_of(jnp.where(last, (CX - 1) * CY, 0), CY)
+        far = pl.multiple_of(jnp.where(last, (CX - 2) * CY, CY), CY)
+        for c in range(C):
+            message[32 * c : 32 * c + 16, :] = gas[c, pl.ds(near, CY), :]
+            message[32 * c + 16 : 32 * c + 32, :] = gas[c, pl.ds(far, CY), :]
+    for message, last in ((radial_a, odd_rad == 0), (radial_b, odd_rad == 1)):
+        near, far = jnp.where(last, CY - 1, 0), jnp.where(last, CY - 2, 1)
+        for c in range(C):
+            for i in range(CX):
+                at = c * CX + i
+                message[at : at + 1, :] = gas[c, pl.ds(i * CY + near, 1), :]
+                message[48 + at : 49 + at, :] = gas[c, pl.ds(i * CY + far, 1), :]
 
 
 def evaporate(mass, temp, axial, radial, samples):
@@ -190,8 +222,15 @@
     lax.fori_loop(0, C, component, 0)
 
 
-def final_kernel(part, gas, viscosity, table, below, above, inner, outer, out, arrivals_out):
-    got = jnp.concatenate([m[m.shape[0] - 8 : m.shape[0], 0:CAP] for m in (below, above, inner, outer)], axis=1)
+def final_kernel(part, gas, viscosity, table, axial_a, axial_b, radial_a, radial_b, out, arrivals_out):
+    odd_ax, odd_rad = parity("ax"), parity("rad")
+    got = []
+    for odd, a, b in ((odd_ax, axial_a, axial_b), (odd_rad, radial_a, radial_b)):
+        base = a.shape[0] - 8
+        in_a, in_b = a[base : base + 8, 0:CAP], b[base : base + 8, 0:CAP]
+        got.append(jnp.where(odd == 1, in_a, in_b))
+        got.append(jnp.where(odd == 1, in_b, in_a))
+    got = jnp.concatenate(got, axis=1)
     where = got[4:5].astype(jnp.int32)
     samples = gather_block(table, where)
     updated, terms = evaporate(got[0:1], got[1:2], got[2:3], got[3:4], samples)
@@ -200,35 +239,40 @@
     lane = lax.broadcasted_iota(jnp.int32, (CY, CZ), 0)
     for i in range(CX):
         rows = slice(CY * i, CY * i + CY)
-        inverse = 1.0 / gas[0, rows, :]
         factor = viscosity[rows, :] * (time_step / 12.0)
-        axial = gas[1, rows, :] * inverse * (time_step / 12.0)
-        radial = gas[2, rows, :] * inverse * (time_step / 12.0)
-        wa = (-factor - axial, 16.0 * factor + 8.0 * axial, 16.0 * factor - 8.0 * axial, axial - factor)
-        wr = (-factor - radial, 16.0 * factor + 8.0 * radial, 16.0 * factor - 8.0 * radial, radial - factor)
-        first = jnp.where(lane == 0, wr[1], jnp.where(lane == 1, wr[0], 0.0))
-        second = jnp.where(lane == 0, wr[0], 0.0)
-        third = jnp.where(lane == CY - 1, wr[2], jnp.where(lane == CY - 2, wr[3], 0.0))
-        fourth = jnp.where(lane == CY - 1, wr[3], 0.0)
+        radial = gas[2, rows, :] / gas[0, rows, :] * (time_step / 12.0)
+        weights = []
+        for last in (odd_rad == 0, odd_rad == 1):
+            speed = jnp.where(last, -1.0, 1.0) * radial
+            first, second = jnp.where(last, CY - 1, 0), jnp.where(last, CY - 2, 1)
+            near, far = 16.0 * factor + 8.0 * speed, -(factor + speed)
+            weights.append((jnp.where(lane == first, near, jnp.where(lane == second, far, 0.0)), jnp.where(lane == first, far, 0.0)))
         for c in range(C):
-            at = (c * CX + i) * 2
+            at = c * CX + i
             value = part[c, rows, :]
-            value = value + first * inner[at + 1 : at + 2, :] + second * inner[at : at + 1, :]
-            value = value + third * outer[at : at + 1, :] + fourth * outer[at + 1 : at + 2, :]
-            b0, b1 = below[32 * c : 32 * c + CY, :], below[32 * c + CY : 32 * c + 2 * CY, :]
-            a0, a1 = above[32 * c : 32 * c + CY, :], above[32 * c + CY : 32 * c + 2 * CY, :]
-            if i == 0:
-                value = value + wa[0] * b0 + wa[1] * b1
-            elif i == 1:
-                value = value + wa[0] * b1
-            elif i == CX - 2:
-                value = value + wa[3] * a0
-            elif i == CX - 1:
-                value = value + wa[2] * a0 + wa[3] * a1
+            for (near, far), message in zip(weights, (radial_a, radial_b)):
+                value = value + near * message[at : at + 1, :] + far * message[48 + at : 49 + at, :]
             slot = (0, 1, 2, None, 3, 0)[c]
             if slot is not None:
                 value = value + source[slot * ROWS + CY * i : slot * ROWS + CY * i + CY, :]
             out[c, rows, :] = value
+    for message, last in ((axial_a, odd_ax == 0), (axial_b, odd_ax == 1)):
+        sign = jnp.where(last, -1.0, 1.0)
+        for k in range(2):
+            rows = pl.ds(pl.multiple_of(jnp.where(last, (CX - 1 - k) * CY, k * CY), CY), CY)
+            factor = viscosity[rows, :] * (time_step / 12.0)
+            speed = sign * (gas[1, rows, :] / gas[0, rows, :] * (time_step / 12.0))
+            near, far = 16.0 * factor + 8.0 * speed, -(factor + speed)
+            for c in range(C):
+                if k == 0:
+                    out[c, rows, :] += near * message[32 * c : 32 * c + CY, :] + far * message[32 * c + CY : 32 * c + 2 * CY, :]
+                else:
+                    out[c, rows, :] += far * message[32 * c : 32 * c + CY, :]
+
+
+def pairs(devices):
+    both = lambda first: [p for i in range(first, devices - 1, 2) for p in ((i, i + 1), (i + 1, i))]
+    return both(0), both(1)
 
 
 def body(gas_state, viscosity, droplets, drop_cells, move_lists, move_counts):
@@ -236,7 +280,7 @@
     thick = viscosity.reshape(ROWS, CZ)
     cells = drop_cells.reshape(32, 128)
     shape = jax.ShapeDtypeStruct
-    up, down, outer, inner, kept = pl.pallas_call(
+    axial_a, axial_b, radial_a, radial_b, kept, gas, drops, cells = pl.pallas_call(
         prep_kernel,
         out_shape=(
             shape((200, CZ), f32),
@@ -244,19 +288,26 @@
             shape((104, CZ), f32),
             shape((104, CZ), f32),
             shape((32, 128), f32),
+            shape((C, ROWS, CZ), f32),
+            shape((4, SLOTS), f32),
+            shape((32, 128), jnp.int32),
         ),
-        in_specs=[VM, VM, VM, VM, SM],
-        out_specs=(VM,) * 5,
+        in_specs=[HB] * 5,
+        out_specs=(VM,) * 8,
+        scratch_shapes=[
+            pltpu.VMEM((1, 4, CAP), jnp.int32),
+            pltpu.SMEM((1, 4), jnp.int32),
+            pltpu.SemaphoreType.DMA((10,)),
+        ],
         compiler_params=params,
         name="prep",
-    )(gas, droplets, cells, move_lists, move_counts)
-    n_ax, n_rad = lax.axis_size("ax"), lax.axis_size("rad")
-    forward = lambda n: [(i, i + 1) for i in range(n - 1)]
-    back = lambda n: [(i + 1, i) for i in range(n - 1)]
-    from_below = lax.ppermute(up, "ax", forward(n_ax))
-    from_above = lax.ppermute(down, "ax", back(n_ax))
-    from_inner = lax.ppermute(outer, "rad", forward(n_rad))
-    from_outer = lax.ppermute(inner, "rad", back(n_rad))
+    )(*(pltpu.with_memory_space_constraint(x, pltpu.HBM) for x in (gas, droplets, cells, move_lists, move_counts)))
+    ax_first, ax_second = pairs(lax.axis_size("ax"))
+    rad_first, rad_second = pairs(lax.axis_size("rad"))
+    radial_a = lax.ppermute(radial_a, "rad", rad_first)
+    radial_b = lax.ppermute(radial_b, "rad", rad_second)
+    axial_a = lax.ppermute(axial_a, "ax", ax_first)
+    axial_b = lax.ppermute(axial_b, "ax", ax_second)
     part, drops_out, table = pl.pallas_call(
         main_kernel,
         out_shape=(
@@ -275,7 +326,7 @@
         compiler_params=params,
         cost_estimate=pl.CostEstimate(flops=8_000_000_000, bytes_accessed=6_000_000, transcendentals=0),
         name="main",
-    )(gas, thick, droplets, cells, kept)
+    )(gas, thick, drops, cells, kept)
     out, arrivals_out = pl.pallas_call(
         final_kernel,
         out_shape=(shape((C, ROWS, CZ), f32), shape((4, 4 * CAP), f32)),
@@ -283,7 +334,7 @@
         out_specs=(VM,) * 2,
         compiler_params=params,
         name="final",
-    )(part, gas, thick, table, from_below, from_above, from_inner, from_outer)
+    )(part, gas, thick, table, axial_a, axial_b, radial_a, radial_b)
     return out.reshape(gas_state.shape), drops_out, arrivals_out
 
 

time: 44.1 us -> 40.6 us (0.921)
  local copies, waits for them, and re-layouts: 4.3 us -> 0.01 us
  Pallas kernels: 16.5 us -> 17.6 us
    unnamed x12 -> x2, local copies, waits for them, and re-layouts: 4.3 us -> 0.01 us
    pallas_call x1, Pallas kernels: 1.03 us -> 1.71 us  [body(): pl.pallas_call(prep_kernel, out_shape=(shape((200, CZ), f32), shape((200,...]
  transfers between devices with their start and end apart: 4 -> 4, of which waited for: 0 -> 0; matrix products, arithmetic and copies ran while one was open for 0% -> 0% of each run, Pallas kernels for 29% -> 31%
where the time goes in v2:
time: 40.6 us; the launch traced here: 40.4 us
  starting transfers between devices  22.1 us (54%)
  Pallas kernels  17.6 us (43%)
  between operations  0.7 us (2%)
    ppermute x1, starting transfers between devices, body(): axial_b = lax.ppermute(axial_b, 'ax', ax_second)  13.5 us
    pallas_call x1, Pallas kernels, body(): pl.pallas_call(main_kernel, out_shape=(shape((C, ROWS, CZ), f32), shape((...  12.7 us
    ppermute x1, starting transfers between devices, body(): axial_a = lax.ppermute(axial_a, 'ax', ax_first)  3.83 us
    pallas_call x1, Pallas kernels, body(): pl.pallas_call(final_kernel, out_shape=(shape((C, ROWS, CZ), f32), shape(...  3.23 us
    ppermute x1, starting transfers between devices, body(): radial_b = lax.ppermute(radial_b, 'rad', rad_second)  2.84 us
    ppermute x1, starting transfers between devices, body(): radial_a = lax.ppermute(radial_a, 'rad', rad_first)  1.92 us
    pallas_call x1, Pallas kernels, body(): pl.pallas_call(prep_kernel, out_shape=(shape((200, CZ), f32), shape((200,...  1.71 us
  transfers between devices with their start and end apart: 4, of which 0 were waited for; matrix products, arithmetic and copies ran while one was open for 0% of the time, Pallas kernels for 31%

profile of v2, /device:TPU:6, one launch (start us, length us, event | category | flops | bytes accessed | tf_op | source)
XLA Modules:
  0.0 40.4 jit_solution(4301244207597270768)
XLA Ops:
  0.6 0.0 copy-start
  0.6 1.7 %prep.1 = (f32[200,512]{1,0:T(8,128)S(1)}, f32[200,512]{1,0:T(8,128)S(1)}, f32[104,512]{1,0:T(8,128)S(1)}, f32[104,512]{1,0:T(8,128)S(1)}, f32[32,128]{1,0:T(8,1...) custom-call(f32[6,128,512]{2,1,0:T(8,128)} %bitcast.6, f32[4,4096]{1,0:T(4,128)} %drops_in.1, ...), custom_call_target="tpu_custom_call" | custom-call | tf_op jit(solution)/shard_map/prep/pallas_call | solution.py:283
  2.4 1.9 %collective-permute-start.2 = (f32[104,512]{1,0:T(8,128)S(1)}, f32[104,512]{1,0:T(8,128)S(1)}, u32[]{:S(2)}, u32[]{:S(2)}) collective-permute-start(f32[104,512]{1,0:T(8,128)S(1)} %get-tuple-element.24), channel_id=1, source_target_pairs={{0,1},{1,0},{2,3},{3,2},{4,5},{5,4},{6,7},{7,6},{8,9},{9,8},{10,11... | collective-permute-start | bytes 638984 | tf_op jit(solution)/shard_map/ppermute | solution.py:307
  4.3 2.8 %collective-permute-start.3 = (f32[104,512]{1,0:T(8,128)S(1)}, f32[104,512]{1,0:T(8,128)S(1)}, u32[]{:S(2)}, u32[]{:S(2)}) collective-permute-start(f32[104,512]{1,0:T(8,128)S(1)} %get-tuple-element.25), channel_id=1, source_target_pairs={{1,2},{2,1},{5,6},{6,5},{9,10},{10,9},{13,14},{14,13},{17,18},{18,... | collective-permute-start | bytes 638984 | tf_op jit(solution)/shard_map/ppermute | solution.py:308
  7.1 3.8 %collective-permute-start = (f32[200,512]{1,0:T(8,128)S(1)}, f32[200,512]{1,0:T(8,128)S(1)}, u32[]{:S(2)}, u32[]{:S(2)}) collective-permute-start(f32[200,512]{1,0:T(8,128)S(1)} %get-tuple-element.22), channel_id=1, source_target_pairs={{0,4},{4,0},{8,12},{12,8},{16,20},{20,16},{24,28},{28,24},{32,36},... | collective-permute-start | bytes 1228808 | tf_op jit(solution)/shard_map/ppermute | solution.py:309
  11.0 13.5 %collective-permute-start.1 = (f32[200,512]{1,0:T(8,128)S(1)}, f32[200,512]{1,0:T(8,128)S(1)}, u32[]{:S(2)}, u32[]{:S(2)}) collective-permute-start(f32[200,512]{1,0:T(8,128)S(1)} %get-tuple-element.23), channel_id=1, source_target_pairs={{4,8},{8,4},{12,16},{16,12},{20,24},{24,20},{28,32},{32,28},{36,40... | collective-permute-start | bytes 1228808 | tf_op jit(solution)/shard_map/ppermute | solution.py:310
  24.5 0.0 copy-done
  24.5 12.7 %main.1 = (f32[6,128,512]{2,1,0:T(8,128)S(1)}, f32[4,4096]{1,0:T(4,128)}, bf16[1024,512]{1,0:T(8,128)(2,1)S(1)}) custom-call(f32[6,128,512]{2,1,0:T(8,128)S(1)} %get-tuple-element.16.gas, f32[128,512]{1,0:T(8,128)S(1)} %bitcast.4, f32[4,4096]{1,0:T(4,128)S(1)} %get-tuple-element.17.drops, s32[32,128]{1,0:T(8,128)S(1)} %get-tuple-element.18.cells, ...), custom_call_target="tpu_custom_call" | custom-call | flops 8000000000 | bytes 6000000 | tf_op jit(solution)/shard_map/main/pallas_call | solution.py:311
  37.1 0.0 collective-permute-done.2.radial_a
  37.1 0.0 collective-permute-done.3.radial_b
  37.1 0.0 collective-permute-done.axial_a
  37.2 0.0 collective-permute-done.1.axial_b
  37.2 3.2 %final.1 = (f32[6,128,512]{2,1,0:T(8,128)}, f32[4,256]{1,0:T(4,128)}) custom-call(f32[6,128,512]{2,1,0:T(8,128)S(1)} %get-tuple-element.20.part, f32[6,128,512]{2,1,0:T(8,128)S(1)} %get-tuple-element.16.gas, f32[128,512]{1,0:T(8,128)S(1)} %bitcast.5, bf16[1024,512]{1,0:T(8,128)(2,1)S(1)} %get-tuple-element.21.table, ...), custom_call_target="tpu_custom_call" | custom-call | tf_op jit(solution)/shard_map/final/pallas_call | solution.py:330
Async XLA Ops:
  0.6 23.8 %copy-start = (f32[8,16,512]{2,1,0:T(8,128)S(1)}, f32[8,16,512]{2,1,0:T(8,128)}, u32[]{:S(2)}) copy-start(f32[8,16,512]{2,1,0:T(8,128)} %param.7) | copy-start | bytes 786436
  2.4 34.8 %collective-permute-start.2 = (f32[104,512]{1,0:T(8,128)S(1)}, f32[104,512]{1,0:T(8,128)S(1)}, u32[]{:S(2)}, u32[]{:S(2)}) collective-permute-start(f32[104,512]{1,0:T(8,128)S(1)} %get-tuple-element.24), channel_id=1, source_target_pairs={{0,1},{1,0},{2,3},{3,2},{4,5},{5,4},{6,7},{7,6},{8,9},{9,8},{10,11... | collective-permute-start | bytes 638984 | tf_op jit(solution)/shard_map/ppermute | solution.py:307
  4.3 32.9 %collective-permute-start.3 = (f32[104,512]{1,0:T(8,128)S(1)}, f32[104,512]{1,0:T(8,128)S(1)}, u32[]{:S(2)}, u32[]{:S(2)}) collective-permute-start(f32[104,512]{1,0:T(8,128)S(1)} %get-tuple-element.25), channel_id=1, source_target_pairs={{1,2},{2,1},{5,6},{6,5},{9,10},{10,9},{13,14},{14,13},{17,18},{18,... | collective-permute-start | bytes 638984 | tf_op jit(solution)/shard_map/ppermute | solution.py:308
  7.1 30.0 %collective-permute-start = (f32[200,512]{1,0:T(8,128)S(1)}, f32[200,512]{1,0:T(8,128)S(1)}, u32[]{:S(2)}, u32[]{:S(2)}) collective-permute-start(f32[200,512]{1,0:T(8,128)S(1)} %get-tuple-element.22), channel_id=1, source_target_pairs={{0,4},{4,0},{8,12},{12,8},{16,20},{20,16},{24,28},{28,24},{32,36},... | collective-permute-start | bytes 1228808 | tf_op jit(solution)/shard_map/ppermute | solution.py:309
  11.0 26.2 %collective-permute-start.1 = (f32[200,512]{1,0:T(8,128)S(1)}, f32[200,512]{1,0:T(8,128)S(1)}, u32[]{:S(2)}, u32[]{:S(2)}) collective-permute-start(f32[200,512]{1,0:T(8,128)S(1)} %get-tuple-element.23), channel_id=1, source_target_pairs={{4,8},{8,4},{12,16},{16,12},{20,24},{24,20},{28,32},{32,28},{36,40... | collective-permute-start | bytes 1228808 | tf_op jit(solution)/shard_map/ppermute | solution.py:310

commit v3 on v2

--- a/solution.py
+++ b/solution.py
@@ -15,7 +15,7 @@
 C, CX, CY, CZ = 6, 8, 16, 512
 ROWS = CX * CY
 SLOTS, CAP = 4096, 64
-params = pltpu.CompilerParams(vmem_limit_bytes=48 << 20)
+params = pltpu.CompilerParams(vmem_limit_bytes=30 << 20)
 
 
 def split2(x):
@@ -30,13 +30,21 @@
     return hi, mid, (rest - mid.astype(f32)).astype(bf16)
 
 
+WRAP = 16
+
+
 def parity(axis):
     return lax.rem(lax.axis_index(axis), 2)
 
 
+def is_early():
+    a, r = lax.axis_index("ax"), lax.axis_index("rad")
+    return ((a > 0) & (lax.rem(a, WRAP) == 0)) | ((a == 0) & (r == 1))
+
+
 def prep_kernel(
     gas_in, drops_in, cells_in, lists_in, counts_in,
-    axial_a, axial_b, radial_a, radial_b, kept, gas, drops, cells, lists, counts, sems,
+    axial_b, axial_a, radial_b, radial_a, kept, gas, drops, cells, lists, counts, sems,
 ):
     small = [
         pltpu.make_async_copy(source, target, sems.at[n])
@@ -78,7 +86,7 @@
     odd_ax, odd_rad = parity("ax"), parity("rad")
     for axis, odd, (even_way, odd_way) in (("ax", odd_ax, (axial_a, axial_b)), ("rad", odd_rad, (radial_a, radial_b))):
         plus, minus = by_way[0:2] if axis == "ax" else by_way[2:4]
-        base = even_way.shape[0] - 8
+        base = 192 if axis == "ax" else 96
         even_way[base : base + 8, 0:CAP] = jnp.where(odd == 0, plus, minus)
         odd_way[base : base + 8, 0:CAP] = jnp.where(odd == 0, minus, plus)
     for copy in large:
@@ -156,6 +164,22 @@
 
 def row_of(ref, lead, first, count):
     return jnp.concatenate([ref[lead, s : s + 1, :] for s in range(first, first + count)], axis=1)
+
+
+def early_kernel(gas, viscosity, drops, cells, kept, axial_b, radial_a, late, *refs):
+    @pl.when(is_early())
+    def _():
+        late[...] = axial_b[...]
+
+        @pl.when(lax.axis_index("ax") == 0)
+        def _():
+            late[0:104, :] = radial_a[0:104, :]
+
+        main_kernel(gas, viscosity, drops, cells, kept, *refs)
+
+
+def late_kernel(gas, viscosity, drops, cells, kept, out_in, drops_in, table_in, *refs):
+    pl.when(jnp.logical_not(is_early()))(lambda: main_kernel(gas, viscosity, drops, cells, kept, *refs))
 
 
 def main_kernel(gas, viscosity, drops, cells, kept, out, drops_out, table, speed, samples, terms, source):
@@ -222,12 +246,21 @@
     lax.fori_loop(0, C, component, 0)
 
 
-def final_kernel(part, gas, viscosity, table, axial_a, axial_b, radial_a, radial_b, out, arrivals_out):
+def final_kernel(
+    part, updated_in, gas, viscosity, table, axial_a, axial_b, radial_a_in, radial_b, late,
+    out, drops_out, arrivals_out, radial_a,
+):
     odd_ax, odd_rad = parity("ax"), parity("rad")
+    from_late = lax.rem(lax.axis_index("ax"), WRAP) == WRAP - 1
+    corner = (lax.axis_index("ax") == 0) & (lax.axis_index("rad") == 0)
+    drops_out[...] = updated_in[...]
+    radial_a[...] = jnp.where(corner, late[0:104, :], radial_a_in[0:104, :])
     got = []
     for odd, a, b in ((odd_ax, axial_a, axial_b), (odd_rad, radial_a, radial_b)):
-        base = a.shape[0] - 8
+        base = 192 if a is axial_a else 96
         in_a, in_b = a[base : base + 8, 0:CAP], b[base : base + 8, 0:CAP]
+        if b is axial_b:
+            in_b = jnp.where(from_late, late[base : base + 8, 0:CAP], in_b)
         got.append(jnp.where(odd == 1, in_a, in_b))
         got.append(jnp.where(odd == 1, in_b, in_a))
     got = jnp.concatenate(got, axis=1)
@@ -256,7 +289,8 @@
             if slot is not None:
                 value = value + source[slot * ROWS + CY * i : slot * ROWS + CY * i + CY, :]
             out[c, rows, :] = value
-    for message, last in ((axial_a, odd_ax == 0), (axial_b, odd_ax == 1)):
+
+    def correct(message, last):
         sign = jnp.where(last, -1.0, 1.0)
         for k in range(2):
             rows = pl.ds(pl.multiple_of(jnp.where(last, (CX - 1 - k) * CY, k * CY), CY), CY)
@@ -269,10 +303,27 @@
                 else:
                     out[c, rows, :] += far * message[32 * c : 32 * c + CY, :]
 
-
-def pairs(devices):
-    both = lambda first: [p for i in range(first, devices - 1, 2) for p in ((i, i + 1), (i + 1, i))]
-    return both(0), both(1)
+    correct(axial_a, odd_ax == 0)
+    pl.when(jnp.logical_not(from_late))(lambda: correct(axial_b, odd_ax == 1))
+    pl.when(from_late)(lambda: correct(late, odd_ax == 1))
+
+
+def routes(n_ax, n_rad):
+    flat = lambda a, r: a * n_rad + r
+    axial_a, axial_b, radial_a, radial_b, late = [], [], [], [], []
+    for a in range(n_ax):
+        for r in range(n_rad):
+            if a + 1 < n_ax:
+                up = (flat(a, r), flat(a + 1, r))
+                (axial_a if a % 2 == 0 else axial_b).append(up)
+                down = late if (a + 1) % WRAP == 0 else axial_a if a % 2 == 0 else axial_b
+                down.append(up[::-1])
+            if r + 1 < n_rad:
+                out = (flat(a, r), flat(a, r + 1))
+                (radial_a if r % 2 == 0 else radial_b).append(out)
+                back = late if a == 0 and r == 0 else radial_a if r % 2 == 0 else radial_b
+                back.append(out[::-1])
+    return axial_a, axial_b, radial_a, radial_b, late
 
 
 def body(gas_state, viscosity, droplets, drop_cells, move_lists, move_counts):
@@ -280,13 +331,13 @@
     thick = viscosity.reshape(ROWS, CZ)
     cells = drop_cells.reshape(32, 128)
     shape = jax.ShapeDtypeStruct
-    axial_a, axial_b, radial_a, radial_b, kept, gas, drops, cells = pl.pallas_call(
+    axial_b, axial_a, radial_b, radial_a, kept, gas, drops, cells = pl.pallas_call(
         prep_kernel,
         out_shape=(
             shape((200, CZ), f32),
             shape((200, CZ), f32),
-            shape((104, CZ), f32),
-            shape((104, CZ), f32),
+            shape((200, CZ), f32),
+            shape((200, CZ), f32),
             shape((32, 128), f32),
             shape((C, ROWS, CZ), f32),
             shape((4, SLOTS), f32),
@@ -302,39 +353,51 @@
         compiler_params=params,
         name="prep",
     )(*(pltpu.with_memory_space_constraint(x, pltpu.HBM) for x in (gas, droplets, cells, move_lists, move_counts)))
-    ax_first, ax_second = pairs(lax.axis_size("ax"))
-    rad_first, rad_second = pairs(lax.axis_size("rad"))
-    radial_a = lax.ppermute(radial_a, "rad", rad_first)
-    radial_b = lax.ppermute(radial_b, "rad", rad_second)
-    axial_a = lax.ppermute(axial_a, "ax", ax_first)
-    axial_b = lax.ppermute(axial_b, "ax", ax_second)
-    part, drops_out, table = pl.pallas_call(
-        main_kernel,
-        out_shape=(
-            shape((C, ROWS, CZ), f32),
-            shape((4, SLOTS), f32),
-            shape((8 * ROWS, CZ), bf16),
-        ),
-        in_specs=[VM] * 5,
+    both = ("ax", "rad")
+    to_a, to_b, to_c, to_d, to_late = routes(lax.axis_size("ax"), lax.axis_size("rad"))
+    came_b = lax.ppermute(axial_b, both, to_b)
+    came_a = lax.ppermute(axial_a, both, to_a)
+    came_d = lax.ppermute(radial_b, both, to_d)
+    came_c = lax.ppermute(radial_a, both, to_c)
+
+    results = (shape((C, ROWS, CZ), f32), shape((4, SLOTS), f32), shape((8 * ROWS, CZ), bf16))
+    scratch = [
+        pltpu.VMEM((3, ROWS, CZ), f32),
+        pltpu.VMEM((4, 32, 128), f32),
+        pltpu.VMEM((4, 32, 128), f32),
+        pltpu.VMEM((4 * ROWS, CZ), f32),
+    ]
+    late, *first = pl.pallas_call(
+        early_kernel,
+        out_shape=(shape((200, CZ), f32), *results),
+        in_specs=[VM] * 7,
+        out_specs=(VM,) * 4,
+        scratch_shapes=scratch,
+        compiler_params=params,
+        cost_estimate=pl.CostEstimate(flops=40000000000, bytes_accessed=6_000_000, transcendentals=0),
+        name="early",
+    )(gas, thick, drops, cells, kept, axial_b, radial_a)
+    came_late = lax.ppermute(late, both, to_late)
+    part, updated, table = pl.pallas_call(
+        late_kernel,
+        out_shape=results,
+        in_specs=[VM] * 8,
         out_specs=(VM,) * 3,
-        scratch_shapes=[
-            pltpu.VMEM((3, ROWS, CZ), f32),
-            pltpu.VMEM((4, 32, 128), f32),
-            pltpu.VMEM((4, 32, 128), f32),
-            pltpu.VMEM((4 * ROWS, CZ), f32),
-        ],
+        scratch_shapes=scratch,
         compiler_params=params,
-        cost_estimate=pl.CostEstimate(flops=8_000_000_000, bytes_accessed=6_000_000, transcendentals=0),
-        name="main",
-    )(gas, thick, drops, cells, kept)
-    out, arrivals_out = pl.pallas_call(
+        input_output_aliases={5: 0, 6: 1, 7: 2},
+        cost_estimate=pl.CostEstimate(flops=0, bytes_accessed=0, transcendentals=0),
+        name="late",
+    )(gas, thick, drops, cells, kept, *first)
+    out, drops_out, arrivals_out = pl.pallas_call(
         final_kernel,
-        out_shape=(shape((C, ROWS, CZ), f32), shape((4, 4 * CAP), f32)),
-        in_specs=[VM] * 8,
-        out_specs=(VM,) * 2,
+        out_shape=(shape((C, ROWS, CZ), f32), shape((4, SLOTS), f32), shape((4, 4 * CAP), f32)),
+        in_specs=[VM] * 10,
+        out_specs=(VM,) * 3,
+        scratch_shapes=[pltpu.VMEM((104, CZ), f32)],
         compiler_params=params,
         name="final",
-    )(part, gas, thick, table, axial_a, axial_b, radial_a, radial_b)
+    )(part, updated, gas, thick, table, came_a, came_b, came_c, came_d, came_late)
     return out.reshape(gas_state.shape), drops_out, arrivals_out
 
 

time: 40.6 us -> 39.1 us (0.963)
  the two profiles are of different devices: /device:TPU:6 before, /device:TPU:8 now
where the time goes in v3:
time: 39.1 us; the launch traced here: 38.9 us
  Pallas kernels  17.4 us (45%)
  starting transfers between devices  11.9 us (30%)
  waiting for transfers between devices  8.91 us (23%)
  between operations  0.74 us (2%)
    pallas_call x1, Pallas kernels, body(): pl.pallas_call(early_kernel, out_shape=(shape((200, CZ), f32), *results),...  12.3 us
    ppermute x1, waiting for transfers between devices, body(): came_late = lax.ppermute(late, both, to_late)  8.9 us
    ppermute x1, starting transfers between devices, body(): came_c = lax.ppermute(radial_a, both, to_c)  4.74 us
    ppermute x1, starting transfers between devices, body(): came_a = lax.ppermute(axial_a, both, to_a)  3.83 us
    pallas_call x1, Pallas kernels, body(): pl.pallas_call(final_kernel, out_shape=(shape((C, ROWS, CZ), f32), shape(...  3.19 us
    pallas_call x1, Pallas kernels, body(): pl.pallas_call(prep_kernel, out_shape=(shape((200, CZ), f32), shape((200,...  1.71 us
    ppermute x1, starting transfers between devices, body(): came_late = lax.ppermute(late, both, to_late)  1.32 us
    ppermute x1, starting transfers between devices, body(): came_b = lax.ppermute(axial_b, both, to_b)  1.29 us
  transfers between devices with their start and end apart: 5, of which 1 were waited for; matrix products, arithmetic and copies ran while one was open for 0% of the time, Pallas kernels for 32%

profile of v3, /device:TPU:8, one launch (start us, length us, event | category | flops | bytes accessed | tf_op | source)
XLA Modules:
  0.0 38.9 jit_solution(968422818310056702)
XLA Ops:
  0.6 0.0 copy-start
  0.6 1.7 %prep.1 = (f32[200,512]{1,0:T(8,128)S(1)}, f32[200,512]{1,0:T(8,128)S(1)}, f32[200,512]{1,0:T(8,128)S(1)}, f32[200,512]{1,0:T(8,128)S(1)}, f32[32,128]{1,0:T(8,1...) custom-call(f32[6,128,512]{2,1,0:T(8,128)} %bitcast.7, f32[4,4096]{1,0:T(4,128)} %drops_in.1, ...), custom_call_target="tpu_custom_call" | custom-call | tf_op jit(solution)/shard_map/prep/pallas_call | solution.py:334
  2.4 3.8 %collective-permute-start = (f32[200,512]{1,0:T(8,128)S(1)}, f32[200,512]{1,0:T(8,128)S(1)}, u32[]{:S(2)}, u32[]{:S(2)}) collective-permute-start(f32[200,512]{1,0:T(8,128)S(1)} %get-tuple-element.33), channel_id=1, source_target_pairs={{0,4},{4,0},{1,5},{5,1},{2,6},{6,2},{3,7},{7,3},{8,12},{12,8},{9,1... | collective-permute-start | bytes 1228808 | tf_op jit(solution)/shard_map/ppermute | solution.py:359
  6.2 0.7 %collective-permute-start.3 = (f32[200,512]{1,0:T(8,128)S(1)}, f32[200,512]{1,0:T(8,128)S(1)}, u32[]{:S(2)}, u32[]{:S(2)}) collective-permute-start(f32[200,512]{1,0:T(8,128)S(1)} %get-tuple-element.34), channel_id=1, source_target_pairs={{1,2},{2,1},{5,6},{6,5},{9,10},{10,9},{13,14},{14,13},{17,18},{18,... | collective-permute-start | bytes 1228808 | tf_op jit(solution)/shard_map/ppermute | solution.py:360
  6.9 1.3 %collective-permute-start.1 = (f32[200,512]{1,0:T(8,128)S(1)}, f32[200,512]{1,0:T(8,128)S(1)}, u32[]{:S(2)}, u32[]{:S(2)}) collective-permute-start(f32[200,512]{1,0:T(8,128)S(1)} %get-tuple-element.25.axial_b), channel_id=1, source_target_pairs={{4,8},{8,4},{5,9},{9,5},{6,10},{10,6},{7,11},{11,7},{12,16},{16,12... | collective-permute-start | bytes 1228808 | tf_op jit(solution)/shard_map/ppermute | solution.py:358
  8.2 4.7 %collective-permute-start.2 = (f32[200,512]{1,0:T(8,128)S(1)}, f32[200,512]{1,0:T(8,128)S(1)}, u32[]{:S(2)}, u32[]{:S(2)}) collective-permute-start(f32[200,512]{1,0:T(8,128)S(1)} %get-tuple-element.26.radial_a), channel_id=1, source_target_pairs={{0,1},{2,3},{3,2},{4,5},{5,4},{6,7},{7,6},{8,9},{9,8},{10,11},{11,... | collective-permute-start | bytes 1228808 | tf_op jit(solution)/shard_map/ppermute | solution.py:361
  12.9 0.0 copy-done
  12.9 12.3 %early.1 = (f32[200,512]{1,0:T(8,128)S(1)}, f32[6,128,512]{2,1,0:T(8,128)S(1)}, f32[4,4096]{1,0:T(4,128)S(1)}, bf16[1024,512]{1,0:T(8,128)(2,1)S(1)}) custom-call(f32[6,128,512]{2,1,0:T(8,128)S(1)} %get-tuple-element.21.gas, f32[128,512]{1,0:T(8,128)S(1)} %bitcast.4, f32[4,4096]{1,0:T(4,128)S(1)} %get-tuple-element.22.drops, ...), custom_call_target="tpu_custom_call" | custom-call | flops 40000000000 | bytes 6000000 | tf_op jit(solution)/shard_map/early/pallas_call | solution.py:370
  25.2 1.3 %collective-permute-start.4 = (f32[200,512]{1,0:T(8,128)S(1)}, f32[200,512]{1,0:T(8,128)S(1)}, u32[]{:S(2)}, u32[]{:S(2)}) collective-permute-start(f32[200,512]{1,0:T(8,128)S(1)} %get-tuple-element.35), channel_id=1, source_target_pairs={{1,0},{64,60},{65,61},{66,62},{67,63},{128,124},{129,125},{130,126... | collective-permute-start | bytes 1228808 | tf_op jit(solution)/shard_map/ppermute | solution.py:380
  26.6 0.2 late.1
  26.8 0.0 collective-permute-done.axial_a
  26.8 0.0 collective-permute-done.3.radial_b
  26.8 0.0 collective-permute-done.1.axial_b
  26.8 0.0 collective-permute-done.2.radial_a_in
  26.8 8.9 %collective-permute-done.4.late = f32[200,512]{1,0:T(8,128)S(1)} collective-permute-done((f32[200,512]{1,0:T(8,128)S(1)}, f32[200,512]{1,0:T(8,128)S(1)}, u32[]{:S(2)}, u32[]{:S(2)}) %collective-permute-start.4) | collective-permute-done | bytes 409632 | tf_op jit(solution)/shard_map/ppermute | solution.py:380
  35.7 3.2 %final.1 = (f32[6,128,512]{2,1,0:T(8,128)}, f32[4,4096]{1,0:T(4,128)}, f32[4,256]{1,0:T(4,128)}) custom-call(f32[6,128,512]{2,1,0:T(8,128)S(1)} %get-tuple-element.30.part, f32[4,4096]{1,0:T(4,128)S(1)} %get-tuple-element.31.updated_in, f32[6,128,512]{2,1,0:T(8,128)S(1)} %get-tuple-element.21.gas, f32[128,512]{1,0:T(8,128)S(1)} %bitcast.6, ...), custom_call_target="tpu_custom_call" | custom-call | tf_op jit(solution)/shard_map/final/pallas_call | solution.py:392
Async XLA Ops:
  0.6 12.3 %copy-start = (f32[8,16,512]{2,1,0:T(8,128)S(1)}, f32[8,16,512]{2,1,0:T(8,128)}, u32[]{:S(2)}) copy-start(f32[8,16,512]{2,1,0:T(8,128)} %param.7) | copy-start | bytes 786436
  2.4 24.4 %collective-permute-start = (f32[200,512]{1,0:T(8,128)S(1)}, f32[200,512]{1,0:T(8,128)S(1)}, u32[]{:S(2)}, u32[]{:S(2)}) collective-permute-start(f32[200,512]{1,0:T(8,128)S(1)} %get-tuple-element.33), channel_id=1, source_target_pairs={{0,4},{4,0},{1,5},{5,1},{2,6},{6,2},{3,7},{7,3},{8,12},{12,8},{9,1... | collective-permute-start | bytes 1228808 | tf_op jit(solution)/shard_map/ppermute | solution.py:359
  6.2 20.6 %collective-permute-start.3 = (f32[200,512]{1,0:T(8,128)S(1)}, f32[200,512]{1,0:T(8,128)S(1)}, u32[]{:S(2)}, u32[]{:S(2)}) collective-permute-start(f32[200,512]{1,0:T(8,128)S(1)} %get-tuple-element.34), channel_id=1, source_target_pairs={{1,2},{2,1},{5,6},{6,5},{9,10},{10,9},{13,14},{14,13},{17,18},{18,... | collective-permute-start | bytes 1228808 | tf_op jit(solution)/shard_map/ppermute | solution.py:360
  6.9 19.9 %collective-permute-start.1 = (f32[200,512]{1,0:T(8,128)S(1)}, f32[200,512]{1,0:T(8,128)S(1)}, u32[]{:S(2)}, u32[]{:S(2)}) collective-permute-start(f32[200,512]{1,0:T(8,128)S(1)} %get-tuple-element.25.axial_b), channel_id=1, source_target_pairs={{4,8},{8,4},{5,9},{9,5},{6,10},{10,6},{7,11},{11,7},{12,16},{16,12... | collective-permute-start | bytes 1228808 | tf_op jit(solution)/shard_map/ppermute | solution.py:358
  8.2 18.6 %collective-permute-start.2 = (f32[200,512]{1,0:T(8,128)S(1)}, f32[200,512]{1,0:T(8,128)S(1)}, u32[]{:S(2)}, u32[]{:S(2)}) collective-permute-start(f32[200,512]{1,0:T(8,128)S(1)} %get-tuple-element.26.radial_a), channel_id=1, source_target_pairs={{0,1},{2,3},{3,2},{4,5},{5,4},{6,7},{7,6},{8,9},{9,8},{10,11},{11,... | collective-permute-start | bytes 1228808 | tf_op jit(solution)/shard_map/ppermute | solution.py:361
  25.2 10.5 %collective-permute-start.4 = (f32[200,512]{1,0:T(8,128)S(1)}, f32[200,512]{1,0:T(8,128)S(1)}, u32[]{:S(2)}, u32[]{:S(2)}) collective-permute-start(f32[200,512]{1,0:T(8,128)S(1)} %get-tuple-element.35), channel_id=1, source_target_pairs={{1,0},{64,60},{65,61},{66,62},{67,63},{128,124},{129,125},{130,126... | collective-permute-start | bytes 1228808 | tf_op jit(solution)/shard_map/ppermute | solution.py:380

commit v4 on v3

--- a/solution.py
+++ b/solution.py
@@ -162,10 +162,6 @@
     return lax.dot_general(spread, twice, (((1,), (1,)), ((), ())), preferred_element_type=f32)
 
 
-def row_of(ref, lead, first, count):
-    return jnp.concatenate([ref[lead, s : s + 1, :] for s in range(first, first + count)], axis=1)
-
-
 def early_kernel(gas, viscosity, drops, cells, kept, axial_b, radial_a, late, *refs):
     @pl.when(is_early())
     def _():
@@ -193,12 +189,20 @@
         table[2 * ROWS * k + ROWS : 2 * ROWS * k + 2 * ROWS, :] = lo
     speed[2] = gas[3] * inverse
 
-    for b in range(8):
-        where = jnp.concatenate([cells[s : s + 1, :] for s in range(4 * b, 4 * b + 4)], axis=1)
+    slot = lax.broadcasted_iota(jnp.int32, (1, SLOTS), 1)
+    filled = jnp.max(jnp.where(drops[0:1, :] > 0.0, slot + 1, 0))
+    blocks = lax.div(filled + 511, 512)
+
+    def sample(b, carry):
+        first = pl.multiple_of(4 * b, 4)
+        where = jnp.concatenate([cells[pl.ds(first + s, 1), :] for s in range(4)], axis=1)
         got = gather_block(table, where)
         for k in range(4):
             for s in range(4):
-                samples[k, 4 * b + s : 4 * b + s + 1, :] = got[k][:, 128 * s : 128 * s + 128]
+                samples[k, pl.ds(first + s, 1), :] = got[k][:, 128 * s : 128 * s + 128]
+        return carry
+
+    lax.fori_loop(0, blocks, sample, 0)
     fields = [
         jnp.concatenate([drops[f : f + 1, 128 * s : 128 * s + 128] for s in range(32)], axis=0) for f in range(1, 4)
     ]
@@ -207,14 +211,16 @@
         terms[f] = new_terms[f]
         for s in range(32):
             drops_out[f : f + 1, 128 * s : 128 * s + 128] = updated[f][s : s + 1, :]
-    for b in range(8):
-        where = jnp.concatenate([cells[s : s + 1, :] for s in range(4 * b, 4 * b + 4)], axis=1)
-        part = deposit_block([row_of(terms, k, 4 * b, 4) for k in range(4)], where)
-        if b == 0:
-            source[...] = part
-        else:
-            source[...] += part
-
+    source[...] = jnp.zeros_like(source)
+
+    def deposit(b, carry):
+        first = pl.multiple_of(4 * b, 4)
+        row = lambda load: jnp.concatenate([load(pl.ds(first + s, 1)) for s in range(4)], axis=1)
+        where = row(lambda at: cells[at, :])
+        source[...] += deposit_block([row(lambda at: terms[k, at, :]) for k in range(4)], where)
+        return carry
+
+    lax.fori_loop(0, blocks, deposit, 0)
     lane = lax.broadcasted_iota(jnp.int32, (CY, CZ), 0)
 
     def component(c, carry):
@@ -246,66 +252,89 @@
     lax.fori_loop(0, C, component, 0)
 
 
+def is_last():
+    a, r = lax.axis_index("ax"), lax.axis_index("rad")
+    return ((lax.rem(a, WRAP) == WRAP - 1) & (a < lax.axis_size("ax") - 1)) | ((a == 0) & (r == 0))
+
+
+def soon_kernel(*refs):
+    pl.when(jnp.logical_not(is_last()))(lambda: final_kernel(None, *refs))
+
+
+def last_kernel(late, part, updated, gas, viscosity, table, axial_a, axial_b, radial_a, radial_b, *refs):
+    given = (part, updated, gas, viscosity, table, axial_a, axial_b, radial_a, radial_b)
+    pl.when(is_last())(lambda: final_kernel(late, *given, *refs[3:]))
+
+
 def final_kernel(
-    part, updated_in, gas, viscosity, table, axial_a, axial_b, radial_a_in, radial_b, late,
-    out, drops_out, arrivals_out, radial_a,
+    late, part, updated_in, gas, viscosity, table, axial_a, axial_b_in, radial_a_in, radial_b,
+    out_hbm, drops_hbm, arrivals_hbm, out, arrivals, axial_b, radial_a, weights, sems,
 ):
+    copies = [
+        pltpu.make_async_copy(updated_in, drops_hbm, sems.at[0]),
+        pltpu.make_async_copy(arrivals, arrivals_hbm, sems.at[1]),
+    ] + [pltpu.make_async_copy(out.at[c], out_hbm.at[c], sems.at[2 + c]) for c in range(C)]
+    copies[0].start()
     odd_ax, odd_rad = parity("ax"), parity("rad")
-    from_late = lax.rem(lax.axis_index("ax"), WRAP) == WRAP - 1
-    corner = (lax.axis_index("ax") == 0) & (lax.axis_index("rad") == 0)
-    drops_out[...] = updated_in[...]
-    radial_a[...] = jnp.where(corner, late[0:104, :], radial_a_in[0:104, :])
+    if late is None:
+        axial_b, radial_a = axial_b_in, radial_a_in
+    else:
+        corner = lax.axis_index("ax") == 0
+        axial_b[...] = jnp.where(corner, axial_b_in[...], late[...])
+        radial_a[0:104, :] = jnp.where(corner, late[0:104, :], radial_a_in[0:104, :])
     got = []
-    for odd, a, b in ((odd_ax, axial_a, axial_b), (odd_rad, radial_a, radial_b)):
-        base = 192 if a is axial_a else 96
+    for odd, a, b, base in ((odd_ax, axial_a, axial_b, 192), (odd_rad, radial_a, radial_b, 96)):
         in_a, in_b = a[base : base + 8, 0:CAP], b[base : base + 8, 0:CAP]
-        if b is axial_b:
-            in_b = jnp.where(from_late, late[base : base + 8, 0:CAP], in_b)
         got.append(jnp.where(odd == 1, in_a, in_b))
         got.append(jnp.where(odd == 1, in_b, in_a))
     got = jnp.concatenate(got, axis=1)
     where = got[4:5].astype(jnp.int32)
     samples = gather_block(table, where)
-    updated, terms = evaporate(got[0:1], got[1:2], got[2:3], got[3:4], samples)
-    arrivals_out[...] = jnp.concatenate(updated, axis=0)
+    changed, terms = evaporate(got[0:1], got[1:2], got[2:3], got[3:4], samples)
+    arrivals[...] = jnp.concatenate(changed, axis=0)
+    copies[1].start()
     source = deposit_block(terms, where)
     lane = lax.broadcasted_iota(jnp.int32, (CY, CZ), 0)
     for i in range(CX):
         rows = slice(CY * i, CY * i + CY)
         factor = viscosity[rows, :] * (time_step / 12.0)
         radial = gas[2, rows, :] / gas[0, rows, :] * (time_step / 12.0)
-        weights = []
-        for last in (odd_rad == 0, odd_rad == 1):
+        for n, last in enumerate((odd_rad == 0, odd_rad == 1)):
             speed = jnp.where(last, -1.0, 1.0) * radial
             first, second = jnp.where(last, CY - 1, 0), jnp.where(last, CY - 2, 1)
             near, far = 16.0 * factor + 8.0 * speed, -(factor + speed)
-            weights.append((jnp.where(lane == first, near, jnp.where(lane == second, far, 0.0)), jnp.where(lane == first, far, 0.0)))
-        for c in range(C):
+            weights[2 * n, rows, :] = jnp.where(lane == first, near, jnp.where(lane == second, far, 0.0))
+            weights[2 * n + 1, rows, :] = jnp.where(lane == first, far, 0.0)
+    edges = []
+    for message, last in ((axial_a, odd_ax == 0), (axial_b, odd_ax == 1)):
+        sign = jnp.where(last, -1.0, 1.0)
+        for k in range(2):
+            rows = pl.ds(pl.multiple_of(jnp.where(last, (CX - 1 - k) * CY, k * CY), CY), CY)
+            edges.append((message, k, rows, sign))
+    for c in range(C):
+        for i in range(CX):
+            rows = slice(CY * i, CY * i + CY)
             at = c * CX + i
             value = part[c, rows, :]
-            for (near, far), message in zip(weights, (radial_a, radial_b)):
-                value = value + near * message[at : at + 1, :] + far * message[48 + at : 49 + at, :]
+            for n, message in enumerate((radial_a, radial_b)):
+                value = value + weights[2 * n, rows, :] * message[at : at + 1, :]
+                value = value + weights[2 * n + 1, rows, :] * message[48 + at : 49 + at, :]
             slot = (0, 1, 2, None, 3, 0)[c]
             if slot is not None:
                 value = value + source[slot * ROWS + CY * i : slot * ROWS + CY * i + CY, :]
             out[c, rows, :] = value
-
-    def correct(message, last):
-        sign = jnp.where(last, -1.0, 1.0)
-        for k in range(2):
-            rows = pl.ds(pl.multiple_of(jnp.where(last, (CX - 1 - k) * CY, k * CY), CY), CY)
+        for message, k, rows, sign in edges:
             factor = viscosity[rows, :] * (time_step / 12.0)
             speed = sign * (gas[1, rows, :] / gas[0, rows, :] * (time_step / 12.0))
             near, far = 16.0 * factor + 8.0 * speed, -(factor + speed)
-            for c in range(C):
-                if k == 0:
-                    out[c, rows, :] += near * message[32 * c : 32 * c + CY, :] + far * message[32 * c + CY : 32 * c + 2 * CY, :]
-                else:
-                    out[c, rows, :] += far * message[32 * c : 32 * c + CY, :]
-
-    correct(axial_a, odd_ax == 0)
-    pl.when(jnp.logical_not(from_late))(lambda: correct(axial_b, odd_ax == 1))
-    pl.when(from_late)(lambda: correct(late, odd_ax == 1))
+            if k == 0:
+                change = near * message[32 * c : 32 * c + CY, :] + far * message[32 * c + CY : 32 * c + 2 * CY, :]
+            else:
+                change = far * message[32 * c : 32 * c + CY, :]
+            out[c, rows, :] += change
+        copies[2 + c].start()
+    for copy in copies:
+        copy.wait()
 
 
 def routes(n_ax, n_rad):
@@ -336,8 +365,8 @@
         out_shape=(
             shape((200, CZ), f32),
             shape((200, CZ), f32),
-            shape((200, CZ), f32),
-            shape((200, CZ), f32),
+            shape((104, CZ), f32),
+            shape((104, CZ), f32),
             shape((32, 128), f32),
             shape((C, ROWS, CZ), f32),
             shape((4, SLOTS), f32),
@@ -389,15 +418,37 @@
         cost_estimate=pl.CostEstimate(flops=0, bytes_accessed=0, transcendentals=0),
         name="late",
     )(gas, thick, drops, cells, kept, *first)
+    finals = (shape((C, ROWS, CZ), f32), shape((4, SLOTS), f32), shape((4, 4 * CAP), f32))
+    scratch = [
+        pltpu.VMEM((C, ROWS, CZ), f32),
+        pltpu.VMEM((4, 4 * CAP), f32),
+        pltpu.VMEM((200, CZ), f32),
+        pltpu.VMEM((104, CZ), f32),
+        pltpu.VMEM((4, ROWS, CZ), f32),
+        pltpu.SemaphoreType.DMA((8,)),
+    ]
+    common = (part, updated, gas, thick, table, came_a, came_b, came_c, came_d)
+    finals_soon = pl.pallas_call(
+        soon_kernel,
+        out_shape=finals,
+        in_specs=[VM] * 9,
+        out_specs=(HB,) * 3,
+        scratch_shapes=scratch,
+        compiler_params=params,
+        cost_estimate=pl.CostEstimate(flops=4_000_000_000, bytes_accessed=3_000_000, transcendentals=0),
+        name="soon",
+    )(*common)
     out, drops_out, arrivals_out = pl.pallas_call(
-        final_kernel,
-        out_shape=(shape((C, ROWS, CZ), f32), shape((4, SLOTS), f32), shape((4, 4 * CAP), f32)),
-        in_specs=[VM] * 10,
-        out_specs=(VM,) * 3,
-        scratch_shapes=[pltpu.VMEM((104, CZ), f32)],
+        last_kernel,
+        out_shape=finals,
+        in_specs=[VM] * 10 + [HB] * 3,
+        out_specs=(HB,) * 3,
+        scratch_shapes=scratch,
         compiler_params=params,
-        name="final",
-    )(part, updated, gas, thick, table, came_a, came_b, came_c, came_d, came_late)
+        input_output_aliases={10: 0, 11: 1, 12: 2},
+        cost_estimate=pl.CostEstimate(flops=0, bytes_accessed=0, transcendentals=0),
+        name="last",
+    )(came_late, *common, *finals_soon)
     return out.reshape(gas_state.shape), drops_out, arrivals_out
 
 

time: 39.1 us -> 36.6 us (0.936)
  the two profiles are of different devices: /device:TPU:8 before, /device:TPU:6 now
where the time goes in v4:
time: 36.6 us; the launch traced here: 36.1 us
  starting transfers between devices  16.1 us (44%)
  Pallas kernels  11.5 us (31%)
  waiting for transfers between devices  7.77 us (21%)
  between operations  0.75 us (2%)
    ppermute x1, waiting for transfers between devices, body(): came_b = lax.ppermute(axial_b, both, to_b)  7.76 us
    ppermute x1, starting transfers between devices, body(): came_late = lax.ppermute(late, both, to_late)  6.92 us
    pallas_call x1, Pallas kernels, body(): pl.pallas_call(early_kernel, out_shape=(shape((200, CZ), f32), *results),...  6.67 us
    ppermute x1, starting transfers between devices, body(): came_a = lax.ppermute(axial_a, both, to_a)  3.83 us
    pallas_call x1, Pallas kernels, body(): pl.pallas_call(soon_kernel, out_shape=finals, in_specs=[VM] * 9, out_spec...  2.96 us
    ppermute x1, starting transfers between devices, body(): came_d = lax.ppermute(radial_b, both, to_d)  2.18 us
    ppermute x1, starting transfers between devices, body(): came_c = lax.ppermute(radial_a, both, to_c)  1.92 us
    pallas_call x1, Pallas kernels, body(): pl.pallas_call(prep_kernel, out_shape=(shape((200, CZ), f32), shape((200,...  1.71 us
  transfers between devices with their start and end apart: 5, of which 1 were waited for; matrix products, arithmetic and copies ran while one was open for 0% of the time, Pallas kernels for 27%

profile of v4, /device:TPU:6, one launch (start us, length us, event | category | flops | bytes accessed | tf_op | source)
XLA Modules:
  0.0 36.1 jit_solution(7114563702119509549)
XLA Ops:
  0.6 0.0 copy-start
  0.6 1.7 %prep.1 = (f32[200,512]{1,0:T(8,128)S(1)}, f32[200,512]{1,0:T(8,128)S(1)}, f32[104,512]{1,0:T(8,128)S(1)}, f32[104,512]{1,0:T(8,128)S(1)}, f32[32,128]{1,0:T(8,1...) custom-call(f32[6,128,512]{2,1,0:T(8,128)} %bitcast.9, f32[4,4096]{1,0:T(4,128)} %drops_in.1, ...), custom_call_target="tpu_custom_call" | custom-call | tf_op jit(solution)/shard_map/prep/pallas_call | solution.py:363
  2.4 2.2 %collective-permute-start.4 = (f32[104,512]{1,0:T(8,128)S(1)}, f32[104,512]{1,0:T(8,128)S(1)}, u32[]{:S(2)}, u32[]{:S(2)}) collective-permute-start(f32[104,512]{1,0:T(8,128)S(1)} %get-tuple-element.38), channel_id=1, source_target_pairs={{1,2},{2,1},{5,6},{6,5},{9,10},{10,9},{13,14},{14,13},{17,18},{18,... | collective-permute-start | bytes 638984 | tf_op jit(solution)/shard_map/ppermute | solution.py:389
  4.5 1.9 %collective-permute-start.3 = (f32[104,512]{1,0:T(8,128)S(1)}, f32[104,512]{1,0:T(8,128)S(1)}, u32[]{:S(2)}, u32[]{:S(2)}) collective-permute-start(f32[104,512]{1,0:T(8,128)S(1)} %get-tuple-element.29.radial_a), channel_id=1, source_target_pairs={{0,1},{2,3},{3,2},{4,5},{5,4},{6,7},{7,6},{8,9},{9,8},{10,11},{11,... | collective-permute-start | bytes 638984 | tf_op jit(solution)/shard_map/ppermute | solution.py:390
  6.5 3.8 %collective-permute-start.1 = (f32[200,512]{1,0:T(8,128)S(1)}, f32[200,512]{1,0:T(8,128)S(1)}, u32[]{:S(2)}, u32[]{:S(2)}) collective-permute-start(f32[200,512]{1,0:T(8,128)S(1)} %get-tuple-element.37), channel_id=1, source_target_pairs={{0,4},{4,0},{1,5},{5,1},{2,6},{6,2},{3,7},{7,3},{8,12},{12,8},{9,1... | collective-permute-start | bytes 1228808 | tf_op jit(solution)/shard_map/ppermute | solution.py:388
  10.3 1.3 %collective-permute-start.2 = (f32[200,512]{1,0:T(8,128)S(1)}, f32[200,512]{1,0:T(8,128)S(1)}, u32[]{:S(2)}, u32[]{:S(2)}) collective-permute-start(f32[200,512]{1,0:T(8,128)S(1)} %get-tuple-element.28.axial_b), channel_id=1, source_target_pairs={{4,8},{8,4},{5,9},{9,5},{6,10},{10,6},{7,11},{11,7},{12,16},{16,12... | collective-permute-start | bytes 1228808 | tf_op jit(solution)/shard_map/ppermute | solution.py:387
  11.6 0.0 copy-done
  11.6 6.7 %early.1 = (f32[200,512]{1,0:T(8,128)S(1)}, f32[6,128,512]{2,1,0:T(8,128)S(1)}, f32[4,4096]{1,0:T(4,128)S(1)}, bf16[1024,512]{1,0:T(8,128)(2,1)S(1)}) custom-call(f32[6,128,512]{2,1,0:T(8,128)S(1)} %get-tuple-element.24.gas.refs_2_, f32[128,512]{1,0:T(8,128)S(1)} %bitcast.4, f32[4,4096]{1,0:T(4,128)S(1)} %get-tuple-element.25.drops, ...), custom_call_target="tpu_custom_call" | custom-call | flops 40000000000 | bytes 6000000 | tf_op jit(solution)/shard_map/early/pallas_call | solution.py:399
  18.3 6.9 %collective-permute-start = (f32[200,512]{1,0:T(8,128)S(1)}, f32[200,512]{1,0:T(8,128)S(1)}, u32[]{:S(2)}, u32[]{:S(2)}) collective-permute-start(f32[200,512]{1,0:T(8,128)S(1)} %get-tuple-element.30), channel_id=1, source_target_pairs={{1,0},{64,60},{65,61},{66,62},{67,63},{128,124},{129,125},{130,126... | collective-permute-start | bytes 1228808 | tf_op jit(solution)/shard_map/ppermute | solution.py:409
  25.3 0.0 collective-permute-done.4.refs_8_.radial_b
  25.3 0.0 collective-permute-done.3.refs_7_.radial_a
  25.3 0.0 collective-permute-done.1.refs_5_.axial_a
  25.3 7.8 %collective-permute-done.2.refs_6_.axial_b = f32[200,512]{1,0:T(8,128)S(1)} collective-permute-done((f32[200,512]{1,0:T(8,128)S(1)}, f32[200,512]{1,0:T(8,128)S(1)}, u32[]{:S(2)}, u32[]{:S(2)}) %collective-permute-start.2) | collective-permute-done | bytes 409632 | tf_op jit(solution)/shard_map/ppermute | solution.py:387
  33.0 3.0 %soon.1 = (f32[6,128,512]{2,1,0:T(8,128)}, f32[4,4096]{1,0:T(4,128)}, f32[4,256]{1,0:T(4,128)}) custom-call(f32[6,128,512]{2,1,0:T(8,128)S(1)} %get-tuple-element.34.refs_0_.part, f32[4,4096]{1,0:T(4,128)S(1)} %get-tuple-element.35.refs_1_.updated, f32[6,128,512]{2,1,0:T(8,128)S(1)} %get-tuple-element.24.gas.refs_2_, f32[128,512]{1,0:T(8,128)S(1)} %bitcast.6, ...), custom_call_target="tpu_custom_call" | custom-call | flops 4000000000 | bytes 3000000 | tf_op jit(solution)/shard_map/soon/pallas_call | solution.py:431
  36.0 0.0 collective-permute-done.late
  36.0 0.1 last.1
  (1 shorter events, 0.0 us)
Async XLA Ops:
  0.6 11.0 %copy-start = (f32[8,16,512]{2,1,0:T(8,128)S(1)}, f32[8,16,512]{2,1,0:T(8,128)}, u32[]{:S(2)}) copy-start(f32[8,16,512]{2,1,0:T(8,128)} %param.7) | copy-start | bytes 786436
  2.4 22.9 %collective-permute-start.4 = (f32[104,512]{1,0:T(8,128)S(1)}, f32[104,512]{1,0:T(8,128)S(1)}, u32[]{:S(2)}, u32[]{:S(2)}) collective-permute-start(f32[104,512]{1,0:T(8,128)S(1)} %get-tuple-element.38), channel_id=1, source_target_pairs={{1,2},{2,1},{5,6},{6,5},{9,10},{10,9},{13,14},{14,13},{17,18},{18,... | collective-permute-start | bytes 638984 | tf_op jit(solution)/shard_map/ppermute | solution.py:389
  4.5 20.7 %collective-permute-start.3 = (f32[104,512]{1,0:T(8,128)S(1)}, f32[104,512]{1,0:T(8,128)S(1)}, u32[]{:S(2)}, u32[]{:S(2)}) collective-permute-start(f32[104,512]{1,0:T(8,128)S(1)} %get-tuple-element.29.radial_a), channel_id=1, source_target_pairs={{0,1},{2,3},{3,2},{4,5},{5,4},{6,7},{7,6},{8,9},{9,8},{10,11},{11,... | collective-permute-start | bytes 638984 | tf_op jit(solution)/shard_map/ppermute | solution.py:390
  6.5 18.8 %collective-permute-start.1 = (f32[200,512]{1,0:T(8,128)S(1)}, f32[200,512]{1,0:T(8,128)S(1)}, u32[]{:S(2)}, u32[]{:S(2)}) collective-permute-start(f32[200,512]{1,0:T(8,128)S(1)} %get-tuple-element.37), channel_id=1, source_target_pairs={{0,4},{4,0},{1,5},{5,1},{2,6},{6,2},{3,7},{7,3},{8,12},{12,8},{9,1... | collective-permute-start | bytes 1228808 | tf_op jit(solution)/shard_map/ppermute | solution.py:388
  10.3 22.7 %collective-permute-start.2 = (f32[200,512]{1,0:T(8,128)S(1)}, f32[200,512]{1,0:T(8,128)S(1)}, u32[]{:S(2)}, u32[]{:S(2)}) collective-permute-start(f32[200,512]{1,0:T(8,128)S(1)} %get-tuple-element.28.axial_b), channel_id=1, source_target_pairs={{4,8},{8,4},{5,9},{9,5},{6,10},{10,6},{7,11},{11,7},{12,16},{16,12... | collective-permute-start | bytes 1228808 | tf_op jit(solution)/shard_map/ppermute | solution.py:387
  18.3 17.7 %collective-permute-start = (f32[200,512]{1,0:T(8,128)S(1)}, f32[200,512]{1,0:T(8,128)S(1)}, u32[]{:S(2)}, u32[]{:S(2)}) collective-permute-start(f32[200,512]{1,0:T(8,128)S(1)} %get-tuple-element.30), channel_id=1, source_target_pairs={{1,0},{64,60},{65,61},{66,62},{67,63},{128,124},{129,125},{130,126... | collective-permute-start | bytes 1228808 | tf_op jit(solution)/shard_map/ppermute | solution.py:409

commit v5 on v4

--- a/solution.py
+++ b/solution.py
@@ -38,13 +38,13 @@
 
 
 def is_early():
-    a, r = lax.axis_index("ax"), lax.axis_index("rad")
-    return ((a > 0) & (lax.rem(a, WRAP) == 0)) | ((a == 0) & (r == 1))
+    a = lax.axis_index("ax")
+    return (a > 0) & (lax.rem(a, WRAP) == 0)
 
 
 def prep_kernel(
     gas_in, drops_in, cells_in, lists_in, counts_in,
-    axial_b, axial_a, radial_b, radial_a, kept, gas, drops, cells, lists, counts, sems,
+    axial_b, axial_a, picks, kept, gas, drops, cells, lists, counts, sems,
 ):
     small = [
         pltpu.make_async_copy(source, target, sems.at[n])
@@ -82,28 +82,35 @@
     chosen = jnp.concatenate(chosen + [jnp.zeros((3, 4 * CAP), f32)], axis=0)
     gone = lax.dot_general(high.astype(bf16), low, (((1,), (1,)), ((), ())), preferred_element_type=f32)
     kept[...] = fields[0] * (1.0 - gone)
-    by_way = [chosen[:, CAP * d : CAP * d + CAP] for d in range(4)]
-    odd_ax, odd_rad = parity("ax"), parity("rad")
-    for axis, odd, (even_way, odd_way) in (("ax", odd_ax, (axial_a, axial_b)), ("rad", odd_rad, (radial_a, radial_b))):
-        plus, minus = by_way[0:2] if axis == "ax" else by_way[2:4]
-        base = 192 if axis == "ax" else 96
-        even_way[base : base + 8, 0:CAP] = jnp.where(odd == 0, plus, minus)
-        odd_way[base : base + 8, 0:CAP] = jnp.where(odd == 0, minus, plus)
+    picks[...] = chosen
     for copy in large:
         copy.wait()
-    for message, last in ((axial_a, odd_ax == 0), (axial_b, odd_ax == 1)):
-        near = pl.multiple_of(jnp.where(last, (CX - 1) * CY, 0), CY)
-        far = pl.multiple_of(jnp.where(last, (CX - 2) * CY, CY), CY)
-        for c in range(C):
-            message[32 * c : 32 * c + 16, :] = gas[c, pl.ds(near, CY), :]
-            message[32 * c + 16 : 32 * c + 32, :] = gas[c, pl.ds(far, CY), :]
-    for message, last in ((radial_a, odd_rad == 0), (radial_b, odd_rad == 1)):
-        near, far = jnp.where(last, CY - 1, 0), jnp.where(last, CY - 2, 1)
-        for c in range(C):
-            for i in range(CX):
-                at = c * CX + i
-                message[at : at + 1, :] = gas[c, pl.ds(i * CY + near, 1), :]
-                message[48 + at : 49 + at, :] = gas[c, pl.ds(i * CY + far, 1), :]
+    pack_axial(gas, picks, axial_b, parity("ax") == 1)
+    pack_axial(gas, picks, axial_a, parity("ax") == 0)
+
+
+def pick_way(picks, axis, last):
+    first = 0 if axis == "ax" else 2 * CAP
+    return jnp.where(last, picks[:, first : first + CAP], picks[:, first + CAP : first + 2 * CAP])
+
+
+def pack_axial(gas, picks, message, last):
+    near = pl.multiple_of(jnp.where(last, (CX - 1) * CY, 0), CY)
+    far = pl.multiple_of(jnp.where(last, (CX - 2) * CY, CY), CY)
+    for c in range(C):
+        message[32 * c : 32 * c + 16, :] = gas[c, pl.ds(near, CY), :]
+        message[32 * c + 16 : 32 * c + 32, :] = gas[c, pl.ds(far, CY), :]
+    message[192:200, 0:CAP] = pick_way(picks, "ax", last)
+
+
+def pack_radial(gas, picks, message, last):
+    near, far = jnp.where(last, CY - 1, 0), jnp.where(last, CY - 2, 1)
+    for c in range(C):
+        for i in range(CX):
+            at = c * CX + i
+            message[at : at + 1, :] = gas[c, pl.ds(i * CY + near, 1), :]
+            message[48 + at : 49 + at, :] = gas[c, pl.ds(i * CY + far, 1), :]
+    message[96:104, 0:CAP] = pick_way(picks, "rad", last)
 
 
 def evaporate(mass, temp, axial, radial, samples):
@@ -162,15 +169,13 @@
     return lax.dot_general(spread, twice, (((1,), (1,)), ((), ())), preferred_element_type=f32)
 
 
-def early_kernel(gas, viscosity, drops, cells, kept, axial_b, radial_a, late, *refs):
+def early_kernel(gas, viscosity, drops, cells, kept, picks, axial_b, late, radial_a, radial_b, *refs):
+    pack_radial(gas, picks, radial_a, parity("rad") == 0)
+    pack_radial(gas, picks, radial_b, parity("rad") == 1)
+
     @pl.when(is_early())
     def _():
         late[...] = axial_b[...]
-
-        @pl.when(lax.axis_index("ax") == 0)
-        def _():
-            late[0:104, :] = radial_a[0:104, :]
-
         main_kernel(gas, viscosity, drops, cells, kept, *refs)
 
 
@@ -191,14 +196,14 @@
 
     slot = lax.broadcasted_iota(jnp.int32, (1, SLOTS), 1)
     filled = jnp.max(jnp.where(drops[0:1, :] > 0.0, slot + 1, 0))
-    blocks = lax.div(filled + 511, 512)
+    blocks = lax.div(filled + 1023, 1024)
 
     def sample(b, carry):
-        first = pl.multiple_of(4 * b, 4)
-        where = jnp.concatenate([cells[pl.ds(first + s, 1), :] for s in range(4)], axis=1)
+        first = pl.multiple_of(8 * b, 8)
+        where = jnp.concatenate([cells[pl.ds(first + s, 1), :] for s in range(8)], axis=1)
         got = gather_block(table, where)
         for k in range(4):
-            for s in range(4):
+            for s in range(8):
                 samples[k, pl.ds(first + s, 1), :] = got[k][:, 128 * s : 128 * s + 128]
         return carry
 
@@ -214,8 +219,8 @@
     source[...] = jnp.zeros_like(source)
 
     def deposit(b, carry):
-        first = pl.multiple_of(4 * b, 4)
-        row = lambda load: jnp.concatenate([load(pl.ds(first + s, 1)) for s in range(4)], axis=1)
+        first = pl.multiple_of(8 * b, 8)
+        row = lambda load: jnp.concatenate([load(pl.ds(first + s, 1)) for s in range(8)], axis=1)
         where = row(lambda at: cells[at, :])
         source[...] += deposit_block([row(lambda at: terms[k, at, :]) for k in range(4)], where)
         return carry
@@ -253,8 +258,8 @@
 
 
 def is_last():
-    a, r = lax.axis_index("ax"), lax.axis_index("rad")
-    return ((lax.rem(a, WRAP) == WRAP - 1) & (a < lax.axis_size("ax") - 1)) | ((a == 0) & (r == 0))
+    a = lax.axis_index("ax")
+    return (lax.rem(a, WRAP) == WRAP - 1) & (a < lax.axis_size("ax") - 1)
 
 
 def soon_kernel(*refs):
@@ -267,8 +272,8 @@
 
 
 def final_kernel(
-    late, part, updated_in, gas, viscosity, table, axial_a, axial_b_in, radial_a_in, radial_b,
-    out_hbm, drops_hbm, arrivals_hbm, out, arrivals, axial_b, radial_a, weights, sems,
+    late, part, updated_in, gas, viscosity, table, axial_a, axial_b_in, radial_a, radial_b,
+    out_hbm, drops_hbm, arrivals_hbm, out, arrivals, weights, sems,
 ):
     copies = [
         pltpu.make_async_copy(updated_in, drops_hbm, sems.at[0]),
@@ -277,11 +282,9 @@
     copies[0].start()
     odd_ax, odd_rad = parity("ax"), parity("rad")
     if late is None:
-        axial_b, radial_a = axial_b_in, radial_a_in
+        axial_b = axial_b_in
     else:
-        corner = lax.axis_index("ax") == 0
-        axial_b[...] = jnp.where(corner, axial_b_in[...], late[...])
-        radial_a[0:104, :] = jnp.where(corner, late[0:104, :], radial_a_in[0:104, :])
+        axial_b = late
     got = []
     for odd, a, b, base in ((odd_ax, axial_a, axial_b, 192), (odd_rad, radial_a, radial_b, 96)):
         in_a, in_b = a[base : base + 8, 0:CAP], b[base : base + 8, 0:CAP]
@@ -350,7 +353,7 @@
             if r + 1 < n_rad:
                 out = (flat(a, r), flat(a, r + 1))
                 (radial_a if r % 2 == 0 else radial_b).append(out)
-                back = late if a == 0 and r == 0 else radial_a if r % 2 == 0 else radial_b
+                back = radial_a if r % 2 == 0 else radial_b
                 back.append(out[::-1])
     return axial_a, axial_b, radial_a, radial_b, late
 
@@ -360,20 +363,19 @@
     thick = viscosity.reshape(ROWS, CZ)
     cells = drop_cells.reshape(32, 128)
     shape = jax.ShapeDtypeStruct
-    axial_b, axial_a, radial_b, radial_a, kept, gas, drops, cells = pl.pallas_call(
+    axial_b, axial_a, picks, kept, gas, drops, cells = pl.pallas_call(
         prep_kernel,
         out_shape=(
             shape((200, CZ), f32),
             shape((200, CZ), f32),
-            shape((104, CZ), f32),
-            shape((104, CZ), f32),
+            shape((8, 4 * CAP), f32),
             shape((32, 128), f32),
             shape((C, ROWS, CZ), f32),
             shape((4, SLOTS), f32),
             shape((32, 128), jnp.int32),
         ),
         in_specs=[HB] * 5,
-        out_specs=(VM,) * 8,
+        out_specs=(VM,) * 7,
         scratch_shapes=[
             pltpu.VMEM((1, 4, CAP), jnp.int32),
             pltpu.SMEM((1, 4), jnp.int32),
@@ -386,9 +388,6 @@
     to_a, to_b, to_c, to_d, to_late = routes(lax.axis_size("ax"), lax.axis_size("rad"))
     came_b = lax.ppermute(axial_b, both, to_b)
     came_a = lax.ppermute(axial_a, both, to_a)
-    came_d = lax.ppermute(radial_b, both, to_d)
-    came_c = lax.ppermute(radial_a, both, to_c)
-
     results = (shape((C, ROWS, CZ), f32), shape((4, SLOTS), f32), shape((8 * ROWS, CZ), bf16))
     scratch = [
         pltpu.VMEM((3, ROWS, CZ), f32),
@@ -396,17 +395,19 @@
         pltpu.VMEM((4, 32, 128), f32),
         pltpu.VMEM((4 * ROWS, CZ), f32),
     ]
-    late, *first = pl.pallas_call(
+    late, radial_a, radial_b, *first = pl.pallas_call(
         early_kernel,
-        out_shape=(shape((200, CZ), f32), *results),
+        out_shape=(shape((200, CZ), f32), shape((104, CZ), f32), shape((104, CZ), f32), *results),
         in_specs=[VM] * 7,
-        out_specs=(VM,) * 4,
+        out_specs=(VM,) * 6,
         scratch_shapes=scratch,
         compiler_params=params,
         cost_estimate=pl.CostEstimate(flops=40000000000, bytes_accessed=6_000_000, transcendentals=0),
         name="early",
-    )(gas, thick, drops, cells, kept, axial_b, radial_a)
+    )(gas, thick, drops, cells, kept, picks, axial_b)
     came_late = lax.ppermute(late, both, to_late)
+    came_d = lax.ppermute(radial_b, both, to_d)
+    came_c = lax.ppermute(radial_a, both, to_c)
     part, updated, table = pl.pallas_call(
         late_kernel,
         out_shape=results,
@@ -422,8 +423,6 @@
     scratch = [
         pltpu.VMEM((C, ROWS, CZ), f32),
         pltpu.VMEM((4, 4 * CAP), f32),
-        pltpu.VMEM((200, CZ), f32),
-        pltpu.VMEM((104, CZ), f32),
         pltpu.VMEM((4, ROWS, CZ), f32),
         pltpu.SemaphoreType.DMA((8,)),
     ]
@@ -435,7 +434,7 @@
         out_specs=(HB,) * 3,
         scratch_shapes=scratch,
         compiler_params=params,
-        cost_estimate=pl.CostEstimate(flops=4_000_000_000, bytes_accessed=3_000_000, transcendentals=0),
+        cost_estimate=pl.CostEstimate(flops=0, bytes_accessed=0, transcendentals=0),
         name="soon",
     )(*common)
     out, drops_out, arrivals_out = pl.pallas_call(

time: 36.6 us -> 35.2 us (0.962)
  the two profiles are of different devices: /device:TPU:6 before, /device:TPU:97 now
where the time goes in v5:
time: 35.2 us; the launch traced here: 35 us
  Pallas kernels  19.1 us (54%)
  starting transfers between devices  15.1 us (43%)
  between operations  0.76 us (2%)
    pallas_call x1, Pallas kernels, body(): pl.pallas_call(late_kernel, out_shape=results, in_specs=[VM] * 8, out_spe...  14.2 us
    ppermute x1, starting transfers between devices, body(): came_b = lax.ppermute(axial_b, both, to_b)  6.38 us
    ppermute x1, starting transfers between devices, body(): came_c = lax.ppermute(radial_a, both, to_c)  3.14 us
    ppermute x1, starting transfers between devices, body(): came_d = lax.ppermute(radial_b, both, to_d)  3.02 us
    pallas_call x1, Pallas kernels, body(): pl.pallas_call(soon_kernel, out_shape=finals, in_specs=[VM] * 9, out_spec...  2.99 us
    ppermute x1, starting transfers between devices, body(): came_a = lax.ppermute(axial_a, both, to_a)  1.92 us
    pallas_call x1, Pallas kernels, body(): pl.pallas_call(prep_kernel, out_shape=(shape((200, CZ), f32), shape((200,...  1.62 us
  transfers between devices with their start and end apart: 5, of which 0 were waited for; matrix products, arithmetic and copies ran while one was open for 0% of the time, Pallas kernels for 50%

profile of v5, /device:TPU:97, one launch (start us, length us, event | category | flops | bytes accessed | tf_op | source)
XLA Modules:
  0.0 35.0 jit_solution(14146521569859063133)
XLA Ops:
  0.6 0.0 copy-start
  0.6 1.6 %prep.1 = (f32[200,512]{1,0:T(8,128)S(1)}, f32[200,512]{1,0:T(8,128)S(1)}, f32[8,256]{1,0:T(8,128)S(1)}, f32[32,128]{1,0:T(8,128)S(1)}, f32[6,128,512]{2,1,0:T(8...) custom-call(f32[6,128,512]{2,1,0:T(8,128)} %bitcast.9, f32[4,4096]{1,0:T(4,128)} %drops_in.1, ...), custom_call_target="tpu_custom_call" | custom-call | tf_op jit(solution)/shard_map/prep/pallas_call | solution.py:366
  2.3 1.9 %collective-permute-start.1 = (f32[200,512]{1,0:T(8,128)S(1)}, f32[200,512]{1,0:T(8,128)S(1)}, u32[]{:S(2)}, u32[]{:S(2)}) collective-permute-start(f32[200,512]{1,0:T(8,128)S(1)} %get-tuple-element.38), channel_id=1, source_target_pairs={{0,4},{4,0},{1,5},{5,1},{2,6},{6,2},{3,7},{7,3},{8,12},{12,8},{9,1... | collective-permute-start | bytes 1228808 | tf_op jit(solution)/shard_map/ppermute | solution.py:390
  4.2 6.4 %collective-permute-start.2 = (f32[200,512]{1,0:T(8,128)S(1)}, f32[200,512]{1,0:T(8,128)S(1)}, u32[]{:S(2)}, u32[]{:S(2)}) collective-permute-start(f32[200,512]{1,0:T(8,128)S(1)} %get-tuple-element.30.axial_b), channel_id=1, source_target_pairs={{4,8},{8,4},{5,9},{9,5},{6,10},{10,6},{7,11},{11,7},{12,16},{16,12... | collective-permute-start | bytes 1228808 | tf_op jit(solution)/shard_map/ppermute | solution.py:389
  10.6 0.0 copy-done
  10.6 0.2 early.1
  10.8 0.7 %collective-permute-start = (f32[200,512]{1,0:T(8,128)S(1)}, f32[200,512]{1,0:T(8,128)S(1)}, u32[]{:S(2)}, u32[]{:S(2)}) collective-permute-start(f32[200,512]{1,0:T(8,128)S(1)} %get-tuple-element.31), channel_id=1, source_target_pairs={{64,60},{65,61},{66,62},{67,63},{128,124},{129,125},{130,126},{131... | collective-permute-start | bytes 1228808 | tf_op jit(solution)/shard_map/ppermute | solution.py:408
  11.4 3.1 %collective-permute-start.3 = (f32[104,512]{1,0:T(8,128)S(1)}, f32[104,512]{1,0:T(8,128)S(1)}, u32[]{:S(2)}, u32[]{:S(2)}) collective-permute-start(f32[104,512]{1,0:T(8,128)S(1)} %get-tuple-element.39), channel_id=1, source_target_pairs={{0,1},{1,0},{2,3},{3,2},{4,5},{5,4},{6,7},{7,6},{8,9},{9,8},{10,11... | collective-permute-start | bytes 638984 | tf_op jit(solution)/shard_map/ppermute | solution.py:410
  14.6 3.0 %collective-permute-start.4 = (f32[104,512]{1,0:T(8,128)S(1)}, f32[104,512]{1,0:T(8,128)S(1)}, u32[]{:S(2)}, u32[]{:S(2)}) collective-permute-start(f32[104,512]{1,0:T(8,128)S(1)} %get-tuple-element.40), channel_id=1, source_target_pairs={{1,2},{2,1},{5,6},{6,5},{9,10},{10,9},{13,14},{14,13},{17,18},{18,... | collective-permute-start | bytes 638984 | tf_op jit(solution)/shard_map/ppermute | solution.py:409
  17.6 14.2 %late.1 = (f32[6,128,512]{2,1,0:T(8,128)S(1)}, f32[4,4096]{1,0:T(4,128)S(1)}, bf16[1024,512]{1,0:T(8,128)(2,1)S(1)}) custom-call(f32[6,128,512]{2,1,0:T(8,128)S(1)} %get-tuple-element.25.gas.refs_2_, f32[128,512]{1,0:T(8,128)S(1)} %bitcast.5, f32[4,4096]{1,0:T(4,128)S(1)} %get-tuple-element.26.drops, ...), custom_call_target="tpu_custom_call", output_to_operand_aliasing={{0}: (5, {}), {1}: (6, {}), {2}: (7, {})} | custom-call | tf_op jit(solution)/shard_map/late/pallas_call | solution.py:411
  31.9 0.0 collective-permute-done.3.refs_7_.radial_a
  31.9 0.0 collective-permute-done.4.refs_8_.radial_b
  31.9 0.0 collective-permute-done.1.refs_5_.axial_a
  31.9 0.0 collective-permute-done.2.refs_6_.axial_b
  31.9 3.0 %soon.1 = (f32[6,128,512]{2,1,0:T(8,128)}, f32[4,4096]{1,0:T(4,128)}, f32[4,256]{1,0:T(4,128)}) custom-call(f32[6,128,512]{2,1,0:T(8,128)S(1)} %get-tuple-element.35.refs_0_.part, f32[4,4096]{1,0:T(4,128)S(1)} %get-tuple-element.36.refs_1_.updated, f32[6,128,512]{2,1,0:T(8,128)S(1)} %get-tuple-element.25.gas.refs_2_, f32[128,512]{1,0:T(8,128)S(1)} %bitcast.6, ...), custom_call_target="tpu_custom_call" | custom-call | tf_op jit(solution)/shard_map/soon/pallas_call | solution.py:430
  34.9 0.0 collective-permute-done.late
  34.9 0.1 last.1
Async XLA Ops:
  0.6 10.0 %copy-start = (f32[8,16,512]{2,1,0:T(8,128)S(1)}, f32[8,16,512]{2,1,0:T(8,128)}, u32[]{:S(2)}) copy-start(f32[8,16,512]{2,1,0:T(8,128)} %param.7) | copy-start | bytes 786436
  2.3 29.6 %collective-permute-start.1 = (f32[200,512]{1,0:T(8,128)S(1)}, f32[200,512]{1,0:T(8,128)S(1)}, u32[]{:S(2)}, u32[]{:S(2)}) collective-permute-start(f32[200,512]{1,0:T(8,128)S(1)} %get-tuple-element.38), channel_id=1, source_target_pairs={{0,4},{4,0},{1,5},{5,1},{2,6},{6,2},{3,7},{7,3},{8,12},{12,8},{9,1... | collective-permute-start | bytes 1228808 | tf_op jit(solution)/shard_map/ppermute | solution.py:390
  4.2 27.7 %collective-permute-start.2 = (f32[200,512]{1,0:T(8,128)S(1)}, f32[200,512]{1,0:T(8,128)S(1)}, u32[]{:S(2)}, u32[]{:S(2)}) collective-permute-start(f32[200,512]{1,0:T(8,128)S(1)} %get-tuple-element.30.axial_b), channel_id=1, source_target_pairs={{4,8},{8,4},{5,9},{9,5},{6,10},{10,6},{7,11},{11,7},{12,16},{16,12... | collective-permute-start | bytes 1228808 | tf_op jit(solution)/shard_map/ppermute | solution.py:389
  10.8 24.1 %collective-permute-start = (f32[200,512]{1,0:T(8,128)S(1)}, f32[200,512]{1,0:T(8,128)S(1)}, u32[]{:S(2)}, u32[]{:S(2)}) collective-permute-start(f32[200,512]{1,0:T(8,128)S(1)} %get-tuple-element.31), channel_id=1, source_target_pairs={{64,60},{65,61},{66,62},{67,63},{128,124},{129,125},{130,126},{131... | collective-permute-start | bytes 1228808 | tf_op jit(solution)/shard_map/ppermute | solution.py:408
  11.4 20.4 %collective-permute-start.3 = (f32[104,512]{1,0:T(8,128)S(1)}, f32[104,512]{1,0:T(8,128)S(1)}, u32[]{:S(2)}, u32[]{:S(2)}) collective-permute-start(f32[104,512]{1,0:T(8,128)S(1)} %get-tuple-element.39), channel_id=1, source_target_pairs={{0,1},{1,0},{2,3},{3,2},{4,5},{5,4},{6,7},{7,6},{8,9},{9,8},{10,11... | collective-permute-start | bytes 638984 | tf_op jit(solution)/shard_map/ppermute | solution.py:410
  14.6 17.3 %collective-permute-start.4 = (f32[104,512]{1,0:T(8,128)S(1)}, f32[104,512]{1,0:T(8,128)S(1)}, u32[]{:S(2)}, u32[]{:S(2)}) collective-permute-start(f32[104,512]{1,0:T(8,128)S(1)} %get-tuple-element.40), channel_id=1, source_target_pairs={{1,2},{2,1},{5,6},{6,5},{9,10},{10,9},{13,14},{14,13},{17,18},{18,... | collective-permute-start | bytes 638984 | tf_op jit(solution)/shard_map/ppermute | solution.py:409

commit v6 on v5

--- a/solution.py
+++ b/solution.py
@@ -44,7 +44,7 @@
 
 def prep_kernel(
     gas_in, drops_in, cells_in, lists_in, counts_in,
-    axial_b, axial_a, picks, kept, gas, drops, cells, lists, counts, sems,
+    axial_a, picks, kept, gas, drops, cells, lists, counts, sems,
 ):
     small = [
         pltpu.make_async_copy(source, target, sems.at[n])
@@ -85,7 +85,6 @@
     picks[...] = chosen
     for copy in large:
         copy.wait()
-    pack_axial(gas, picks, axial_b, parity("ax") == 1)
     pack_axial(gas, picks, axial_a, parity("ax") == 0)
 
 
@@ -169,21 +168,82 @@
     return lax.dot_general(spread, twice, (((1,), (1,)), ((), ())), preferred_element_type=f32)
 
 
-def early_kernel(gas, viscosity, drops, cells, kept, picks, axial_b, late, radial_a, radial_b, *refs):
+def early_kernel(gas, viscosity, drops, cells, kept, picks, late, axial_b, radial_a, radial_b, *refs):
+    pack_axial(gas, picks, axial_b, parity("ax") == 1)
+    pl.when(is_early())(lambda: pack_axial(gas, picks, late, parity("ax") == 1))
     pack_radial(gas, picks, radial_a, parity("rad") == 0)
     pack_radial(gas, picks, radial_b, parity("rad") == 1)
-
-    @pl.when(is_early())
+    pl.when(is_early() | (parity("ax") == 1))(lambda: stencil_part(gas, viscosity, *refs))
+    pl.when(is_early())(lambda: droplet_part(drops, cells, kept, *refs))
+
+
+def late_kernel(gas, viscosity, drops, cells, kept, out_in, drops_in, table_in, *refs):
+    @pl.when(jnp.logical_not(is_early()))
     def _():
-        late[...] = axial_b[...]
-        main_kernel(gas, viscosity, drops, cells, kept, *refs)
-
-
-def late_kernel(gas, viscosity, drops, cells, kept, out_in, drops_in, table_in, *refs):
-    pl.when(jnp.logical_not(is_early()))(lambda: main_kernel(gas, viscosity, drops, cells, kept, *refs))
-
-
-def main_kernel(gas, viscosity, drops, cells, kept, out, drops_out, table, speed, samples, terms, source):
+        pl.when(parity("ax") == 0)(lambda: stencil_part(gas, viscosity, *refs))
+        droplet_part(drops, cells, kept, *refs)
+
+
+def droplet_part(drops, cells, kept, out, drops_out, table, speed, samples, terms, source):
+    slot = lax.broadcasted_iota(jnp.int32, (1, SLOTS), 1)
+    filled = jnp.max(jnp.where(drops[0:1, :] > 0.0, slot + 1, 0))
+    blocks = lax.div(filled + 1023, 1024)
+
+    def join(load, first, rows):
+        return jnp.concatenate([load(pl.ds(first + s, 1)) for s in range(rows)], axis=1)
+
+    def sample(first, rows):
+        got = gather_block(table, join(lambda at: cells[at, :], first, rows))
+        for k in range(4):
+            for s in range(rows):
+                samples[k, pl.ds(first + s, 1), :] = got[k][:, 128 * s : 128 * s + 128]
+
+    def deposit(first, rows):
+        where = join(lambda at: cells[at, :], first, rows)
+        return deposit_block([join(lambda at: terms[k, at, :], first, rows) for k in range(4)], where)
+
+    def sample_loop(b, carry):
+        sample(pl.multiple_of(8 * b, 8), 8)
+        return carry
+
+    def deposit_loop(b, carry):
+        source[...] += deposit(pl.multiple_of(8 * b, 8), 8)
+        return carry
+
+    @pl.when(blocks == 4)
+    def _():
+        for b in range(8):
+            sample(4 * b, 4)
+
+    @pl.when(blocks < 4)
+    def _():
+        lax.fori_loop(0, blocks, sample_loop, 0)
+
+    fields = [
+        jnp.concatenate([drops[f : f + 1, 128 * s : 128 * s + 128] for s in range(32)], axis=0) for f in range(1, 4)
+    ]
+    updated, new_terms = evaporate(kept[...], *fields, [samples[k] for k in range(4)])
+    for f in range(4):
+        terms[f] = new_terms[f]
+        for s in range(32):
+            drops_out[f : f + 1, 128 * s : 128 * s + 128] = updated[f][s : s + 1, :]
+
+    @pl.when(blocks == 4)
+    def _():
+        source[...] = deposit(0, 4)
+        for b in range(1, 8):
+            source[...] += deposit(4 * b, 4)
+
+    @pl.when(blocks < 4)
+    def _():
+        source[...] = jnp.zeros_like(source)
+        lax.fori_loop(0, blocks, deposit_loop, 0)
+
+    for c, slot in ((0, 0), (1, 1), (2, 2), (4, 3), (5, 0)):
+        out[c] += source[slot * ROWS : slot * ROWS + ROWS, :]
+
+
+def stencil_part(gas, viscosity, out, drops_out, table, speed, samples, terms, source):
     inverse = 1.0 / gas[0]
     for k, c in enumerate((1, 2, 4, 5)):
         quotient = gas[c] * inverse
@@ -193,44 +253,9 @@
         table[2 * ROWS * k : 2 * ROWS * k + ROWS, :] = hi
         table[2 * ROWS * k + ROWS : 2 * ROWS * k + 2 * ROWS, :] = lo
     speed[2] = gas[3] * inverse
-
-    slot = lax.broadcasted_iota(jnp.int32, (1, SLOTS), 1)
-    filled = jnp.max(jnp.where(drops[0:1, :] > 0.0, slot + 1, 0))
-    blocks = lax.div(filled + 1023, 1024)
-
-    def sample(b, carry):
-        first = pl.multiple_of(8 * b, 8)
-        where = jnp.concatenate([cells[pl.ds(first + s, 1), :] for s in range(8)], axis=1)
-        got = gather_block(table, where)
-        for k in range(4):
-            for s in range(8):
-                samples[k, pl.ds(first + s, 1), :] = got[k][:, 128 * s : 128 * s + 128]
-        return carry
-
-    lax.fori_loop(0, blocks, sample, 0)
-    fields = [
-        jnp.concatenate([drops[f : f + 1, 128 * s : 128 * s + 128] for s in range(32)], axis=0) for f in range(1, 4)
-    ]
-    updated, new_terms = evaporate(kept[...], *fields, [samples[k] for k in range(4)])
-    for f in range(4):
-        terms[f] = new_terms[f]
-        for s in range(32):
-            drops_out[f : f + 1, 128 * s : 128 * s + 128] = updated[f][s : s + 1, :]
-    source[...] = jnp.zeros_like(source)
-
-    def deposit(b, carry):
-        first = pl.multiple_of(8 * b, 8)
-        row = lambda load: jnp.concatenate([load(pl.ds(first + s, 1)) for s in range(8)], axis=1)
-        where = row(lambda at: cells[at, :])
-        source[...] += deposit_block([row(lambda at: terms[k, at, :]) for k in range(4)], where)
-        return carry
-
-    lax.fori_loop(0, blocks, deposit, 0)
     lane = lax.broadcasted_iota(jnp.int32, (CY, CZ), 0)
 
     def component(c, carry):
-        slot = jnp.where(c < 3, c, jnp.where(c == 5, 0, c - 1))
-        scale = jnp.where(c == 3, 0.0, 1.0)
         layers = [gas[c, CY * i : CY * i + CY, :] for i in range(CX)]
         for i in range(CX):
             rows = slice(CY * i, CY * i + CY)
@@ -250,8 +275,7 @@
             for j, n in enumerate((ax, ra, az)):
                 slope = (8.0 * (n[2] - n[1]) - (n[3] - n[0])) * (1.0 / 12.0)
                 transport = transport + speed[j, rows, :] * slope
-            advanced = x + time_step * (viscosity[rows, :] * laplace - transport)
-            out[c, rows, :] = advanced + scale * source[pl.ds(pl.multiple_of(slot * ROWS + CY * i, CY), CY), :]
+            out[c, rows, :] = x + time_step * (viscosity[rows, :] * laplace - transport)
         return carry
 
     lax.fori_loop(0, C, component, 0)
@@ -363,11 +387,10 @@
     thick = viscosity.reshape(ROWS, CZ)
     cells = drop_cells.reshape(32, 128)
     shape = jax.ShapeDtypeStruct
-    axial_b, axial_a, picks, kept, gas, drops, cells = pl.pallas_call(
+    axial_a, picks, kept, gas, drops, cells = pl.pallas_call(
         prep_kernel,
         out_shape=(
-            shape((200, CZ), f32),
-            shape((200, CZ), f32),
+            shape((208, CZ), f32),
             shape((8, 4 * CAP), f32),
             shape((32, 128), f32),
             shape((C, ROWS, CZ), f32),
@@ -375,7 +398,7 @@
             shape((32, 128), jnp.int32),
         ),
         in_specs=[HB] * 5,
-        out_specs=(VM,) * 7,
+        out_specs=(VM,) * 6,
         scratch_shapes=[
             pltpu.VMEM((1, 4, CAP), jnp.int32),
             pltpu.SMEM((1, 4), jnp.int32),
@@ -386,7 +409,6 @@
     )(*(pltpu.with_memory_space_constraint(x, pltpu.HBM) for x in (gas, droplets, cells, move_lists, move_counts)))
     both = ("ax", "rad")
     to_a, to_b, to_c, to_d, to_late = routes(lax.axis_size("ax"), lax.axis_size("rad"))
-    came_b = lax.ppermute(axial_b, both, to_b)
     came_a = lax.ppermute(axial_a, both, to_a)
     results = (shape((C, ROWS, CZ), f32), shape((4, SLOTS), f32), shape((8 * ROWS, CZ), bf16))
     scratch = [
@@ -395,17 +417,18 @@
         pltpu.VMEM((4, 32, 128), f32),
         pltpu.VMEM((4 * ROWS, CZ), f32),
     ]
-    late, radial_a, radial_b, *first = pl.pallas_call(
+    late, axial_b, radial_a, radial_b, *first = pl.pallas_call(
         early_kernel,
-        out_shape=(shape((200, CZ), f32), shape((104, CZ), f32), shape((104, CZ), f32), *results),
-        in_specs=[VM] * 7,
-        out_specs=(VM,) * 6,
+        out_shape=(shape((208, CZ), f32), shape((200, CZ), f32), shape((104, CZ), f32), shape((104, CZ), f32), *results),
+        in_specs=[VM] * 6,
+        out_specs=(VM,) * 7,
         scratch_shapes=scratch,
         compiler_params=params,
         cost_estimate=pl.CostEstimate(flops=40000000000, bytes_accessed=6_000_000, transcendentals=0),
         name="early",
-    )(gas, thick, drops, cells, kept, picks, axial_b)
+    )(gas, thick, drops, cells, kept, picks)
     came_late = lax.ppermute(late, both, to_late)
+    came_b = lax.ppermute(axial_b, both, to_b)
     came_d = lax.ppermute(radial_b, both, to_d)
     came_c = lax.ppermute(radial_a, both, to_c)
     part, updated, table = pl.pallas_call(

time: 35.2 us -> 45.2 us (1.28)
  the two profiles are of different devices: /device:TPU:97 before, /device:TPU:6 now
where the time goes in v6:
time: 45.2 us; the launch traced here: 45 us
  starting transfers between devices  19.5 us (43%)
  waiting for transfers between devices  12.9 us (29%)
  Pallas kernels  11.6 us (26%)
  between operations  0.92 us (2%)
    ppermute x1, starting transfers between devices, body(): came_late = lax.ppermute(late, both, to_late)  10.6 us
    ppermute x1, waiting for transfers between devices, body(): came_b = lax.ppermute(axial_b, both, to_b)  7.98 us
    pallas_call x1, Pallas kernels, body(): pl.pallas_call(early_kernel, out_shape=(shape((208, CZ), f32), shape((200...  6.61 us
    ppermute x1, waiting for transfers between devices, body(): came_d = lax.ppermute(radial_b, both, to_d)  4.96 us
    ppermute x1, starting transfers between devices, body(): came_a = lax.ppermute(axial_a, both, to_a)  3.83 us
    pallas_call x1, Pallas kernels, body(): pl.pallas_call(soon_kernel, out_shape=finals, in_specs=[VM] * 9, out_spec...  3.01 us
    ppermute x1, starting transfers between devices, body(): came_d = lax.ppermute(radial_b, both, to_d)  1.94 us
    ppermute x1, starting transfers between devices, body(): came_c = lax.ppermute(radial_a, both, to_c)  1.92 us
  transfers between devices with their start and end apart: 5, of which 2 were waited for; matrix products, arithmetic and copies ran while one was open for 0% of the time, Pallas kernels for 22%

profile of v6, /device:TPU:6, one launch (start us, length us, event | category | flops | bytes accessed | tf_op | source)
XLA Modules:
  0.0 45.0 jit_solution(10791630084202073335)
XLA Ops:
  0.6 0.0 copy-start
  0.6 1.6 %prep.1 = (f32[208,512]{1,0:T(8,128)S(1)}, f32[8,256]{1,0:T(8,128)S(1)}, f32[32,128]{1,0:T(8,128)S(1)}, f32[6,128,512]{2,1,0:T(8,128)S(1)}, f32[4,4096]{1,0:T(4,128)S(1)}, /*index=5*/s32[32,128]{1,0:T(8,128)S(1)}) custom-call(f32[6,128,512]{2,1,0:T(8,128)} %bitcast.9, f32[4,4096]{1,0:T(4,128)} %drops_in.1, s32[32,128]{1,0:T(8,128)} %bitcast.10, ...), custom_call_target="tpu_custom_call" | custom-call | tf_op jit(solution)/shard_map/prep/pallas_call | solution.py:390
  2.3 3.8 %collective-permute-start.1 = (f32[208,512]{1,0:T(8,128)S(1)}, f32[208,512]{1,0:T(8,128)S(1)}, u32[]{:S(2)}, u32[]{:S(2)}) collective-permute-start(f32[208,512]{1,0:T(8,128)S(1)} %get-tuple-element.37), channel_id=1, source_target_pairs={{0,4},{4,0},{1,5},{5,1},{2,6},{6,2},{3,7},{7,3},{8,12},{12,8},{9,1... | collective-permute-start | bytes 1277960 | tf_op jit(solution)/shard_map/ppermute | solution.py:412
  6.1 0.0 copy-done
  6.1 6.6 %early.1 = (f32[208,512]{1,0:T(8,128)S(1)}, f32[200,512]{1,0:T(8,128)S(1)}, f32[104,512]{1,0:T(8,128)S(1)}, f32[104,512]{1,0:T(8,128)S(1)}, f32[6,128,512]{2,1,0...) custom-call(f32[6,128,512]{2,1,0:T(8,128)S(1)} %get-tuple-element.25.gas.refs_2_, ...), custom_call_target="tpu_custom_call" | custom-call | flops 40000000000 | bytes 6000000 | tf_op jit(solution)/shard_map/early/pallas_call | solution.py:420
  12.7 10.6 %collective-permute-start = (f32[208,512]{1,0:T(8,128)S(1)}, f32[208,512]{1,0:T(8,128)S(1)}, u32[]{:S(2)}, u32[]{:S(2)}) collective-permute-start(f32[208,512]{1,0:T(8,128)S(1)} %get-tuple-element.30), channel_id=1, source_target_pairs={{64,60},{65,61},{66,62},{67,63},{128,124},{129,125},{130,126},{131... | collective-permute-start | bytes 1277960 | tf_op jit(solution)/shard_map/ppermute | solution.py:430
  23.3 1.3 %collective-permute-start.2 = (f32[200,512]{1,0:T(8,128)S(1)}, f32[200,512]{1,0:T(8,128)S(1)}, u32[]{:S(2)}, u32[]{:S(2)}) collective-permute-start(f32[200,512]{1,0:T(8,128)S(1)} %get-tuple-element.38), channel_id=1, source_target_pairs={{4,8},{8,4},{5,9},{9,5},{6,10},{10,6},{7,11},{11,7},{12,16},{16,12... | collective-permute-start | bytes 1228808 | tf_op jit(solution)/shard_map/ppermute | solution.py:431
  24.6 1.9 %collective-permute-start.3 = (f32[104,512]{1,0:T(8,128)S(1)}, f32[104,512]{1,0:T(8,128)S(1)}, u32[]{:S(2)}, u32[]{:S(2)}) collective-permute-start(f32[104,512]{1,0:T(8,128)S(1)} %get-tuple-element.39), channel_id=1, source_target_pairs={{0,1},{1,0},{2,3},{3,2},{4,5},{5,4},{6,7},{7,6},{8,9},{9,8},{10,11... | collective-permute-start | bytes 638984 | tf_op jit(solution)/shard_map/ppermute | solution.py:433
  26.5 1.9 %collective-permute-start.4 = (f32[104,512]{1,0:T(8,128)S(1)}, f32[104,512]{1,0:T(8,128)S(1)}, u32[]{:S(2)}, u32[]{:S(2)}) collective-permute-start(f32[104,512]{1,0:T(8,128)S(1)} %get-tuple-element.40), channel_id=1, source_target_pairs={{1,2},{2,1},{5,6},{6,5},{9,10},{10,9},{13,14},{14,13},{17,18},{18,... | collective-permute-start | bytes 638984 | tf_op jit(solution)/shard_map/ppermute | solution.py:432
  28.5 0.2 late.1
  28.7 0.0 collective-permute-done.3.refs_7_.radial_a
  28.7 5.0 %collective-permute-done.4.refs_8_.radial_b = f32[104,512]{1,0:T(8,128)S(1)} collective-permute-done((f32[104,512]{1,0:T(8,128)S(1)}, f32[104,512]{1,0:T(8,128)S(1)}, u32[]{:S(2)}, u32[]{:S(2)}) %collective-permute-start.4) | collective-permute-done | bytes 213024 | tf_op jit(solution)/shard_map/ppermute | solution.py:432
  33.7 8.0 %collective-permute-done.2.refs_6_.axial_b = f32[200,512]{1,0:T(8,128)S(1)} collective-permute-done((f32[200,512]{1,0:T(8,128)S(1)}, f32[200,512]{1,0:T(8,128)S(1)}, u32[]{:S(2)}, u32[]{:S(2)}) %collective-permute-start.2) | collective-permute-done | bytes 409632 | tf_op jit(solution)/shard_map/ppermute | solution.py:431
  41.7 0.0 collective-permute-done.1.refs_5_.axial_a
  41.7 3.0 %soon.1 = (f32[6,128,512]{2,1,0:T(8,128)}, f32[4,4096]{1,0:T(4,128)}, f32[4,256]{1,0:T(4,128)}) custom-call(f32[6,128,512]{2,1,0:T(8,128)S(1)} %get-tuple-element.34.refs_0_.part, f32[4,4096]{1,0:T(4,128)S(1)} %get-tuple-element.35.refs_1_.updated, f32[6,128,512]{2,1,0:T(8,128)S(1)} %get-tuple-element.25.gas.refs_2_, f32[128,512]{1,0:T(8,128)S(1)} %bitcast.6, ...), custom_call_target="tpu_custom_call" | custom-call | tf_op jit(solution)/shard_map/soon/pallas_call | solution.py:453
  44.7 0.0 collective-permute-done.late
  44.7 0.1 last.1
Async XLA Ops:
  0.6 5.5 %copy-start = (f32[8,16,512]{2,1,0:T(8,128)S(1)}, f32[8,16,512]{2,1,0:T(8,128)}, u32[]{:S(2)}) copy-start(f32[8,16,512]{2,1,0:T(8,128)} %param.7) | copy-start | bytes 786436
  2.3 39.4 %collective-permute-start.1 = (f32[208,512]{1,0:T(8,128)S(1)}, f32[208,512]{1,0:T(8,128)S(1)}, u32[]{:S(2)}, u32[]{:S(2)}) collective-permute-start(f32[208,512]{1,0:T(8,128)S(1)} %get-tuple-element.37), channel_id=1, source_target_pairs={{0,4},{4,0},{1,5},{5,1},{2,6},{6,2},{3,7},{7,3},{8,12},{12,8},{9,1... | collective-permute-start | bytes 1277960 | tf_op jit(solution)/shard_map/ppermute | solution.py:412
  12.7 32.0 %collective-permute-start = (f32[208,512]{1,0:T(8,128)S(1)}, f32[208,512]{1,0:T(8,128)S(1)}, u32[]{:S(2)}, u32[]{:S(2)}) collective-permute-start(f32[208,512]{1,0:T(8,128)S(1)} %get-tuple-element.30), channel_id=1, source_target_pairs={{64,60},{65,61},{66,62},{67,63},{128,124},{129,125},{130,126},{131... | collective-permute-start | bytes 1277960 | tf_op jit(solution)/shard_map/ppermute | solution.py:430
  23.3 18.4 %collective-permute-start.2 = (f32[200,512]{1,0:T(8,128)S(1)}, f32[200,512]{1,0:T(8,128)S(1)}, u32[]{:S(2)}, u32[]{:S(2)}) collective-permute-start(f32[200,512]{1,0:T(8,128)S(1)} %get-tuple-element.38), channel_id=1, source_target_pairs={{4,8},{8,4},{5,9},{9,5},{6,10},{10,6},{7,11},{11,7},{12,16},{16,12... | collective-permute-start | bytes 1228808 | tf_op jit(solution)/shard_map/ppermute | solution.py:431
  24.6 4.1 %collective-permute-start.3 = (f32[104,512]{1,0:T(8,128)S(1)}, f32[104,512]{1,0:T(8,128)S(1)}, u32[]{:S(2)}, u32[]{:S(2)}) collective-permute-start(f32[104,512]{1,0:T(8,128)S(1)} %get-tuple-element.39), channel_id=1, source_target_pairs={{0,1},{1,0},{2,3},{3,2},{4,5},{5,4},{6,7},{7,6},{8,9},{9,8},{10,11... | collective-permute-start | bytes 638984 | tf_op jit(solution)/shard_map/ppermute | solution.py:433
  26.5 7.2 %collective-permute-start.4 = (f32[104,512]{1,0:T(8,128)S(1)}, f32[104,512]{1,0:T(8,128)S(1)}, u32[]{:S(2)}, u32[]{:S(2)}) collective-permute-start(f32[104,512]{1,0:T(8,128)S(1)} %get-tuple-element.40), channel_id=1, source_target_pairs={{1,2},{2,1},{5,6},{6,5},{9,10},{10,9},{13,14},{14,13},{17,18},{18,... | collective-permute-start | bytes 638984 | tf_op jit(solution)/shard_map/ppermute | solution.py:432

commit v7 on v6

--- a/solution.py
+++ b/solution.py
@@ -168,23 +168,31 @@
     return lax.dot_general(spread, twice, (((1,), (1,)), ((), ())), preferred_element_type=f32)
 
 
-def early_kernel(gas, viscosity, drops, cells, kept, picks, late, axial_b, radial_a, radial_b, *refs):
+def stencil_soon():
+    a = lax.axis_index("ax")
+    return is_early() | ((lax.rem(a, 2) == 1) & (lax.rem(a, WRAP) != WRAP - 1))
+
+
+def first_kernel(gas, viscosity, picks, axial_b, radial_a, radial_b, out, table, speed):
     pack_axial(gas, picks, axial_b, parity("ax") == 1)
-    pl.when(is_early())(lambda: pack_axial(gas, picks, late, parity("ax") == 1))
     pack_radial(gas, picks, radial_a, parity("rad") == 0)
     pack_radial(gas, picks, radial_b, parity("rad") == 1)
-    pl.when(is_early() | (parity("ax") == 1))(lambda: stencil_part(gas, viscosity, *refs))
-    pl.when(is_early())(lambda: droplet_part(drops, cells, kept, *refs))
-
-
-def late_kernel(gas, viscosity, drops, cells, kept, out_in, drops_in, table_in, *refs):
-    @pl.when(jnp.logical_not(is_early()))
+    pl.when(stencil_soon())(lambda: stencil_part(gas, viscosity, out, table, speed))
+
+
+def early_kernel(gas, picks, drops, cells, kept, out_in, table, late, out, drops_out, *scratch):
+    @pl.when(is_early())
     def _():
-        pl.when(parity("ax") == 0)(lambda: stencil_part(gas, viscosity, *refs))
-        droplet_part(drops, cells, kept, *refs)
-
-
-def droplet_part(drops, cells, kept, out, drops_out, table, speed, samples, terms, source):
+        pack_axial(gas, picks, late, parity("ax") == 1)
+        droplet_part(drops, cells, kept, table, out, drops_out, *scratch)
+
+
+def late_kernel(gas, viscosity, drops, cells, kept, out_in, drops_in, table_in, out, drops_out, table, speed, *scratch):
+    pl.when(jnp.logical_not(stencil_soon()))(lambda: stencil_part(gas, viscosity, out, table, speed))
+    pl.when(jnp.logical_not(is_early()))(lambda: droplet_part(drops, cells, kept, table, out, drops_out, *scratch))
+
+
+def droplet_part(drops, cells, kept, table, out, drops_out, samples, terms, source):
     slot = lax.broadcasted_iota(jnp.int32, (1, SLOTS), 1)
     filled = jnp.max(jnp.where(drops[0:1, :] > 0.0, slot + 1, 0))
     blocks = lax.div(filled + 1023, 1024)
@@ -243,7 +251,7 @@
         out[c] += source[slot * ROWS : slot * ROWS + ROWS, :]
 
 
-def stencil_part(gas, viscosity, out, drops_out, table, speed, samples, terms, source):
+def stencil_part(gas, viscosity, out, table, speed):
     inverse = 1.0 / gas[0]
     for k, c in enumerate((1, 2, 4, 5)):
         quotient = gas[c] * inverse
@@ -410,38 +418,47 @@
     both = ("ax", "rad")
     to_a, to_b, to_c, to_d, to_late = routes(lax.axis_size("ax"), lax.axis_size("rad"))
     came_a = lax.ppermute(axial_a, both, to_a)
-    results = (shape((C, ROWS, CZ), f32), shape((4, SLOTS), f32), shape((8 * ROWS, CZ), bf16))
-    scratch = [
-        pltpu.VMEM((3, ROWS, CZ), f32),
-        pltpu.VMEM((4, 32, 128), f32),
-        pltpu.VMEM((4, 32, 128), f32),
-        pltpu.VMEM((4 * ROWS, CZ), f32),
-    ]
-    late, axial_b, radial_a, radial_b, *first = pl.pallas_call(
-        early_kernel,
-        out_shape=(shape((208, CZ), f32), shape((200, CZ), f32), shape((104, CZ), f32), shape((104, CZ), f32), *results),
-        in_specs=[VM] * 6,
-        out_specs=(VM,) * 7,
-        scratch_shapes=scratch,
+    part, updated, table = shape((C, ROWS, CZ), f32), shape((4, SLOTS), f32), shape((8 * ROWS, CZ), bf16)
+    speed = [pltpu.VMEM((3, ROWS, CZ), f32)]
+    scratch = [pltpu.VMEM((4, 32, 128), f32), pltpu.VMEM((4, 32, 128), f32), pltpu.VMEM((4 * ROWS, CZ), f32)]
+    cost = lambda flops: pl.CostEstimate(flops=flops, bytes_accessed=0, transcendentals=0)
+
+    axial_b, radial_a, radial_b, part, table = pl.pallas_call(
+        first_kernel,
+        out_shape=(shape((200, CZ), f32), shape((104, CZ), f32), shape((104, CZ), f32), part, table),
+        in_specs=[VM] * 3,
+        out_specs=(VM,) * 5,
+        scratch_shapes=speed,
         compiler_params=params,
-        cost_estimate=pl.CostEstimate(flops=40000000000, bytes_accessed=6_000_000, transcendentals=0),
-        name="early",
-    )(gas, thick, drops, cells, kept, picks)
-    came_late = lax.ppermute(late, both, to_late)
+        cost_estimate=cost(4000000000),
+        name="first",
+    )(gas, thick, picks)
     came_b = lax.ppermute(axial_b, both, to_b)
     came_d = lax.ppermute(radial_b, both, to_d)
     came_c = lax.ppermute(radial_a, both, to_c)
-    part, updated, table = pl.pallas_call(
-        late_kernel,
-        out_shape=results,
-        in_specs=[VM] * 8,
+    late, part, updated = pl.pallas_call(
+        early_kernel,
+        out_shape=(shape((208, CZ), f32), shape(part.shape, f32), updated),
+        in_specs=[VM] * 7,
         out_specs=(VM,) * 3,
         scratch_shapes=scratch,
         compiler_params=params,
+        input_output_aliases={5: 1},
+        cost_estimate=cost(0),
+        name="early",
+    )(gas, picks, drops, cells, kept, part, table)
+    came_late = lax.ppermute(late, both, to_late)
+    part, updated, table = pl.pallas_call(
+        late_kernel,
+        out_shape=tuple(shape(x.shape, x.dtype) for x in (part, updated, table)),
+        in_specs=[VM] * 8,
+        out_specs=(VM,) * 3,
+        scratch_shapes=speed + scratch,
+        compiler_params=params,
         input_output_aliases={5: 0, 6: 1, 7: 2},
-        cost_estimate=pl.CostEstimate(flops=0, bytes_accessed=0, transcendentals=0),
+        cost_estimate=cost(0),
         name="late",
-    )(gas, thick, drops, cells, kept, *first)
+    )(gas, thick, drops, cells, kept, part, updated, table)
     finals = (shape((C, ROWS, CZ), f32), shape((4, SLOTS), f32), shape((4, 4 * CAP), f32))
     scratch = [
         pltpu.VMEM((C, ROWS, CZ), f32),
@@ -457,7 +474,7 @@
         out_specs=(HB,) * 3,
         scratch_shapes=scratch,
         compiler_params=params,
-        cost_estimate=pl.CostEstimate(flops=0, bytes_accessed=0, transcendentals=0),
+        cost_estimate=pl.CostEstimate(flops=4000000000, bytes_accessed=0, transcendentals=0),
         name="soon",
     )(*common)
     out, drops_out, arrivals_out = pl.pallas_call(

time: 45.2 us -> 37.2 us (0.82)
  the two profiles are of different devices: /device:TPU:6 before, /device:TPU:65 now
where the time goes in v7:
time: 37.2 us; the launch traced here: 37 us
  Pallas kernels  18.2 us (49%)
  starting transfers between devices  17.8 us (48%)
  between operations  0.95 us (3%)
    pallas_call x1, Pallas kernels, body(): pl.pallas_call(late_kernel, out_shape=tuple((shape(x.shape, x.dtype) for...  13.3 us
    ppermute x1, starting transfers between devices, body(): came_c = lax.ppermute(radial_a, both, to_c)  8.33 us
    ppermute x1, starting transfers between devices, body(): came_a = lax.ppermute(axial_a, both, to_a)  3.55 us
    ppermute x1, starting transfers between devices, body(): came_b = lax.ppermute(axial_b, both, to_b)  3.27 us
    pallas_call x1, Pallas kernels, body(): pl.pallas_call(soon_kernel, out_shape=finals, in_specs=[VM] * 9, out_spec...  3.01 us
    ppermute x1, starting transfers between devices, body(): came_d = lax.ppermute(radial_b, both, to_d)  1.92 us
    pallas_call x1, Pallas kernels, body(): pl.pallas_call(prep_kernel, out_shape=(shape((208, CZ), f32), shape((8, 4...  1.61 us
  transfers between devices with their start and end apart: 5, of which 0 were waited for; matrix products, arithmetic and copies ran while one was open for 0% of the time, Pallas kernels for 45%

profile of v7, /device:TPU:65, one launch (start us, length us, event | category | flops | bytes accessed | tf_op | source)
XLA Modules:
  0.0 37.0 jit_solution(1448333071539839877)
XLA Ops:
  0.6 0.0 copy-start
  0.6 1.6 %prep.1 = (f32[208,512]{1,0:T(8,128)S(1)}, f32[8,256]{1,0:T(8,128)S(1)}, f32[32,128]{1,0:T(8,128)S(1)}, f32[6,128,512]{2,1,0:T(8,128)S(1)}, f32[4,4096]{1,0:T(4,128)S(1)}, /*index=5*/s32[32,128]{1,0:T(8,128)S(1)}) custom-call(f32[6,128,512]{2,1,0:T(8,128)} %bitcast.9, f32[4,4096]{1,0:T(4,128)} %drops_in.1, s32[32,128]{1,0:T(8,128)} %bitcast.10, ...), custom_call_target="tpu_custom_call" | custom-call | tf_op jit(solution)/shard_map/prep/pallas_call | solution.py:398
  2.3 3.5 %collective-permute-start.1 = (f32[208,512]{1,0:T(8,128)S(1)}, f32[208,512]{1,0:T(8,128)S(1)}, u32[]{:S(2)}, u32[]{:S(2)}) collective-permute-start(f32[208,512]{1,0:T(8,128)S(1)} %get-tuple-element.39), channel_id=1, source_target_pairs={{0,4},{4,0},{1,5},{5,1},{2,6},{6,2},{3,7},{7,3},{8,12},{12,8},{9,1... | collective-permute-start | bytes 1277960 | tf_op jit(solution)/shard_map/ppermute | solution.py:420
  5.8 0.0 copy-done
  5.8 0.2 first.1
  6.0 3.3 %collective-permute-start.2 = (f32[200,512]{1,0:T(8,128)S(1)}, f32[200,512]{1,0:T(8,128)S(1)}, u32[]{:S(2)}, u32[]{:S(2)}) collective-permute-start(f32[200,512]{1,0:T(8,128)S(1)} %get-tuple-element.40), channel_id=1, source_target_pairs={{4,8},{8,4},{5,9},{9,5},{6,10},{10,6},{7,11},{11,7},{12,16},{16,12... | collective-permute-start | bytes 1228808 | tf_op jit(solution)/shard_map/ppermute | solution.py:436
  9.3 8.3 %collective-permute-start.3 = (f32[104,512]{1,0:T(8,128)S(1)}, f32[104,512]{1,0:T(8,128)S(1)}, u32[]{:S(2)}, u32[]{:S(2)}) collective-permute-start(f32[104,512]{1,0:T(8,128)S(1)} %get-tuple-element.41), channel_id=1, source_target_pairs={{0,1},{1,0},{2,3},{3,2},{4,5},{5,4},{6,7},{7,6},{8,9},{9,8},{10,11... | collective-permute-start | bytes 638984 | tf_op jit(solution)/shard_map/ppermute | solution.py:438
  17.6 1.9 %collective-permute-start.4 = (f32[104,512]{1,0:T(8,128)S(1)}, f32[104,512]{1,0:T(8,128)S(1)}, u32[]{:S(2)}, u32[]{:S(2)}) collective-permute-start(f32[104,512]{1,0:T(8,128)S(1)} %get-tuple-element.42), channel_id=1, source_target_pairs={{1,2},{2,1},{5,6},{6,5},{9,10},{10,9},{13,14},{14,13},{17,18},{18,... | collective-permute-start | bytes 638984 | tf_op jit(solution)/shard_map/ppermute | solution.py:437
  19.6 0.7 %collective-permute-start = (f32[208,512]{1,0:T(8,128)S(1)}, f32[208,512]{1,0:T(8,128)S(1)}, u32[]{:S(2)}, u32[]{:S(2)}) collective-permute-start(f32[208,512]{1,0:T(8,128)S(1)} %get-tuple-element.33), channel_id=1, source_target_pairs={{64,60},{65,61},{66,62},{67,63},{128,124},{129,125},{130,126},{131... | collective-permute-start | bytes 1277960 | tf_op jit(solution)/shard_map/ppermute | solution.py:450
  20.3 13.3 %late.1 = (f32[6,128,512]{2,1,0:T(8,128)S(1)}, f32[4,4096]{1,0:T(4,128)S(1)}, bf16[1024,512]{1,0:T(8,128)(2,1)S(1)}) custom-call(f32[6,128,512]{2,1,0:T(8,128)S(1)} %get-tuple-element.26.gas.refs_2_, f32[128,512]{1,0:T(8,128)S(1)} %bitcast.5, f32[4,4096]{1,0:T(4,128)S(1)} %get-tuple-element.28.drops, ...), custom_call_target="tpu_custom_call", output_to_operand_aliasing={{0}: (5, {}), {1}: (6, {}), {2}: (7, {})} | custom-call | tf_op jit(solution)/shard_map/late/pallas_call | solution.py:451
  33.6 0.0 collective-permute-done.3.refs_7_.radial_a
  33.6 0.0 collective-permute-done.4.refs_8_.radial_b
  33.6 0.0 collective-permute-done.2.refs_6_.axial_b
  33.6 0.0 collective-permute-done.1.refs_5_.axial_a
  33.6 3.0 %soon.1 = (f32[6,128,512]{2,1,0:T(8,128)}, f32[4,4096]{1,0:T(4,128)}, f32[4,256]{1,0:T(4,128)}) custom-call(f32[6,128,512]{2,1,0:T(8,128)S(1)} %get-tuple-element.36.refs_0_.part, f32[4,4096]{1,0:T(4,128)S(1)} %get-tuple-element.37.refs_1_.updated, f32[6,128,512]{2,1,0:T(8,128)S(1)} %get-tuple-element.26.gas.refs_2_, f32[128,512]{1,0:T(8,128)S(1)} %bitcast.6, ...), custom_call_target="tpu_custom_call" | custom-call | flops 4000000000 | tf_op jit(solution)/shard_map/soon/pallas_call | solution.py:470
  36.7 0.0 collective-permute-done.late
  36.7 0.1 last.1
  (1 shorter events, 0.0 us)
Async XLA Ops:
  0.6 5.2 %copy-start = (f32[8,16,512]{2,1,0:T(8,128)S(1)}, f32[8,16,512]{2,1,0:T(8,128)}, u32[]{:S(2)}) copy-start(f32[8,16,512]{2,1,0:T(8,128)} %param.7) | copy-start | bytes 786436
  2.3 31.4 %collective-permute-start.1 = (f32[208,512]{1,0:T(8,128)S(1)}, f32[208,512]{1,0:T(8,128)S(1)}, u32[]{:S(2)}, u32[]{:S(2)}) collective-permute-start(f32[208,512]{1,0:T(8,128)S(1)} %get-tuple-element.39), channel_id=1, source_target_pairs={{0,4},{4,0},{1,5},{5,1},{2,6},{6,2},{3,7},{7,3},{8,12},{12,8},{9,1... | collective-permute-start | bytes 1277960 | tf_op jit(solution)/shard_map/ppermute | solution.py:420
  6.0 27.6 %collective-permute-start.2 = (f32[200,512]{1,0:T(8,128)S(1)}, f32[200,512]{1,0:T(8,128)S(1)}, u32[]{:S(2)}, u32[]{:S(2)}) collective-permute-start(f32[200,512]{1,0:T(8,128)S(1)} %get-tuple-element.40), channel_id=1, source_target_pairs={{4,8},{8,4},{5,9},{9,5},{6,10},{10,6},{7,11},{11,7},{12,16},{16,12... | collective-permute-start | bytes 1228808 | tf_op jit(solution)/shard_map/ppermute | solution.py:436
  9.3 24.3 %collective-permute-start.3 = (f32[104,512]{1,0:T(8,128)S(1)}, f32[104,512]{1,0:T(8,128)S(1)}, u32[]{:S(2)}, u32[]{:S(2)}) collective-permute-start(f32[104,512]{1,0:T(8,128)S(1)} %get-tuple-element.41), channel_id=1, source_target_pairs={{0,1},{1,0},{2,3},{3,2},{4,5},{5,4},{6,7},{7,6},{8,9},{9,8},{10,11... | collective-permute-start | bytes 638984 | tf_op jit(solution)/shard_map/ppermute | solution.py:438
  17.6 16.0 %collective-permute-start.4 = (f32[104,512]{1,0:T(8,128)S(1)}, f32[104,512]{1,0:T(8,128)S(1)}, u32[]{:S(2)}, u32[]{:S(2)}) collective-permute-start(f32[104,512]{1,0:T(8,128)S(1)} %get-tuple-element.42), channel_id=1, source_target_pairs={{1,2},{2,1},{5,6},{6,5},{9,10},{10,9},{13,14},{14,13},{17,18},{18,... | collective-permute-start | bytes 638984 | tf_op jit(solution)/shard_map/ppermute | solution.py:437
  19.6 17.1 %collective-permute-start = (f32[208,512]{1,0:T(8,128)S(1)}, f32[208,512]{1,0:T(8,128)S(1)}, u32[]{:S(2)}, u32[]{:S(2)}) collective-permute-start(f32[208,512]{1,0:T(8,128)S(1)} %get-tuple-element.33), channel_id=1, source_target_pairs={{64,60},{65,61},{66,62},{67,63},{128,124},{129,125},{130,126},{131... | collective-permute-start | bytes 1277960 | tf_op jit(solution)/shard_map/ppermute | solution.py:450

commit v8 on v7

--- a/solution.py
+++ b/solution.py
@@ -142,26 +142,19 @@
     return (lax.broadcasted_iota(jnp.int32, (size, width), 0) == index).astype(f32).astype(bf16)
 
 
-def gather_block(table, where):
-    around = one_hot(where & (CZ - 1), CZ)
-    got = jnp.dot(table[...], around, preferred_element_type=f32)
+def gather_block(table, around, where):
+    got = jnp.dot(table[...], jnp.concatenate([around, around], axis=0), preferred_element_type=f32)
     mask = lax.broadcasted_iota(jnp.int32, (ROWS, where.shape[1]), 0) == (where >> 9)
-    samples = []
-    for k in range(4):
-        both = got[2 * ROWS * k : 2 * ROWS * k + ROWS] + got[2 * ROWS * k + ROWS : 2 * ROWS * k + 2 * ROWS]
-        samples.append(jnp.sum(jnp.where(mask, both, 0.0), axis=0, keepdims=True))
-    return samples
-
-
-def deposit_block(terms, where):
-    around = one_hot(where & (CZ - 1), CZ)
-    mask = lax.broadcasted_iota(jnp.int32, (ROWS, where.shape[1]), 0) == (where >> 9)
+    return [
+        jnp.sum(jnp.where(mask, got[ROWS * k : ROWS * k + ROWS], 0.0), axis=0, keepdims=True) for k in range(4)
+    ]
+
+
+def deposit_block(terms, around, where):
+    row = one_hot(where >> 9, ROWS)
     halves = [split2(t) for t in terms]
     spread = jnp.concatenate(
-        [
-            jnp.concatenate([jnp.where(mask, h[side].astype(f32), 0.0).astype(bf16) for h in halves], axis=0)
-            for side in range(2)
-        ],
+        [jnp.concatenate([row * h[side] for h in halves], axis=0) for side in range(2)],
         axis=1,
     )
     twice = jnp.concatenate([around, around], axis=1)
@@ -170,7 +163,7 @@
 
 def stencil_soon():
     a = lax.axis_index("ax")
-    return is_early() | ((lax.rem(a, 2) == 1) & (lax.rem(a, WRAP) != WRAP - 1))
+    return is_early() | ((lax.rem(a, 2) == 1) & (a > 1) & (lax.rem(a, WRAP) != WRAP - 1))
 
 
 def first_kernel(gas, viscosity, picks, axial_b, radial_a, radial_b, out, table, speed):
@@ -192,7 +185,7 @@
     pl.when(jnp.logical_not(is_early()))(lambda: droplet_part(drops, cells, kept, table, out, drops_out, *scratch))
 
 
-def droplet_part(drops, cells, kept, table, out, drops_out, samples, terms, source):
+def droplet_part(drops, cells, kept, table, out, drops_out, samples, terms, source, hots):
     slot = lax.broadcasted_iota(jnp.int32, (1, SLOTS), 1)
     filled = jnp.max(jnp.where(drops[0:1, :] > 0.0, slot + 1, 0))
     blocks = lax.div(filled + 1023, 1024)
@@ -200,15 +193,23 @@
     def join(load, first, rows):
         return jnp.concatenate([load(pl.ds(first + s, 1)) for s in range(rows)], axis=1)
 
+    def lanes(first, rows):
+        return pl.ds(first * 128 if isinstance(first, int) else pl.multiple_of(first * 128, 128 * rows), 128 * rows)
+
     def sample(first, rows):
-        got = gather_block(table, join(lambda at: cells[at, :], first, rows))
+        where = join(lambda at: cells[at, :], first, rows)
+        around = one_hot(where & (CZ - 1), CZ)
+        hots[:, lanes(first, rows)] = around
+        got = gather_block(table, around, where)
         for k in range(4):
             for s in range(rows):
                 samples[k, pl.ds(first + s, 1), :] = got[k][:, 128 * s : 128 * s + 128]
 
     def deposit(first, rows):
         where = join(lambda at: cells[at, :], first, rows)
-        return deposit_block([join(lambda at: terms[k, at, :], first, rows) for k in range(4)], where)
+        return deposit_block(
+            [join(lambda at: terms[k, at, :], first, rows) for k in range(4)], hots[:, lanes(first, rows)], where
+        )
 
     def sample_loop(b, carry):
         sample(pl.multiple_of(8 * b, 8), 8)
@@ -253,37 +254,33 @@
 
 def stencil_part(gas, viscosity, out, table, speed):
     inverse = 1.0 / gas[0]
+    scale = time_step / 12.0
     for k, c in enumerate((1, 2, 4, 5)):
         quotient = gas[c] * inverse
         if k < 2:
-            speed[k] = quotient
+            speed[k] = quotient * scale
         hi, lo = split2(quotient)
-        table[2 * ROWS * k : 2 * ROWS * k + ROWS, :] = hi
-        table[2 * ROWS * k + ROWS : 2 * ROWS * k + 2 * ROWS, :] = lo
-    speed[2] = gas[3] * inverse
-    lane = lax.broadcasted_iota(jnp.int32, (CY, CZ), 0)
+        table[ROWS * k : ROWS * k + ROWS, 0:CZ] = hi
+        table[ROWS * k : ROWS * k + ROWS, CZ : 2 * CZ] = lo
+    speed[2] = gas[3] * inverse * scale
+    speed[3] = viscosity[...] * scale
 
     def component(c, carry):
         layers = [gas[c, CY * i : CY * i + CY, :] for i in range(CX)]
+        zero = jnp.zeros_like(layers[0])
         for i in range(CX):
             rows = slice(CY * i, CY * i + CY)
             x = layers[i]
-            zero = jnp.zeros_like(x)
             ax = [layers[i + k] if 0 <= i + k < CX else zero for k in (-2, -1, 1, 2)]
-            ra = []
-            for k in (-2, -1, 1, 2):
-                moved = pltpu.roll(x, (-k) % CY, axis=0)
-                ok = (lane + k >= 0) & (lane + k < CY)
-                ra.append(jnp.where(ok, moved, 0.0))
+            tall = jnp.concatenate([x, zero[0:8]], axis=0)
+            ra = [pltpu.roll(tall, (-k) % (CY + 8), axis=0)[0:CY] for k in (-2, -1, 1, 2)]
             az = [pltpu.roll(x, (-k) % CZ, axis=1) for k in (-2, -1, 1, 2)]
             near = (ax[1] + ax[2]) + (ra[1] + ra[2]) + (az[1] + az[2])
             far = (ax[0] + ax[3]) + (ra[0] + ra[3]) + (az[0] + az[3])
-            laplace = (16.0 * near - far - 90.0 * x) * (1.0 / 12.0)
-            transport = zero
+            value = x + speed[3, rows, :] * (16.0 * near - far - 90.0 * x)
             for j, n in enumerate((ax, ra, az)):
-                slope = (8.0 * (n[2] - n[1]) - (n[3] - n[0])) * (1.0 / 12.0)
-                transport = transport + speed[j, rows, :] * slope
-            out[c, rows, :] = x + time_step * (viscosity[rows, :] * laplace - transport)
+                value = value - speed[j, rows, :] * (8.0 * (n[2] - n[1]) - (n[3] - n[0]))
+            out[c, rows, :] = value
         return carry
 
     lax.fori_loop(0, C, component, 0)
@@ -324,11 +321,12 @@
         got.append(jnp.where(odd == 1, in_b, in_a))
     got = jnp.concatenate(got, axis=1)
     where = got[4:5].astype(jnp.int32)
-    samples = gather_block(table, where)
+    around = one_hot(where & (CZ - 1), CZ)
+    samples = gather_block(table, around, where)
     changed, terms = evaporate(got[0:1], got[1:2], got[2:3], got[3:4], samples)
     arrivals[...] = jnp.concatenate(changed, axis=0)
     copies[1].start()
-    source = deposit_block(terms, where)
+    source = deposit_block(terms, around, where)
     lane = lax.broadcasted_iota(jnp.int32, (CY, CZ), 0)
     for i in range(CX):
         rows = slice(CY * i, CY * i + CY)
@@ -418,9 +416,9 @@
     both = ("ax", "rad")
     to_a, to_b, to_c, to_d, to_late = routes(lax.axis_size("ax"), lax.axis_size("rad"))
     came_a = lax.ppermute(axial_a, both, to_a)
-    part, updated, table = shape((C, ROWS, CZ), f32), shape((4, SLOTS), f32), shape((8 * ROWS, CZ), bf16)
-    speed = [pltpu.VMEM((3, ROWS, CZ), f32)]
-    scratch = [pltpu.VMEM((4, 32, 128), f32), pltpu.VMEM((4, 32, 128), f32), pltpu.VMEM((4 * ROWS, CZ), f32)]
+    part, updated, table = shape((C, ROWS, CZ), f32), shape((4, SLOTS), f32), shape((4 * ROWS, 2 * CZ), bf16)
+    speed = [pltpu.VMEM((4, ROWS, CZ), f32)]
+    scratch = [pltpu.VMEM((4, 32, 128), f32), pltpu.VMEM((4, 32, 128), f32), pltpu.VMEM((4 * ROWS, CZ), f32), pltpu.VMEM((CZ, SLOTS), bf16)]
     cost = lambda flops: pl.CostEstimate(flops=flops, bytes_accessed=0, transcendentals=0)
 
     axial_b, radial_a, radial_b, part, table = pl.pallas_call(

time: 37.2 us -> 34.5 us (0.927)
  the two profiles are of different devices: /device:TPU:65 before, /device:TPU:6 now
where the time goes in v8:
time: 34.5 us; the launch traced here: 34.2 us
  starting transfers between devices  17.5 us (51%)
  Pallas kernels  11.2 us (32%)
  waiting for transfers between devices  4.52 us (13%)
  between operations  0.92 us (3%)
    ppermute x1, starting transfers between devices, body(): came_late = lax.ppermute(late, both, to_late)  7.67 us
    ppermute x1, starting transfers between devices, body(): came_a = lax.ppermute(axial_a, both, to_a)  3.83 us
    pallas_call x1, Pallas kernels, body(): pl.pallas_call(early_kernel, out_shape=(shape((208, CZ), f32), shape(part...  3.45 us
    pallas_call x1, Pallas kernels, body(): pl.pallas_call(first_kernel, out_shape=(shape((200, CZ), f32), shape((104...  3.04 us
    pallas_call x1, Pallas kernels, body(): pl.pallas_call(soon_kernel, out_shape=finals, in_specs=[VM] * 9, out_spec...  2.99 us
    ppermute x1, starting transfers between devices, body(): came_d = lax.ppermute(radial_b, both, to_d)  2.84 us
    ppermute x1, waiting for transfers between devices, body(): came_b = lax.ppermute(axial_b, both, to_b)  2.3 us
    ppermute x1, waiting for transfers between devices, body(): came_late = lax.ppermute(late, both, to_late)  2.21 us
  transfers between devices with their start and end apart: 5, of which 2 were waited for; matrix products, arithmetic and copies ran while one was open for 0% of the time, Pallas kernels for 28%

profile of v8, /device:TPU:6, one launch (start us, length us, event | category | flops | bytes accessed | tf_op | source)
XLA Modules:
  0.0 34.2 jit_solution(8482024635362248794)
XLA Ops:
  0.6 0.0 copy-start
  0.6 1.6 %prep.1 = (f32[208,512]{1,0:T(8,128)S(1)}, f32[8,256]{1,0:T(8,128)S(1)}, f32[32,128]{1,0:T(8,128)S(1)}, f32[6,128,512]{2,1,0:T(8,128)S(1)}, f32[4,4096]{1,0:T(4,128)S(1)}, /*index=5*/s32[32,128]{1,0:T(8,128)S(1)}) custom-call(f32[6,128,512]{2,1,0:T(8,128)} %bitcast.9, f32[4,4096]{1,0:T(4,128)} %drops_in.1, s32[32,128]{1,0:T(8,128)} %bitcast.10, ...), custom_call_target="tpu_custom_call" | custom-call | tf_op jit(solution)/shard_map/prep/pallas_call | solution.py:396
  2.3 3.8 %collective-permute-start.1 = (f32[208,512]{1,0:T(8,128)S(1)}, f32[208,512]{1,0:T(8,128)S(1)}, u32[]{:S(2)}, u32[]{:S(2)}) collective-permute-start(f32[208,512]{1,0:T(8,128)S(1)} %get-tuple-element.39), channel_id=1, source_target_pairs={{0,4},{4,0},{1,5},{5,1},{2,6},{6,2},{3,7},{7,3},{8,12},{12,8},{9,1... | collective-permute-start | bytes 1277960 | tf_op jit(solution)/shard_map/ppermute | solution.py:418
  6.1 0.0 copy-done
  6.1 3.0 %first.1 = (f32[200,512]{1,0:T(8,128)S(1)}, f32[104,512]{1,0:T(8,128)S(1)}, f32[104,512]{1,0:T(8,128)S(1)}, f32[6,128,512]{2,1,0:T(8,128)S(1)}, bf16[512,1024]{1,0:T(8,128)(2,1)S(1)}) custom-call(f32[6,128,512]{2,1,0:T(8,128)S(1)} %get-tuple-element.26.gas.refs_2_, f32[128,512]{1,0:T(8,128)S(1)} %bitcast.4, f32[8,256]{1,0:T(8,128)S(1)} %get-tuple-element.27.picks), custom_call_target="tpu_custom_call" | custom-call | flops 4000000000 | tf_op jit(solution)/shard_map/first/pallas_call | solution.py:424
  9.2 1.3 %collective-permute-start.2 = (f32[200,512]{1,0:T(8,128)S(1)}, f32[200,512]{1,0:T(8,128)S(1)}, u32[]{:S(2)}, u32[]{:S(2)}) collective-permute-start(f32[200,512]{1,0:T(8,128)S(1)} %get-tuple-element.40), channel_id=1, source_target_pairs={{4,8},{8,4},{5,9},{9,5},{6,10},{10,6},{7,11},{11,7},{12,16},{16,12... | collective-permute-start | bytes 1228808 | tf_op jit(solution)/shard_map/ppermute | solution.py:434
  10.5 1.9 %collective-permute-start.3 = (f32[104,512]{1,0:T(8,128)S(1)}, f32[104,512]{1,0:T(8,128)S(1)}, u32[]{:S(2)}, u32[]{:S(2)}) collective-permute-start(f32[104,512]{1,0:T(8,128)S(1)} %get-tuple-element.41), channel_id=1, source_target_pairs={{0,1},{1,0},{2,3},{3,2},{4,5},{5,4},{6,7},{7,6},{8,9},{9,8},{10,11... | collective-permute-start | bytes 638984 | tf_op jit(solution)/shard_map/ppermute | solution.py:436
  12.4 2.8 %collective-permute-start.4 = (f32[104,512]{1,0:T(8,128)S(1)}, f32[104,512]{1,0:T(8,128)S(1)}, u32[]{:S(2)}, u32[]{:S(2)}) collective-permute-start(f32[104,512]{1,0:T(8,128)S(1)} %get-tuple-element.42), channel_id=1, source_target_pairs={{1,2},{2,1},{5,6},{6,5},{9,10},{10,9},{13,14},{14,13},{17,18},{18,... | collective-permute-start | bytes 638984 | tf_op jit(solution)/shard_map/ppermute | solution.py:435
  15.2 3.5 %early.1 = (f32[208,512]{1,0:T(8,128)S(1)}, f32[6,128,512]{2,1,0:T(8,128)S(1)}, f32[4,4096]{1,0:T(4,128)S(1)}) custom-call(f32[6,128,512]{2,1,0:T(8,128)S(1)} %get-tuple-element.26.gas.refs_2_, f32[8,256]{1,0:T(8,128)S(1)} %get-tuple-element.27.picks, f32[4,4096]{1,0:T(4,128)S(1)} %get-tuple-element.28.drops, ...), custom_call_target="tpu_custom_call", output_to_operand_aliasing={{1}: (5, {})} | custom-call | tf_op jit(solution)/shard_map/early/pallas_call | solution.py:437
  18.7 7.7 %collective-permute-start = (f32[208,512]{1,0:T(8,128)S(1)}, f32[208,512]{1,0:T(8,128)S(1)}, u32[]{:S(2)}, u32[]{:S(2)}) collective-permute-start(f32[208,512]{1,0:T(8,128)S(1)} %get-tuple-element.33), channel_id=1, source_target_pairs={{64,60},{65,61},{66,62},{67,63},{128,124},{129,125},{130,126},{131... | collective-permute-start | bytes 1277960 | tf_op jit(solution)/shard_map/ppermute | solution.py:448
  26.4 0.0 collective-permute-done.3.refs_7_.radial_a
  26.4 0.0 collective-permute-done.4.refs_8_.radial_b
  26.4 2.3 %collective-permute-done.2.refs_6_.axial_b = f32[200,512]{1,0:T(8,128)S(1)} collective-permute-done((f32[200,512]{1,0:T(8,128)S(1)}, f32[200,512]{1,0:T(8,128)S(1)}, u32[]{:S(2)}, u32[]{:S(2)}) %collective-permute-start.2) | collective-permute-done | bytes 409632 | tf_op jit(solution)/shard_map/ppermute | solution.py:434
  28.7 0.0 collective-permute-done.1.refs_5_.axial_a
  28.7 3.0 %soon.1 = (f32[6,128,512]{2,1,0:T(8,128)}, f32[4,4096]{1,0:T(4,128)}, f32[4,256]{1,0:T(4,128)}) custom-call(f32[6,128,512]{2,1,0:T(8,128)S(1)} %get-tuple-element.36.refs_0_.part, f32[4,4096]{1,0:T(4,128)S(1)} %get-tuple-element.37.refs_1_.updated, f32[6,128,512]{2,1,0:T(8,128)S(1)} %get-tuple-element.26.gas.refs_2_, f32[128,512]{1,0:T(8,128)S(1)} %bitcast.6, ...), custom_call_target="tpu_custom_call" | custom-call | flops 4000000000 | tf_op jit(solution)/shard_map/soon/pallas_call | solution.py:468
  31.7 2.2 %collective-permute-done.late = f32[208,512]{1,0:T(8,128)S(1)} collective-permute-done((f32[208,512]{1,0:T(8,128)S(1)}, f32[208,512]{1,0:T(8,128)S(1)}, u32[]{:S(2)}, u32[]{:S(2)}) %collective-permute-start) | collective-permute-done | bytes 426016 | tf_op jit(solution)/shard_map/ppermute | solution.py:448
  33.9 0.1 last.1
  (1 shorter events, 0.0 us)
Async XLA Ops:
  0.6 5.5 %copy-start = (f32[8,16,512]{2,1,0:T(8,128)S(1)}, f32[8,16,512]{2,1,0:T(8,128)}, u32[]{:S(2)}) copy-start(f32[8,16,512]{2,1,0:T(8,128)} %param.7) | copy-start | bytes 786436
  2.3 26.5 %collective-permute-start.1 = (f32[208,512]{1,0:T(8,128)S(1)}, f32[208,512]{1,0:T(8,128)S(1)}, u32[]{:S(2)}, u32[]{:S(2)}) collective-permute-start(f32[208,512]{1,0:T(8,128)S(1)} %get-tuple-element.39), channel_id=1, source_target_pairs={{0,4},{4,0},{1,5},{5,1},{2,6},{6,2},{3,7},{7,3},{8,12},{12,8},{9,1... | collective-permute-start | bytes 1277960 | tf_op jit(solution)/shard_map/ppermute | solution.py:418
  9.2 19.6 %collective-permute-start.2 = (f32[200,512]{1,0:T(8,128)S(1)}, f32[200,512]{1,0:T(8,128)S(1)}, u32[]{:S(2)}, u32[]{:S(2)}) collective-permute-start(f32[200,512]{1,0:T(8,128)S(1)} %get-tuple-element.40), channel_id=1, source_target_pairs={{4,8},{8,4},{5,9},{9,5},{6,10},{10,6},{7,11},{11,7},{12,16},{16,12... | collective-permute-start | bytes 1228808 | tf_op jit(solution)/shard_map/ppermute | solution.py:434
  10.5 16.0 %collective-permute-start.3 = (f32[104,512]{1,0:T(8,128)S(1)}, f32[104,512]{1,0:T(8,128)S(1)}, u32[]{:S(2)}, u32[]{:S(2)}) collective-permute-start(f32[104,512]{1,0:T(8,128)S(1)} %get-tuple-element.41), channel_id=1, source_target_pairs={{0,1},{1,0},{2,3},{3,2},{4,5},{5,4},{6,7},{7,6},{8,9},{9,8},{10,11... | collective-permute-start | bytes 638984 | tf_op jit(solution)/shard_map/ppermute | solution.py:436
  12.4 14.0 %collective-permute-start.4 = (f32[104,512]{1,0:T(8,128)S(1)}, f32[104,512]{1,0:T(8,128)S(1)}, u32[]{:S(2)}, u32[]{:S(2)}) collective-permute-start(f32[104,512]{1,0:T(8,128)S(1)} %get-tuple-element.42), channel_id=1, source_target_pairs={{1,2},{2,1},{5,6},{6,5},{9,10},{10,9},{13,14},{14,13},{17,18},{18,... | collective-permute-start | bytes 638984 | tf_op jit(solution)/shard_map/ppermute | solution.py:435
  18.7 15.2 %collective-permute-start = (f32[208,512]{1,0:T(8,128)S(1)}, f32[208,512]{1,0:T(8,128)S(1)}, u32[]{:S(2)}, u32[]{:S(2)}) collective-permute-start(f32[208,512]{1,0:T(8,128)S(1)} %get-tuple-element.33), channel_id=1, source_target_pairs={{64,60},{65,61},{66,62},{67,63},{128,124},{129,125},{130,126},{131... | collective-permute-start | bytes 1277960 | tf_op jit(solution)/shard_map/ppermute | solution.py:448

commit v9 on v8

--- a/solution.py
+++ b/solution.py
@@ -162,8 +162,9 @@
 
 
 def stencil_soon():
-    a = lax.axis_index("ax")
-    return is_early() | ((lax.rem(a, 2) == 1) & (a > 1) & (lax.rem(a, WRAP) != WRAP - 1))
+    a, r = lax.axis_index("ax"), lax.axis_index("rad")
+    near_first = ((a == 0) & (r == 1)) | ((a == 1) & (r == 1)) | ((a == 2) & (r <= 1))
+    return is_early() | near_first | ((lax.rem(a, 2) == 1) & (a > 1) & (lax.rem(a, WRAP) != WRAP - 1))
 
 
 def first_kernel(gas, viscosity, picks, axial_b, radial_a, radial_b, out, table, speed):
@@ -442,7 +443,7 @@
         scratch_shapes=scratch,
         compiler_params=params,
         input_output_aliases={5: 1},
-        cost_estimate=cost(0),
+        cost_estimate=cost(4000000000),
         name="early",
     )(gas, picks, drops, cells, kept, part, table)
     came_late = lax.ppermute(late, both, to_late)
@@ -472,7 +473,7 @@
         out_specs=(HB,) * 3,
         scratch_shapes=scratch,
         compiler_params=params,
-        cost_estimate=pl.CostEstimate(flops=4000000000, bytes_accessed=0, transcendentals=0),
+        cost_estimate=pl.CostEstimate(flops=0, bytes_accessed=0, transcendentals=0),
         name="soon",
     )(*common)
     out, drops_out, arrivals_out = pl.pallas_call(

time: 34.5 us -> 42.2 us (1.22)
  waiting for transfers between devices: 4.52 us -> 13.2 us
  starting transfers between devices: 17.5 us -> 16.8 us
    ppermute x1, waiting for transfers between devices: 2.3 us -> 7.98 us  [body(): came_b = lax.ppermute(axial_b, both, to_b)]
    ppermute x1, waiting for transfers between devices: 0.01 us -> 5.17 us  [body(): came_d = lax.ppermute(radial_b, both, to_d)]
    ppermute x1, waiting for transfers between devices: 2.21 us -> 0.01 us  [body(): came_late = lax.ppermute(late, both, to_late)]
    ppermute x1, starting transfers between devices: 2.84 us -> 1.94 us  [body(): came_d = lax.ppermute(radial_b, both, to_d)]
  transfers between devices with their start and end apart: 5 -> 5, of which waited for: 2 -> 2; matrix products, arithmetic and copies ran while one was open for 0% -> 0% of each run, Pallas kernels for 28% -> 22%
where the time goes in v9:
time: 42.2 us; the launch traced here: 42 us
  starting transfers between devices  16.8 us (40%)
  waiting for transfers between devices  13.2 us (31%)
  Pallas kernels  11.1 us (26%)
  between operations  0.92 us (2%)
    ppermute x1, waiting for transfers between devices, body(): came_b = lax.ppermute(axial_b, both, to_b)  7.98 us
    ppermute x1, starting transfers between devices, body(): came_late = lax.ppermute(late, both, to_late)  7.69 us
    ppermute x1, waiting for transfers between devices, body(): came_d = lax.ppermute(radial_b, both, to_d)  5.17 us
    ppermute x1, starting transfers between devices, body(): came_a = lax.ppermute(axial_a, both, to_a)  3.83 us
    pallas_call x1, Pallas kernels, body(): pl.pallas_call(early_kernel, out_shape=(shape((208, CZ), f32), shape(part...  3.28 us
    pallas_call x1, Pallas kernels, body(): pl.pallas_call(first_kernel, out_shape=(shape((200, CZ), f32), shape((104...  3.04 us
    pallas_call x1, Pallas kernels, body(): pl.pallas_call(soon_kernel, out_shape=finals, in_specs=[VM] * 9, out_spec...  3.02 us
    ppermute x1, starting transfers between devices, body(): came_d = lax.ppermute(radial_b, both, to_d)  1.94 us
  transfers between devices with their start and end apart: 5, of which 2 were waited for; matrix products, arithmetic and copies ran while one was open for 0% of the time, Pallas kernels for 22%

profile of v9, /device:TPU:6, one launch (start us, length us, event | category | flops | bytes accessed | tf_op | source)
XLA Modules:
  0.0 42.0 jit_solution(5276374142693865437)
XLA Ops:
  0.6 0.0 copy-start
  0.6 1.6 %prep.1 = (f32[208,512]{1,0:T(8,128)S(1)}, f32[8,256]{1,0:T(8,128)S(1)}, f32[32,128]{1,0:T(8,128)S(1)}, f32[6,128,512]{2,1,0:T(8,128)S(1)}, f32[4,4096]{1,0:T(4,128)S(1)}, /*index=5*/s32[32,128]{1,0:T(8,128)S(1)}) custom-call(f32[6,128,512]{2,1,0:T(8,128)} %bitcast.9, f32[4,4096]{1,0:T(4,128)} %drops_in.1, s32[32,128]{1,0:T(8,128)} %bitcast.10, ...), custom_call_target="tpu_custom_call" | custom-call | tf_op jit(solution)/shard_map/prep/pallas_call | solution.py:397
  2.3 3.8 %collective-permute-start.1 = (f32[208,512]{1,0:T(8,128)S(1)}, f32[208,512]{1,0:T(8,128)S(1)}, u32[]{:S(2)}, u32[]{:S(2)}) collective-permute-start(f32[208,512]{1,0:T(8,128)S(1)} %get-tuple-element.39), channel_id=1, source_target_pairs={{0,4},{4,0},{1,5},{5,1},{2,6},{6,2},{3,7},{7,3},{8,12},{12,8},{9,1... | collective-permute-start | bytes 1277960 | tf_op jit(solution)/shard_map/ppermute | solution.py:419
  6.1 0.0 copy-done
  6.1 3.0 %first.1 = (f32[200,512]{1,0:T(8,128)S(1)}, f32[104,512]{1,0:T(8,128)S(1)}, f32[104,512]{1,0:T(8,128)S(1)}, f32[6,128,512]{2,1,0:T(8,128)S(1)}, bf16[512,1024]{1,0:T(8,128)(2,1)S(1)}) custom-call(f32[6,128,512]{2,1,0:T(8,128)S(1)} %get-tuple-element.26.gas.refs_2_, f32[128,512]{1,0:T(8,128)S(1)} %bitcast.4, f32[8,256]{1,0:T(8,128)S(1)} %get-tuple-element.27.picks), custom_call_target="tpu_custom_call" | custom-call | flops 4000000000 | tf_op jit(solution)/shard_map/first/pallas_call | solution.py:425
  9.2 3.3 %early.1 = (f32[208,512]{1,0:T(8,128)S(1)}, f32[6,128,512]{2,1,0:T(8,128)S(1)}, f32[4,4096]{1,0:T(4,128)S(1)}) custom-call(f32[6,128,512]{2,1,0:T(8,128)S(1)} %get-tuple-element.26.gas.refs_2_, f32[8,256]{1,0:T(8,128)S(1)} %get-tuple-element.27.picks, f32[4,4096]{1,0:T(4,128)S(1)} %get-tuple-element.28.drops, ...), custom_call_target="tpu_custom_call", output_to_operand_aliasing={{1}: (5, {})} | custom-call | flops 4000000000 | tf_op jit(solution)/shard_map/early/pallas_call | solution.py:438
  12.4 7.7 %collective-permute-start = (f32[208,512]{1,0:T(8,128)S(1)}, f32[208,512]{1,0:T(8,128)S(1)}, u32[]{:S(2)}, u32[]{:S(2)}) collective-permute-start(f32[208,512]{1,0:T(8,128)S(1)} %get-tuple-element.33), channel_id=1, source_target_pairs={{64,60},{65,61},{66,62},{67,63},{128,124},{129,125},{130,126},{131... | collective-permute-start | bytes 1277960 | tf_op jit(solution)/shard_map/ppermute | solution.py:449
  20.1 1.5 %collective-permute-start.2 = (f32[200,512]{1,0:T(8,128)S(1)}, f32[200,512]{1,0:T(8,128)S(1)}, u32[]{:S(2)}, u32[]{:S(2)}) collective-permute-start(f32[200,512]{1,0:T(8,128)S(1)} %get-tuple-element.40), channel_id=1, source_target_pairs={{4,8},{8,4},{5,9},{9,5},{6,10},{10,6},{7,11},{11,7},{12,16},{16,12... | collective-permute-start | bytes 1228808 | tf_op jit(solution)/shard_map/ppermute | solution.py:435
  21.6 1.9 %collective-permute-start.3 = (f32[104,512]{1,0:T(8,128)S(1)}, f32[104,512]{1,0:T(8,128)S(1)}, u32[]{:S(2)}, u32[]{:S(2)}) collective-permute-start(f32[104,512]{1,0:T(8,128)S(1)} %get-tuple-element.41), channel_id=1, source_target_pairs={{0,1},{1,0},{2,3},{3,2},{4,5},{5,4},{6,7},{7,6},{8,9},{9,8},{10,11... | collective-permute-start | bytes 638984 | tf_op jit(solution)/shard_map/ppermute | solution.py:437
  23.5 1.9 %collective-permute-start.4 = (f32[104,512]{1,0:T(8,128)S(1)}, f32[104,512]{1,0:T(8,128)S(1)}, u32[]{:S(2)}, u32[]{:S(2)}) collective-permute-start(f32[104,512]{1,0:T(8,128)S(1)} %get-tuple-element.42), channel_id=1, source_target_pairs={{1,2},{2,1},{5,6},{6,5},{9,10},{10,9},{13,14},{14,13},{17,18},{18,... | collective-permute-start | bytes 638984 | tf_op jit(solution)/shard_map/ppermute | solution.py:436
  25.5 0.0 collective-permute-done.3.refs_7_.radial_a
  25.5 5.2 %collective-permute-done.4.refs_8_.radial_b = f32[104,512]{1,0:T(8,128)S(1)} collective-permute-done((f32[104,512]{1,0:T(8,128)S(1)}, f32[104,512]{1,0:T(8,128)S(1)}, u32[]{:S(2)}, u32[]{:S(2)}) %collective-permute-start.4) | collective-permute-done | bytes 213024 | tf_op jit(solution)/shard_map/ppermute | solution.py:436
  30.7 8.0 %collective-permute-done.2.refs_6_.axial_b = f32[200,512]{1,0:T(8,128)S(1)} collective-permute-done((f32[200,512]{1,0:T(8,128)S(1)}, f32[200,512]{1,0:T(8,128)S(1)}, u32[]{:S(2)}, u32[]{:S(2)}) %collective-permute-start.2) | collective-permute-done | bytes 409632 | tf_op jit(solution)/shard_map/ppermute | solution.py:435
  38.7 0.0 collective-permute-done.1.refs_5_.axial_a
  38.7 3.0 %soon.1 = (f32[6,128,512]{2,1,0:T(8,128)}, f32[4,4096]{1,0:T(4,128)}, f32[4,256]{1,0:T(4,128)}) custom-call(f32[6,128,512]{2,1,0:T(8,128)S(1)} %get-tuple-element.36.refs_0_.part, f32[4,4096]{1,0:T(4,128)S(1)} %get-tuple-element.37.refs_1_.updated, f32[6,128,512]{2,1,0:T(8,128)S(1)} %get-tuple-element.26.gas.refs_2_, f32[128,512]{1,0:T(8,128)S(1)} %bitcast.6, ...), custom_call_target="tpu_custom_call" | custom-call | tf_op jit(solution)/shard_map/soon/pallas_call | solution.py:469
  41.7 0.0 collective-permute-done.late
  41.7 0.1 last.1
  (1 shorter events, 0.0 us)
Async XLA Ops:
  0.6 5.5 %copy-start = (f32[8,16,512]{2,1,0:T(8,128)S(1)}, f32[8,16,512]{2,1,0:T(8,128)}, u32[]{:S(2)}) copy-start(f32[8,16,512]{2,1,0:T(8,128)} %param.7) | copy-start | bytes 786436
  2.3 36.4 %collective-permute-start.1 = (f32[208,512]{1,0:T(8,128)S(1)}, f32[208,512]{1,0:T(8,128)S(1)}, u32[]{:S(2)}, u32[]{:S(2)}) collective-permute-start(f32[208,512]{1,0:T(8,128)S(1)} %get-tuple-element.39), channel_id=1, source_target_pairs={{0,4},{4,0},{1,5},{5,1},{2,6},{6,2},{3,7},{7,3},{8,12},{12,8},{9,1... | collective-permute-start | bytes 1277960 | tf_op jit(solution)/shard_map/ppermute | solution.py:419
  12.4 29.3 %collective-permute-start = (f32[208,512]{1,0:T(8,128)S(1)}, f32[208,512]{1,0:T(8,128)S(1)}, u32[]{:S(2)}, u32[]{:S(2)}) collective-permute-start(f32[208,512]{1,0:T(8,128)S(1)} %get-tuple-element.33), channel_id=1, source_target_pairs={{64,60},{65,61},{66,62},{67,63},{128,124},{129,125},{130,126},{131... | collective-permute-start | bytes 1277960 | tf_op jit(solution)/shard_map/ppermute | solution.py:449
  20.1 18.6 %collective-permute-start.2 = (f32[200,512]{1,0:T(8,128)S(1)}, f32[200,512]{1,0:T(8,128)S(1)}, u32[]{:S(2)}, u32[]{:S(2)}) collective-permute-start(f32[200,512]{1,0:T(8,128)S(1)} %get-tuple-element.40), channel_id=1, source_target_pairs={{4,8},{8,4},{5,9},{9,5},{6,10},{10,6},{7,11},{11,7},{12,16},{16,12... | collective-permute-start | bytes 1228808 | tf_op jit(solution)/shard_map/ppermute | solution.py:435
  21.6 3.9 %collective-permute-start.3 = (f32[104,512]{1,0:T(8,128)S(1)}, f32[104,512]{1,0:T(8,128)S(1)}, u32[]{:S(2)}, u32[]{:S(2)}) collective-permute-start(f32[104,512]{1,0:T(8,128)S(1)} %get-tuple-element.41), channel_id=1, source_target_pairs={{0,1},{1,0},{2,3},{3,2},{4,5},{5,4},{6,7},{7,6},{8,9},{9,8},{10,11... | collective-permute-start | bytes 638984 | tf_op jit(solution)/shard_map/ppermute | solution.py:437
  23.5 7.2 %collective-permute-start.4 = (f32[104,512]{1,0:T(8,128)S(1)}, f32[104,512]{1,0:T(8,128)S(1)}, u32[]{:S(2)}, u32[]{:S(2)}) collective-permute-start(f32[104,512]{1,0:T(8,128)S(1)} %get-tuple-element.42), channel_id=1, source_target_pairs={{1,2},{2,1},{5,6},{6,5},{9,10},{10,9},{13,14},{14,13},{17,18},{18,... | collective-permute-start | bytes 638984 | tf_op jit(solution)/shard_map/ppermute | solution.py:436

commit v10 on v9

--- a/solution.py
+++ b/solution.py
@@ -397,7 +397,7 @@
     axial_a, picks, kept, gas, drops, cells = pl.pallas_call(
         prep_kernel,
         out_shape=(
-            shape((208, CZ), f32),
+            shape((200, CZ), f32),
             shape((8, 4 * CAP), f32),
             shape((32, 128), f32),
             shape((C, ROWS, CZ), f32),
@@ -437,13 +437,13 @@
     came_c = lax.ppermute(radial_a, both, to_c)
     late, part, updated = pl.pallas_call(
         early_kernel,
-        out_shape=(shape((208, CZ), f32), shape(part.shape, f32), updated),
+        out_shape=(shape((200, CZ), f32), shape(part.shape, f32), updated),
         in_specs=[VM] * 7,
         out_specs=(VM,) * 3,
         scratch_shapes=scratch,
         compiler_params=params,
         input_output_aliases={5: 1},
-        cost_estimate=cost(4000000000),
+        cost_estimate=cost(0),
         name="early",
     )(gas, picks, drops, cells, kept, part, table)
     came_late = lax.ppermute(late, both, to_late)
@@ -473,7 +473,7 @@
         out_specs=(HB,) * 3,
         scratch_shapes=scratch,
         compiler_params=params,
-        cost_estimate=pl.CostEstimate(flops=0, bytes_accessed=0, transcendentals=0),
+        cost_estimate=pl.CostEstimate(flops=4000000000, bytes_accessed=0, transcendentals=0),
         name="soon",
     )(*common)
     out, drops_out, arrivals_out = pl.pallas_call(

time: 42.2 us -> 35.4 us (0.84)
  the two profiles are of different devices: /device:TPU:6 before, /device:TPU:34 now
where the time goes in v10:
time: 35.4 us; the launch traced here: 35.2 us
  Pallas kernels  18.6 us (53%)
  starting transfers between devices  15.7 us (44%)
  between operations  0.95 us (3%)
    pallas_call x1, Pallas kernels, body(): pl.pallas_call(late_kernel, out_shape=tuple((shape(x.shape, x.dtype) for...  13.2 us
    ppermute x1, starting transfers between devices, body(): came_b = lax.ppermute(axial_b, both, to_b)  5.63 us
    ppermute x1, starting transfers between devices, body(): came_d = lax.ppermute(radial_b, both, to_d)  5.41 us
    pallas_call x1, Pallas kernels, body(): pl.pallas_call(soon_kernel, out_shape=finals, in_specs=[VM] * 9, out_spec...  3.25 us
    ppermute x1, starting transfers between devices, body(): came_a = lax.ppermute(axial_a, both, to_a)  2.02 us
    ppermute x1, starting transfers between devices, body(): came_c = lax.ppermute(radial_a, both, to_c)  1.92 us
    pallas_call x1, Pallas kernels, body(): pl.pallas_call(prep_kernel, out_shape=(shape((200, CZ), f32), shape((8, 4...  1.61 us
  transfers between devices with their start and end apart: 5, of which 0 were waited for; matrix products, arithmetic and copies ran while one was open for 0% of the time, Pallas kernels for 48%

profile of v10, /device:TPU:34, one launch (start us, length us, event | category | flops | bytes accessed | tf_op | source)
XLA Modules:
  0.0 35.2 jit_solution(5864047364220540528)
XLA Ops:
  0.6 0.0 copy-start
  0.6 1.6 %prep.1 = (f32[200,512]{1,0:T(8,128)S(1)}, f32[8,256]{1,0:T(8,128)S(1)}, f32[32,128]{1,0:T(8,128)S(1)}, f32[6,128,512]{2,1,0:T(8,128)S(1)}, f32[4,4096]{1,0:T(4,128)S(1)}, /*index=5*/s32[32,128]{1,0:T(8,128)S(1)}) custom-call(f32[6,128,512]{2,1,0:T(8,128)} %bitcast.9, f32[4,4096]{1,0:T(4,128)} %drops_in.1, s32[32,128]{1,0:T(8,128)} %bitcast.10, ...), custom_call_target="tpu_custom_call" | custom-call | tf_op jit(solution)/shard_map/prep/pallas_call | solution.py:397
  2.3 2.0 %collective-permute-start.1 = (f32[200,512]{1,0:T(8,128)S(1)}, f32[200,512]{1,0:T(8,128)S(1)}, u32[]{:S(2)}, u32[]{:S(2)}) collective-permute-start(f32[200,512]{1,0:T(8,128)S(1)} %get-tuple-element.39), channel_id=1, source_target_pairs={{0,4},{4,0},{1,5},{5,1},{2,6},{6,2},{3,7},{7,3},{8,12},{12,8},{9,1... | collective-permute-start | bytes 1228808 | tf_op jit(solution)/shard_map/ppermute | solution.py:419
  4.3 0.0 copy-done
  4.3 0.2 first.1
  4.5 5.6 %collective-permute-start.2 = (f32[200,512]{1,0:T(8,128)S(1)}, f32[200,512]{1,0:T(8,128)S(1)}, u32[]{:S(2)}, u32[]{:S(2)}) collective-permute-start(f32[200,512]{1,0:T(8,128)S(1)} %get-tuple-element.40), channel_id=1, source_target_pairs={{4,8},{8,4},{5,9},{9,5},{6,10},{10,6},{7,11},{11,7},{12,16},{16,12... | collective-permute-start | bytes 1228808 | tf_op jit(solution)/shard_map/ppermute | solution.py:435
  10.1 1.9 %collective-permute-start.3 = (f32[104,512]{1,0:T(8,128)S(1)}, f32[104,512]{1,0:T(8,128)S(1)}, u32[]{:S(2)}, u32[]{:S(2)}) collective-permute-start(f32[104,512]{1,0:T(8,128)S(1)} %get-tuple-element.41), channel_id=1, source_target_pairs={{0,1},{1,0},{2,3},{3,2},{4,5},{5,4},{6,7},{7,6},{8,9},{9,8},{10,11... | collective-permute-start | bytes 638984 | tf_op jit(solution)/shard_map/ppermute | solution.py:437
  12.1 5.4 %collective-permute-start.4 = (f32[104,512]{1,0:T(8,128)S(1)}, f32[104,512]{1,0:T(8,128)S(1)}, u32[]{:S(2)}, u32[]{:S(2)}) collective-permute-start(f32[104,512]{1,0:T(8,128)S(1)} %get-tuple-element.42), channel_id=1, source_target_pairs={{1,2},{2,1},{5,6},{6,5},{9,10},{10,9},{13,14},{14,13},{17,18},{18,... | collective-permute-start | bytes 638984 | tf_op jit(solution)/shard_map/ppermute | solution.py:436
  17.5 0.2 early.1
  17.7 0.7 %collective-permute-start = (f32[200,512]{1,0:T(8,128)S(1)}, f32[200,512]{1,0:T(8,128)S(1)}, u32[]{:S(2)}, u32[]{:S(2)}) collective-permute-start(f32[200,512]{1,0:T(8,128)S(1)} %get-tuple-element.33), channel_id=1, source_target_pairs={{64,60},{65,61},{66,62},{67,63},{128,124},{129,125},{130,126},{131... | collective-permute-start | bytes 1228808 | tf_op jit(solution)/shard_map/ppermute | solution.py:449
  18.4 13.2 %late.1 = (f32[6,128,512]{2,1,0:T(8,128)S(1)}, f32[4,4096]{1,0:T(4,128)S(1)}, bf16[512,1024]{1,0:T(8,128)(2,1)S(1)}) custom-call(f32[6,128,512]{2,1,0:T(8,128)S(1)} %get-tuple-element.26.gas.refs_2_, f32[128,512]{1,0:T(8,128)S(1)} %bitcast.5, f32[4,4096]{1,0:T(4,128)S(1)} %get-tuple-element.28.drops, ...), custom_call_target="tpu_custom_call", output_to_operand_aliasing={{0}: (5, {}), {1}: (6, {}), {2}: (7, {})} | custom-call | tf_op jit(solution)/shard_map/late/pallas_call | solution.py:450
  31.6 0.0 collective-permute-done.3.refs_7_.radial_a
  31.6 0.0 collective-permute-done.4.refs_8_.radial_b
  31.7 0.0 collective-permute-done.1.refs_5_.axial_a
  31.7 0.0 collective-permute-done.2.refs_6_.axial_b
  31.7 3.2 %soon.1 = (f32[6,128,512]{2,1,0:T(8,128)}, f32[4,4096]{1,0:T(4,128)}, f32[4,256]{1,0:T(4,128)}) custom-call(f32[6,128,512]{2,1,0:T(8,128)S(1)} %get-tuple-element.36.refs_0_.part, f32[4,4096]{1,0:T(4,128)S(1)} %get-tuple-element.37.refs_1_.updated, f32[6,128,512]{2,1,0:T(8,128)S(1)} %get-tuple-element.26.gas.refs_2_, f32[128,512]{1,0:T(8,128)S(1)} %bitcast.6, ...), custom_call_target="tpu_custom_call" | custom-call | flops 4000000000 | tf_op jit(solution)/shard_map/soon/pallas_call | solution.py:469
  34.9 0.0 collective-permute-done.late
  34.9 0.1 last.1
Async XLA Ops:
  0.6 3.7 %copy-start = (f32[8,16,512]{2,1,0:T(8,128)S(1)}, f32[8,16,512]{2,1,0:T(8,128)}, u32[]{:S(2)}) copy-start(f32[8,16,512]{2,1,0:T(8,128)} %param.7) | copy-start | bytes 786436
  2.3 29.4 %collective-permute-start.1 = (f32[200,512]{1,0:T(8,128)S(1)}, f32[200,512]{1,0:T(8,128)S(1)}, u32[]{:S(2)}, u32[]{:S(2)}) collective-permute-start(f32[200,512]{1,0:T(8,128)S(1)} %get-tuple-element.39), channel_id=1, source_target_pairs={{0,4},{4,0},{1,5},{5,1},{2,6},{6,2},{3,7},{7,3},{8,12},{12,8},{9,1... | collective-permute-start | bytes 1228808 | tf_op jit(solution)/shard_map/ppermute | solution.py:419
  4.5 27.2 %collective-permute-start.2 = (f32[200,512]{1,0:T(8,128)S(1)}, f32[200,512]{1,0:T(8,128)S(1)}, u32[]{:S(2)}, u32[]{:S(2)}) collective-permute-start(f32[200,512]{1,0:T(8,128)S(1)} %get-tuple-element.40), channel_id=1, source_target_pairs={{4,8},{8,4},{5,9},{9,5},{6,10},{10,6},{7,11},{11,7},{12,16},{16,12... | collective-permute-start | bytes 1228808 | tf_op jit(solution)/shard_map/ppermute | solution.py:435
  10.1 21.5 %collective-permute-start.3 = (f32[104,512]{1,0:T(8,128)S(1)}, f32[104,512]{1,0:T(8,128)S(1)}, u32[]{:S(2)}, u32[]{:S(2)}) collective-permute-start(f32[104,512]{1,0:T(8,128)S(1)} %get-tuple-element.41), channel_id=1, source_target_pairs={{0,1},{1,0},{2,3},{3,2},{4,5},{5,4},{6,7},{7,6},{8,9},{9,8},{10,11... | collective-permute-start | bytes 638984 | tf_op jit(solution)/shard_map/ppermute | solution.py:437
  12.1 19.6 %collective-permute-start.4 = (f32[104,512]{1,0:T(8,128)S(1)}, f32[104,512]{1,0:T(8,128)S(1)}, u32[]{:S(2)}, u32[]{:S(2)}) collective-permute-start(f32[104,512]{1,0:T(8,128)S(1)} %get-tuple-element.42), channel_id=1, source_target_pairs={{1,2},{2,1},{5,6},{6,5},{9,10},{10,9},{13,14},{14,13},{17,18},{18,... | collective-permute-start | bytes 638984 | tf_op jit(solution)/shard_map/ppermute | solution.py:436
  17.7 17.3 %collective-permute-start = (f32[200,512]{1,0:T(8,128)S(1)}, f32[200,512]{1,0:T(8,128)S(1)}, u32[]{:S(2)}, u32[]{:S(2)}) collective-permute-start(f32[200,512]{1,0:T(8,128)S(1)} %get-tuple-element.33), channel_id=1, source_target_pairs={{64,60},{65,61},{66,62},{67,63},{128,124},{129,125},{130,126},{131... | collective-permute-start | bytes 1228808 | tf_op jit(solution)/shard_map/ppermute | solution.py:449

commit v11 on v10

--- a/solution.py
+++ b/solution.py
@@ -163,7 +163,7 @@
 
 def stencil_soon():
     a, r = lax.axis_index("ax"), lax.axis_index("rad")
-    near_first = ((a == 0) & (r == 1)) | ((a == 1) & (r == 1)) | ((a == 2) & (r <= 1))
+    near_first = (a == 0) & (r == 1)
     return is_early() | near_first | ((lax.rem(a, 2) == 1) & (a > 1) & (lax.rem(a, WRAP) != WRAP - 1))
 
 

time: 35.4 us -> 34.4 us (0.972)
  the two profiles are of different devices: /device:TPU:34 before, /device:TPU:6 now
where the time goes in v11:
time: 34.4 us; the launch traced here: 33.8 us
  starting transfers between devices  17.5 us (51%)
  Pallas kernels  11.2 us (33%)
  waiting for transfers between devices  4.13 us (12%)
  between operations  0.93 us (3%)
    ppermute x1, starting transfers between devices, body(): came_late = lax.ppermute(late, both, to_late)  7.67 us
    ppermute x1, starting transfers between devices, body(): came_a = lax.ppermute(axial_a, both, to_a)  3.83 us
    pallas_call x1, Pallas kernels, body(): pl.pallas_call(early_kernel, out_shape=(shape((200, CZ), f32), shape(part...  3.46 us
    pallas_call x1, Pallas kernels, body(): pl.pallas_call(first_kernel, out_shape=(shape((200, CZ), f32), shape((104...  3.04 us
    pallas_call x1, Pallas kernels, body(): pl.pallas_call(soon_kernel, out_shape=finals, in_specs=[VM] * 9, out_spec...  3.03 us
    ppermute x1, starting transfers between devices, body(): came_d = lax.ppermute(radial_b, both, to_d)  2.84 us
    ppermute x1, waiting for transfers between devices, body(): came_b = lax.ppermute(axial_b, both, to_b)  2.29 us
    ppermute x1, starting transfers between devices, body(): came_c = lax.ppermute(radial_a, both, to_c)  1.92 us
  transfers between devices with their start and end apart: 5, of which 2 were waited for; matrix products, arithmetic and copies ran while one was open for 0% of the time, Pallas kernels for 28%

profile of v11, /device:TPU:6, one launch (start us, length us, event | category | flops | bytes accessed | tf_op | source)
XLA Modules:
  0.0 33.8 jit_solution(17263656396879816268)
XLA Ops:
  0.6 0.0 copy-start
  0.6 1.6 %prep.1 = (f32[200,512]{1,0:T(8,128)S(1)}, f32[8,256]{1,0:T(8,128)S(1)}, f32[32,128]{1,0:T(8,128)S(1)}, f32[6,128,512]{2,1,0:T(8,128)S(1)}, f32[4,4096]{1,0:T(4,128)S(1)}, /*index=5*/s32[32,128]{1,0:T(8,128)S(1)}) custom-call(f32[6,128,512]{2,1,0:T(8,128)} %bitcast.9, f32[4,4096]{1,0:T(4,128)} %drops_in.1, s32[32,128]{1,0:T(8,128)} %bitcast.10, ...), custom_call_target="tpu_custom_call" | custom-call | tf_op jit(solution)/shard_map/prep/pallas_call | solution.py:397
  2.3 3.8 %collective-permute-start.1 = (f32[200,512]{1,0:T(8,128)S(1)}, f32[200,512]{1,0:T(8,128)S(1)}, u32[]{:S(2)}, u32[]{:S(2)}) collective-permute-start(f32[200,512]{1,0:T(8,128)S(1)} %get-tuple-element.39), channel_id=1, source_target_pairs={{0,4},{4,0},{1,5},{5,1},{2,6},{6,2},{3,7},{7,3},{8,12},{12,8},{9,1... | collective-permute-start | bytes 1228808 | tf_op jit(solution)/shard_map/ppermute | solution.py:419
  6.1 0.0 copy-done
  6.1 3.0 %first.1 = (f32[200,512]{1,0:T(8,128)S(1)}, f32[104,512]{1,0:T(8,128)S(1)}, f32[104,512]{1,0:T(8,128)S(1)}, f32[6,128,512]{2,1,0:T(8,128)S(1)}, bf16[512,1024]{1,0:T(8,128)(2,1)S(1)}) custom-call(f32[6,128,512]{2,1,0:T(8,128)S(1)} %get-tuple-element.26.gas.refs_2_, f32[128,512]{1,0:T(8,128)S(1)} %bitcast.4, f32[8,256]{1,0:T(8,128)S(1)} %get-tuple-element.27.picks), custom_call_target="tpu_custom_call" | custom-call | flops 4000000000 | tf_op jit(solution)/shard_map/first/pallas_call | solution.py:425
  9.2 1.3 %collective-permute-start.2 = (f32[200,512]{1,0:T(8,128)S(1)}, f32[200,512]{1,0:T(8,128)S(1)}, u32[]{:S(2)}, u32[]{:S(2)}) collective-permute-start(f32[200,512]{1,0:T(8,128)S(1)} %get-tuple-element.40), channel_id=1, source_target_pairs={{4,8},{8,4},{5,9},{9,5},{6,10},{10,6},{7,11},{11,7},{12,16},{16,12... | collective-permute-start | bytes 1228808 | tf_op jit(solution)/shard_map/ppermute | solution.py:435
  10.5 1.9 %collective-permute-start.3 = (f32[104,512]{1,0:T(8,128)S(1)}, f32[104,512]{1,0:T(8,128)S(1)}, u32[]{:S(2)}, u32[]{:S(2)}) collective-permute-start(f32[104,512]{1,0:T(8,128)S(1)} %get-tuple-element.41), channel_id=1, source_target_pairs={{0,1},{1,0},{2,3},{3,2},{4,5},{5,4},{6,7},{7,6},{8,9},{9,8},{10,11... | collective-permute-start | bytes 638984 | tf_op jit(solution)/shard_map/ppermute | solution.py:437
  12.4 2.8 %collective-permute-start.4 = (f32[104,512]{1,0:T(8,128)S(1)}, f32[104,512]{1,0:T(8,128)S(1)}, u32[]{:S(2)}, u32[]{:S(2)}) collective-permute-start(f32[104,512]{1,0:T(8,128)S(1)} %get-tuple-element.42), channel_id=1, source_target_pairs={{1,2},{2,1},{5,6},{6,5},{9,10},{10,9},{13,14},{14,13},{17,18},{18,... | collective-permute-start | bytes 638984 | tf_op jit(solution)/shard_map/ppermute | solution.py:436
  15.2 3.5 %early.1 = (f32[200,512]{1,0:T(8,128)S(1)}, f32[6,128,512]{2,1,0:T(8,128)S(1)}, f32[4,4096]{1,0:T(4,128)S(1)}) custom-call(f32[6,128,512]{2,1,0:T(8,128)S(1)} %get-tuple-element.26.gas.refs_2_, f32[8,256]{1,0:T(8,128)S(1)} %get-tuple-element.27.picks, f32[4,4096]{1,0:T(4,128)S(1)} %get-tuple-element.28.drops, ...), custom_call_target="tpu_custom_call", output_to_operand_aliasing={{1}: (5, {})} | custom-call | tf_op jit(solution)/shard_map/early/pallas_call | solution.py:438
  18.7 7.7 %collective-permute-start = (f32[200,512]{1,0:T(8,128)S(1)}, f32[200,512]{1,0:T(8,128)S(1)}, u32[]{:S(2)}, u32[]{:S(2)}) collective-permute-start(f32[200,512]{1,0:T(8,128)S(1)} %get-tuple-element.33), channel_id=1, source_target_pairs={{64,60},{65,61},{66,62},{67,63},{128,124},{129,125},{130,126},{131... | collective-permute-start | bytes 1228808 | tf_op jit(solution)/shard_map/ppermute | solution.py:449
  26.4 0.0 collective-permute-done.3.refs_7_.radial_a
  26.4 0.0 collective-permute-done.4.refs_8_.radial_b
  26.4 0.0 collective-permute-done.1.refs_5_.axial_a
  26.4 2.3 %collective-permute-done.2.refs_6_.axial_b = f32[200,512]{1,0:T(8,128)S(1)} collective-permute-done((f32[200,512]{1,0:T(8,128)S(1)}, f32[200,512]{1,0:T(8,128)S(1)}, u32[]{:S(2)}, u32[]{:S(2)}) %collective-permute-start.2) | collective-permute-done | bytes 409632 | tf_op jit(solution)/shard_map/ppermute | solution.py:435
  28.7 3.0 %soon.1 = (f32[6,128,512]{2,1,0:T(8,128)}, f32[4,4096]{1,0:T(4,128)}, f32[4,256]{1,0:T(4,128)}) custom-call(f32[6,128,512]{2,1,0:T(8,128)S(1)} %get-tuple-element.36.refs_0_.part, f32[4,4096]{1,0:T(4,128)S(1)} %get-tuple-element.37.refs_1_.updated, f32[6,128,512]{2,1,0:T(8,128)S(1)} %get-tuple-element.26.gas.refs_2_, f32[128,512]{1,0:T(8,128)S(1)} %bitcast.6, ...), custom_call_target="tpu_custom_call" | custom-call | flops 4000000000 | tf_op jit(solution)/shard_map/soon/pallas_call | solution.py:469
  31.8 1.8 %collective-permute-done.late = f32[200,512]{1,0:T(8,128)S(1)} collective-permute-done((f32[200,512]{1,0:T(8,128)S(1)}, f32[200,512]{1,0:T(8,128)S(1)}, u32[]{:S(2)}, u32[]{:S(2)}) %collective-permute-start) | collective-permute-done | bytes 409632 | tf_op jit(solution)/shard_map/ppermute | solution.py:449
  33.6 0.1 last.1
  (1 shorter events, 0.0 us)
Async XLA Ops:
  0.6 5.5 %copy-start = (f32[8,16,512]{2,1,0:T(8,128)S(1)}, f32[8,16,512]{2,1,0:T(8,128)}, u32[]{:S(2)}) copy-start(f32[8,16,512]{2,1,0:T(8,128)} %param.7) | copy-start | bytes 786436
  2.3 24.2 %collective-permute-start.1 = (f32[200,512]{1,0:T(8,128)S(1)}, f32[200,512]{1,0:T(8,128)S(1)}, u32[]{:S(2)}, u32[]{:S(2)}) collective-permute-start(f32[200,512]{1,0:T(8,128)S(1)} %get-tuple-element.39), channel_id=1, source_target_pairs={{0,4},{4,0},{1,5},{5,1},{2,6},{6,2},{3,7},{7,3},{8,12},{12,8},{9,1... | collective-permute-start | bytes 1228808 | tf_op jit(solution)/shard_map/ppermute | solution.py:419
  9.2 19.6 %collective-permute-start.2 = (f32[200,512]{1,0:T(8,128)S(1)}, f32[200,512]{1,0:T(8,128)S(1)}, u32[]{:S(2)}, u32[]{:S(2)}) collective-permute-start(f32[200,512]{1,0:T(8,128)S(1)} %get-tuple-element.40), channel_id=1, source_target_pairs={{4,8},{8,4},{5,9},{9,5},{6,10},{10,6},{7,11},{11,7},{12,16},{16,12... | collective-permute-start | bytes 1228808 | tf_op jit(solution)/shard_map/ppermute | solution.py:435
  10.5 16.0 %collective-permute-start.3 = (f32[104,512]{1,0:T(8,128)S(1)}, f32[104,512]{1,0:T(8,128)S(1)}, u32[]{:S(2)}, u32[]{:S(2)}) collective-permute-start(f32[104,512]{1,0:T(8,128)S(1)} %get-tuple-element.41), channel_id=1, source_target_pairs={{0,1},{1,0},{2,3},{3,2},{4,5},{5,4},{6,7},{7,6},{8,9},{9,8},{10,11... | collective-permute-start | bytes 638984 | tf_op jit(solution)/shard_map/ppermute | solution.py:437
  12.4 14.0 %collective-permute-start.4 = (f32[104,512]{1,0:T(8,128)S(1)}, f32[104,512]{1,0:T(8,128)S(1)}, u32[]{:S(2)}, u32[]{:S(2)}) collective-permute-start(f32[104,512]{1,0:T(8,128)S(1)} %get-tuple-element.42), channel_id=1, source_target_pairs={{1,2},{2,1},{5,6},{6,5},{9,10},{10,9},{13,14},{14,13},{17,18},{18,... | collective-permute-start | bytes 638984 | tf_op jit(solution)/shard_map/ppermute | solution.py:436
  18.7 14.9 %collective-permute-start = (f32[200,512]{1,0:T(8,128)S(1)}, f32[200,512]{1,0:T(8,128)S(1)}, u32[]{:S(2)}, u32[]{:S(2)}) collective-permute-start(f32[200,512]{1,0:T(8,128)S(1)} %get-tuple-element.33), channel_id=1, source_target_pairs={{64,60},{65,61},{66,62},{67,63},{128,124},{129,125},{130,126},{131... | collective-permute-start | bytes 1228808 | tf_op jit(solution)/shard_map/ppermute | solution.py:449
